TPU v7x, 32 devices: a whole 2x2x4 slice. The times are simulated.
32 devices in a mesh: dp: 8 (over y, x, core), expert: 4 (over z).
Axes of the slice: x: 2, y: 2, z: 4, core: 2. Of those that a mesh axis runs over, the one named last changes fastest.
Arguments:
- grad_out: bfloat16 [8192, 3072], P(('dp', 'expert')), may hold values from -1.5 to 1.5
- routes: int32 [8192, 2], P(('dp', 'expert')), may hold values from 0 to 63, as said below
- gate_levels: int32 [8192, 2], P(('dp', 'expert')), may hold values from 1 to 15
- saved_inputs: bfloat16 [1536, 3072], P(('dp', 'expert')), may hold values from -6 to 6
- w_gate: bfloat16 [3072, 2048], P(None, 'expert'), may hold values from -0.109375 to 0.109375
- w_up: bfloat16 [3072, 2048], P(None, 'expert'), may hold values from -0.109375 to 0.109375
- w_down: bfloat16 [2048, 3072], P('expert'), may hold values from -0.1875 to 0.1875
Outputs:
- input_grad: bfloat16 [8192, 3072], P(('dp', 'expert'))
- gate_grad: float32 [8192, 2], P(('dp', 'expert'))
- weight_grad: float32 [3072, 3, 2048], P('dp', None, 'expert')
Inputs may be any that keep to these rules, and one draw needn't show every extreme that they name: `routes`: the ids of one token differ. A device's tokens name each expert below 2 at most 12 times; in every block one of them is named exactly 12 times, and the same one for all 4 blocks of one replica.
All inputs are finite; a program needn't handle non-finite values.
Results may differ from a plain program's by a relative error of at most 0.012.
Values may be sent and summed in bfloat16 or wider, within the bound.
No kernel may reach another device: no remote copies, remote signals or barrier semaphores. Data moves between devices by JAX's collectives and lax.ppermute only.
A program may use at most 128 MiB of HBM per device.

v0:
```python
import jax
import jax.numpy as jnp
from jax import lax
from jax.sharding import PartitionSpec as P

EXPERTS_W = 2


def rows_product(left, right):
    return lax.dot_general(
        left, right, (((0,), (0,)), ((), ())), preferred_element_type=jnp.float32
    )


def back_product(left, right):
    return lax.dot_general(
        left, right, (((1,), (1,)), ((), ())), preferred_element_type=jnp.float32
    )


def per_device(grad_out, routes, gate_levels, saved_inputs, w_gate, w_up, w_down):
    group = lax.axis_size("expert")
    shards = group // EXPERTS_W
    capacity = saved_inputs.shape[0] // group
    width = grad_out.shape[1]
    hits = (routes[:, :, None] == jnp.arange(EXPERTS_W, dtype=jnp.int32)).astype(jnp.int32)
    member = jnp.sum(hits, axis=1)
    levels = jnp.sum(hits * gate_levels[:, :, None], axis=1)
    slots = jnp.cumsum(member, axis=0) - 1
    placed = (member[None] == 1) & (
        slots[None] == jnp.arange(capacity, dtype=jnp.int32)[:, None, None]
    )
    table = jnp.transpose(placed, (2, 0, 1))
    table_half = table.astype(jnp.bfloat16)
    table_full = table.astype(jnp.float32)
    picked = jnp.einsum(
        "ect,td->ecd", table_half, grad_out, preferred_element_type=jnp.float32
    ).astype(jnp.bfloat16)
    slot_gate = (
        jnp.einsum(
            "ect,te->ec", table_full, levels.astype(jnp.float32), precision=lax.Precision.HIGHEST
        )
        / 16.0
    )
    send_rows = jnp.repeat(picked, shards, axis=0)
    send_gate = jnp.repeat(slot_gate, shards, axis=0).astype(jnp.bfloat16)
    recv_rows, recv_gate = (
        lax.all_to_all(send_rows, "expert", split_axis=0, concat_axis=0, tiled=True),
        lax.all_to_all(send_gate, "expert", split_axis=0, concat_axis=0, tiled=True),
    )
    grad_rows = recv_rows.reshape(group * capacity, width)
    gates = recv_gate.reshape(group * capacity, 1).astype(jnp.float32)
    pre_gate = jnp.dot(saved_inputs, w_gate, preferred_element_type=jnp.float32)
    pre_up = jnp.dot(saved_inputs, w_up, preferred_element_type=jnp.float32)
    projected = back_product(grad_rows, w_down)
    sigma = jax.nn.sigmoid(pre_gate)
    activ = pre_gate * sigma
    hidden = activ * pre_up
    gate_part = jnp.sum(hidden * projected, axis=1).astype(jnp.bfloat16)
    d_hidden = gates * projected
    d_up = (d_hidden * activ).astype(jnp.bfloat16)
    d_pre = (d_hidden * pre_up * sigma * (1.0 + pre_gate * (1.0 - sigma))).astype(jnp.bfloat16)
    scaled_hidden = (gates * hidden).astype(jnp.bfloat16)
    input_part = (back_product(d_pre, w_gate) + back_product(d_up, w_up)).astype(jnp.bfloat16)
    back_rows, back_gate = (
        lax.all_to_all(
            input_part.reshape(group, capacity, width),
            "expert",
            split_axis=0,
            concat_axis=0,
            tiled=True,
        ),
        lax.all_to_all(
            gate_part.reshape(group, capacity), "expert", split_axis=0, concat_axis=0, tiled=True
        ),
    )
    gate_share = lax.psum_scatter(
        rows_product(saved_inputs, d_pre), "dp", scatter_dimension=0, tiled=True
    )
    up_share = lax.psum_scatter(
        rows_product(saved_inputs, d_up), "dp", scatter_dimension=0, tiled=True
    )
    down_share = lax.psum_scatter(
        rows_product(grad_rows, scaled_hidden), "dp", scatter_dimension=0, tiled=True
    )
    weight_grad = jnp.stack([gate_share, up_share, down_share], axis=1)
    summed = back_rows.astype(jnp.float32).reshape(EXPERTS_W, shards, capacity, width).sum(axis=1)
    gate_summed = back_gate.astype(jnp.float32).reshape(EXPERTS_W, shards, capacity).sum(axis=1)
    input_grad = jnp.einsum(
        "ect,ecd->td", table_full, summed, precision=lax.Precision.HIGHEST
    ).astype(jnp.bfloat16)
    per_expert = jnp.einsum("ect,ec->te", table_full, gate_summed, precision=lax.Precision.HIGHEST)
    gate_grad = jnp.sum(hits.astype(jnp.float32) * per_expert[:, None, :], axis=2)
    return (input_grad, gate_grad, weight_grad)


def solution(mesh):
    in_specs = (
        P(("dp", "expert"), None),
        P(("dp", "expert"), None),
        P(("dp", "expert"), None),
        P(("dp", "expert"), None),
        P(None, "expert"),
        P(None, "expert"),
        P("expert", None),
    )
    out_specs = (P(("dp", "expert"), None), P(("dp", "expert"), None), P("dp", None, "expert"))
    return jax.shard_map(
        per_device, mesh=mesh, in_specs=in_specs, out_specs=out_specs, check_vma=False
    )
```

profile of v0, /device:TPU:0, one launch (start us, length us, event | category | flops | bytes accessed | tf_op | source)
XLA Modules:
  0.0 252.4 jit_solution(5768723761823906397)
XLA Ops:
  7.2 0.0 copy-start
  7.2 0.0 copy-start.2
  7.2 0.9 select_reduce_fusion
  8.1 0.6 reduce-window.6
  8.7 0.2 slice_reduce_fusion
  8.9 0.2 reduce-window.9
  9.1 0.1 add_bitcast_fusion
  9.2 0.1 fusion.12
  9.3 0.6 copy.24
  9.9 6.3 %all-to-all-start = ((bf16[4,1,12]{2,1,0:T(2,128)(2,1)}), bf16[4,1,12]{2,1,0:T(2,128)(2,1)S(1)}, u32[]{:S(2)}, u32[]{:S(2)}) async-start(bf16[4,1,12]{2,1,0:T(2,128)(2,1)} %copy.24), calls=%async_computation | async-start | bytes 4096 | tf_op jit(solution)/shard_map/all_to_all | solution.py:49
  16.3 2.5 convolution_convert_fusion
  18.7 3.0 %all-to-all-done = bf16[4,1,12]{2,1,0:T(2,128)(2,1)S(1)} async-done(((bf16[4,1,12]{2,1,0:T(2,128)(2,1)}), bf16[4,1,12]{2,1,0:T(2,128)(2,1)S(1)}, u32[]{:S(2)}, u32[]{:S(2)}) %all-to-all-start) | async-done | bytes 128 | tf_op jit(solution)/shard_map/all_to_all | solution.py:49
  21.7 1.7 broadcast_in_dim.5
  23.4 4.1 %all-to-all-start.1 = ((bf16[4,12,3072]{2,1,0:T(8,128)(2,1)}), bf16[4,12,3072]{2,1,0:T(8,128)(2,1)}, u32[]{:S(2)}, u32[]{:S(2)}) async-start(bf16[4,12,3072]{2,1,0:T(8,128)(2,1)} %bitcast.57), calls=%async_computation.1 | async-start | bytes 786432 | tf_op jit(solution)/shard_map/all_to_all | solution.py:48
  27.5 0.0 reduce-scatter.4.cloned.1.call-start
  27.6 0.0 copy-done.2
  27.6 2.5 fusion.26
  30.1 0.0 copy-done
  30.1 1.3 fusion.27
  31.4 0.1 reshape.92
  31.5 6.6 %all-to-all-done.1 = bf16[4,12,3072]{2,1,0:T(8,128)(2,1)} async-done(((bf16[4,12,3072]{2,1,0:T(8,128)(2,1)}), bf16[4,12,3072]{2,1,0:T(8,128)(2,1)}, u32[]{:S(2)}, u32[]{:S(2)}) %all-to-all-start.1) | async-done | bytes 294944 | tf_op jit(solution)/shard_map/all_to_all | solution.py:48
  38.1 1.8 reshape.88
  39.9 3.7 %multiply_reduce_fusion = (bf16[48]{0:T(256)(128)(2,1)S(1)}, bf16[48,512]{1,0:T(8,128)(2,1)S(1)}, bf16[48,512]{1,0:T(8,128)(2,1)}) fusion(f32[48,512]{1,0:T(8,128)S(1)} %fusion.26, f32[48,512]{1,0:T(8,128)} %fusion.27, f32[48]{0:T(128)S(1)} %reshape.92, bf16[48,3072]{1,0:T(8,128)(2,1)} %reshape.88, bf16[512,3072]{1,0:T(8,128)(2,1)} %param.13), kind=kOutput, calls=%fused_computation.11 | convolution fusion | flops 151412688 | bytes 3735840 | tf_op jit(solution)/shard_map/dot_general | solution.py:16
  43.6 0.0 copy-start.5
  43.6 0.6 copy-done.5
  44.2 3.7 %convolution_bitcast_fusion.1 = f32[3072,512]{0,1:T(8,128)} fusion(bf16[48,512]{1,0:T(8,128)(2,1)S(1)} %get-tuple-element.18, bf16[48,3072]{1,0:T(8,128)(2,1)S(1)} %copy-done.2), kind=kOutput, calls=%fused_computation.1 | convolution fusion | flops 150994944 | bytes 6635520 | tf_op jit(solution)/shard_map/dot_general | solution.py:10
  47.9 0.0 reduce-scatter.4.cloned.1.call-update
  47.9 0.0 reduce-scatter.6.cloned.1.call-start
  48.0 4.5 %convolution_bitcast_fusion = f32[3072,512]{0,1:T(8,128)} fusion(bf16[48,512]{1,0:T(8,128)(2,1)} %get-tuple-element.19, bf16[48,3072]{1,0:T(8,128)(2,1)S(1)} %copy-done.2), kind=kOutput, calls=%fused_computation | convolution fusion | flops 150994944 | bytes 6635520 | tf_op jit(solution)/shard_map/dot_general | solution.py:10
  52.4 0.0 copy-start.3
  52.4 0.0 reduce-scatter.6.cloned.1.call-update
  52.4 0.0 reduce-scatter.8.cloned.1.call-start
  52.5 0.9 copy-done.3
  53.4 5.1 %fusion.4 = f32[3072,512]{0,1:T(8,128)} fusion(bf16[48,3072]{1,0:T(8,128)(2,1)S(1)} %copy-done.3, f32[48]{0:T(128)S(1)} %reshape.92, f32[48,512]{1,0:T(8,128)S(1)} %fusion.26, f32[48,512]{1,0:T(8,128)} %fusion.27), kind=kOutput, calls=%fused_computation.16 | convolution fusion | flops 151166976 | bytes 6783168 | tf_op jit(solution)/shard_map/dot_general | solution.py:10
  58.5 0.0 copy-start.6
  58.5 0.0 reduce-scatter.8.cloned.1.call-update
  58.5 0.0 copy-start.4
  58.5 0.7 convert_element_type.99
  59.2 3.2 %all-to-all-start.3 = ((bf16[4,1,12]{2,1,0:T(2,128)(2,1)}), bf16[4,1,12]{2,1,0:T(2,128)(2,1)S(1)}, u32[]{:S(2)}, u32[]{:S(2)}) async-start(bf16[4,1,12]{2,1,0:T(2,128)(2,1)} %convert_element_type.99), calls=%async_computation.3 | async-start | bytes 4096 | tf_op jit(solution)/shard_map/all_to_all | solution.py:73
  62.4 0.0 copy-done.6
  62.4 0.0 copy-start.1
  62.4 1.0 fusion.28
  63.4 0.0 copy-done.4
  63.5 0.9 copy-done.1
  64.4 0.0 copy-start.7
  64.4 1.0 fusion.1
  65.4 0.8 reshape.89
  66.2 1.6 all-to-all-done.3
  67.8 0.0 copy-start.8
  67.8 0.6 copy-done.8
  68.4 3.5 %all-to-all-start.2 = ((bf16[4,12,3072]{2,1,0:T(8,128)(2,1)}), bf16[4,12,3072]{2,1,0:T(8,128)(2,1)S(1)}, u32[]{:S(2)}, u32[]{:S(2)}) async-start(bf16[4,12,3072]{2,1,0:T(8,128)(2,1)} %reshape.89), calls=%async_computation.2 | async-start | bytes 786432 | tf_op jit(solution)/shard_map/all_to_all | solution.py:66
  71.9 0.7 convert_element_type.98
  72.6 0.6 reduce_sum.61
  73.2 0.8 fusion.8
  74.0 0.0 copy-done.7
  74.0 0.6 fusion.23
  74.6 6.8 %all-to-all-done.2 = bf16[4,12,3072]{2,1,0:T(8,128)(2,1)S(1)} async-done(((bf16[4,12,3072]{2,1,0:T(8,128)(2,1)}), bf16[4,12,3072]{2,1,0:T(8,128)(2,1)S(1)}, u32[]{:S(2)}, u32[]{:S(2)}) %all-to-all-start.2) | async-done | bytes 294944 | tf_op jit(solution)/shard_map/all_to_all | solution.py:66
  81.4 0.1 convert_reduce_fusion
  81.5 2.6 %fusion = bf16[256,3072]{1,0:T(8,128)(2,1)} fusion(f32[2,12,3072]{2,1,0:T(8,128)S(1)} %convert_reduce_fusion, s32[2,256]{1,0:T(2,128)S(1)} %bitcast.65, pred[2,256]{1,0:T(4,128)(4,1)S(1)} %broadcast_compare_fusion), kind=kOutput, calls=%fused_computation.3 | convolution fusion | flops 227291136 | bytes 1870336 | tf_op jit(solution)/shard_map/ect,ecd->td/dot_general | solution.py:89
  84.1 24.9 %reduce-scatter.4.cloned.1.call-done = f32[384,512]{0,1:T(8,128)} async-done(((f32[3072,512]{0,1:T(8,128)}), f32[384,512]{0,1:T(8,128)}) %reduce-scatter.4.cloned.1.call-update) | async-done | bytes 786448 | tf_op jit(solution)/shard_map/reduce_scatter | solution.py:77
  109.0 65.5 %reduce-scatter.6.cloned.1.call-done = f32[384,512]{0,1:T(8,128)} async-done(((f32[3072,512]{0,1:T(8,128)}), f32[384,512]{0,1:T(8,128)}) %reduce-scatter.6.cloned.1.call-update) | async-done | bytes 786448 | tf_op jit(solution)/shard_map/reduce_scatter | solution.py:80
  174.5 65.1 %reduce-scatter.8.cloned.1.call-done = f32[384,512]{0,1:T(8,128)} async-done(((f32[3072,512]{0,1:T(8,128)}), f32[384,512]{0,1:T(8,128)}) %reduce-scatter.8.cloned.1.call-update) | async-done | bytes 786448 | tf_op jit(solution)/shard_map/reduce_scatter | solution.py:83
  239.6 3.2 %pad_maximum_fusion = f32[384,3,512]{0,2,1:T(8,128)} fusion(f32[384,1,512]{0,2,1:T(8,128)} %bitcast.60, f32[384,1,512]{0,2,1:T(8,128)} %bitcast.59, f32[384,1,512]{0,2,1:T(8,128)} %bitcast.58), kind=kLoop, calls=%fused_computation.7 | loop fusion | flops 1179648 | bytes 4718592 | tf_op jit(solution)/shard_map/stack | solution.py:86
  242.8 3.0 %copy.27 = f32[384,3,512]{2,0,1:T(8,128)} copy(f32[384,3,512]{0,2,1:T(8,128)} %pad_maximum_fusion) | data formatting | bytes 4718592
  (8 shorter events, 0.1 us)
Async XLA Ops:
  7.2 23.0 %copy-start = (bf16[3072,512]{1,0:T(8,128)(2,1)S(1)}, bf16[3072,512]{1,0:T(8,128)(2,1)}, u32[]{:S(2)}) copy-start(bf16[3072,512]{1,0:T(8,128)(2,1)} %param.11) | copy-start | bytes 9437188
  7.2 20.4 %copy-start.2 = (bf16[48,3072]{1,0:T(8,128)(2,1)S(1)}, bf16[48,3072]{1,0:T(8,128)(2,1)}, u32[]{:S(2)}) copy-start(bf16[48,3072]{1,0:T(8,128)(2,1)} %param.10) | copy-start | bytes 884740
  9.9 11.8 %all-to-all-start = ((bf16[4,1,12]{2,1,0:T(2,128)(2,1)}), bf16[4,1,12]{2,1,0:T(2,128)(2,1)S(1)}, u32[]{:S(2)}, u32[]{:S(2)}) async-start(bf16[4,1,12]{2,1,0:T(2,128)(2,1)} %copy.24), calls=%async_computation | async-start | bytes 4096 | tf_op jit(solution)/shard_map/all_to_all | solution.py:49
  23.4 14.7 %all-to-all-start.1 = ((bf16[4,12,3072]{2,1,0:T(8,128)(2,1)}), bf16[4,12,3072]{2,1,0:T(8,128)(2,1)}, u32[]{:S(2)}, u32[]{:S(2)}) async-start(bf16[4,12,3072]{2,1,0:T(8,128)(2,1)} %bitcast.57), calls=%async_computation.1 | async-start | bytes 786432 | tf_op jit(solution)/shard_map/all_to_all | solution.py:48
  27.5 81.4 %reduce-scatter.4.cloned.1.call-start = ((), (), s32[]{:S(2)}) async-start(), calls=%async_computation.7 | async-start | bytes 7077888 | tf_op jit(solution)/shard_map/reduce_scatter | solution.py:77
  43.6 0.6 copy-start.5
  47.9 126.6 %reduce-scatter.6.cloned.1.call-start = ((), (), s32[]{:S(2)}) async-start(), calls=%async_computation.8 | async-start | bytes 7077888 | tf_op jit(solution)/shard_map/reduce_scatter | solution.py:80
  52.4 1.0 copy-start.3
  52.4 187.2 %reduce-scatter.8.cloned.1.call-start = ((), (), s32[]{:S(2)}) async-start(), calls=%async_computation.9 | async-start | bytes 7077888 | tf_op jit(solution)/shard_map/reduce_scatter | solution.py:83
  58.5 3.9 %copy-start.6 = (bf16[48,512]{1,0:T(8,128)(2,1)S(1)}, bf16[48,512]{1,0:T(8,128)(2,1)}, u32[]{:S(2)}) copy-start(bf16[48,512]{1,0:T(8,128)(2,1)} %copy-done.5) | copy-start | bytes 147460
  58.5 5.0 %copy-start.4 = (bf16[48,512]{1,0:T(8,128)(2,1)S(1)}, bf16[48,512]{1,0:T(8,128)(2,1)}, u32[]{:S(2)}) copy-start(bf16[48,512]{1,0:T(8,128)(2,1)} %get-tuple-element.19) | copy-start | bytes 147460
  59.2 8.7 %all-to-all-start.3 = ((bf16[4,1,12]{2,1,0:T(2,128)(2,1)}), bf16[4,1,12]{2,1,0:T(2,128)(2,1)S(1)}, u32[]{:S(2)}, u32[]{:S(2)}) async-start(bf16[4,1,12]{2,1,0:T(2,128)(2,1)} %convert_element_type.99), calls=%async_computation.3 | async-start | bytes 4096 | tf_op jit(solution)/shard_map/all_to_all | solution.py:73
  62.4 2.0 copy-start.1
  64.4 9.6 %copy-start.7 = (s32[256,2]{0,1:T(2,128)S(1)}, s32[256,2]{0,1:T(2,128)}, u32[]{:S(2)}) copy-start(s32[256,2]{0,1:T(2,128)} %param.8) | copy-start | bytes 6148
  67.8 0.6 copy-start.8
  68.4 13.0 %all-to-all-start.2 = ((bf16[4,12,3072]{2,1,0:T(8,128)(2,1)}), bf16[4,12,3072]{2,1,0:T(8,128)(2,1)S(1)}, u32[]{:S(2)}, u32[]{:S(2)}) async-start(bf16[4,12,3072]{2,1,0:T(8,128)(2,1)} %reshape.89), calls=%async_computation.2 | async-start | bytes 786432 | tf_op jit(solution)/shard_map/all_to_all | solution.py:66
Sparse Core Ops, SparseCore 0:
  48.0 60.8 reduce-scatter.3
  112.7 61.7 reduce-scatter.5
  177.9 61.7 reduce-scatter.7
where the time goes:
time: 253 us; the launch traced here: 252 us
  waiting for transfers between devices  174 us (69%)
  matrix products  28.7 us (11%)
  starting transfers between devices  17.3 us (7%)
  between operations  13.9 us (5%)
  local copies, waits for them, and re-layouts  12 us (5%)
  other arithmetic  6.89 us (3%)
    reduce_scatter x1, waiting for transfers between devices, per_device(): lax.psum_scatter(rows_product(saved_inputs, d_up), 'dp', scatter_dimensio...  65.5 us
    reduce_scatter x1, waiting for transfers between devices, per_device(): lax.psum_scatter(rows_product(grad_rows, scaled_hidden), 'dp', scatter_di...  65.1 us
    reduce_scatter x1, waiting for transfers between devices, per_device(): lax.psum_scatter(rows_product(saved_inputs, d_pre), 'dp', scatter_dimensi...  24.9 us
    dot_general x3, matrix products, rows_product(): lax.dot_general(left, right, (((0,), (0,)), ((), ())), preferred_element_...  13.2 us
    all_to_all x1, waiting for transfers between devices, per_device(): lax.all_to_all(input_part.reshape(group, capacity, width), 'expert', spli...  6.8 us
    all_to_all x1, waiting for transfers between devices, per_device(): lax.all_to_all(send_rows, 'expert', split_axis=0, concat_axis=0, tiled=True)  6.59 us
    all_to_all x1, starting transfers between devices, per_device(): lax.all_to_all(send_gate, 'expert', split_axis=0, concat_axis=0, tiled=True)  6.32 us
    unnamed x20, local copies, waits for them, and re-layouts  6.12 us
  transfers between devices with their start and end apart: 7, of which 7 were waited for; matrix products, arithmetic and copies ran while one was open for 10% of the time, Pallas kernels for 0%

commit v1 on v0

v1 whole, which is shorter than its diff:
```python
import functools

import jax
import jax.numpy as jnp
from jax import lax
from jax.experimental import pallas as pl
from jax.experimental.pallas import tpu as pltpu
from jax.sharding import PartitionSpec as P

EXPERTS_W = 2
SEND_CUTS = 4
BACK_CUTS = 2
GATE_LANES = 128
W_CHUNKS = 4
PAIRED = 8
F32 = jnp.float32
BF16 = jnp.bfloat16
VMEM = pl.BlockSpec(memory_space=pltpu.VMEM)
HBM = pl.BlockSpec(memory_space=pl.ANY)


def nn(left, right):
    return lax.dot_general(left, right, (((1,), (0,)), ((), ())), preferred_element_type=F32)


def nt(left, right):
    return lax.dot_general(left, right, (((1,), (1,)), ((), ())), preferred_element_type=F32)


def tn(left, right):
    return lax.dot_general(left, right, (((0,), (0,)), ((), ())), preferred_element_type=F32)


def iota(shape, dim):
    return lax.broadcasted_iota(jnp.int32, shape, dim)


def call(kernel, outs, args, specs, scratch=(), flops=0, moved=0, name=None):
    return pl.pallas_call(
        kernel,
        out_shape=outs,
        in_specs=specs,
        out_specs=jax.tree.map(lambda _: VMEM, outs),
        scratch_shapes=scratch,
        compiler_params=pltpu.CompilerParams(vmem_limit_bytes=40 * 1024 * 1024),
        cost_estimate=pl.CostEstimate(flops=flops, bytes_accessed=moved, transcendentals=0),
        name=name,
    )(*args)


def pick_kernel(shards, capacity, routes, levels, grad, own_out, other_out, slots_out):
    tokens, width = grad.shape
    span = width // SEND_CUTS
    rows = SEND_CUTS * capacity
    mine = lax.axis_index("expert") // shards
    upto = (iota((tokens, tokens), 0) <= iota((tokens, tokens), 1)).astype(BF16)
    first, second = routes[0:1, :], routes[1:2, :]
    found = jnp.zeros((8, tokens), F32)
    for expert in range(EXPERTS_W):
        hit = ((first == expert) | (second == expert)).astype(F32)
        found = jnp.where(iota((8, tokens), 0) == expert, hit, found)
    counted = nn(found.astype(BF16), upto)
    slots = jnp.where(found > 0, counted - 1.0, -4096.0).astype(jnp.int32)
    slots_out[...] = slots
    for which, out in ((0, own_out), (1, other_out)):
        expert = mine if which == 0 else 1 - mine
        slot = jnp.where(expert == 0, slots[0:1, :], slots[1:2, :])
        level = jnp.where(first == expert, levels[0:1, :], levels[1:2, :])
        gate = level.astype(F32) * (1.0 / 16.0)
        total = jnp.zeros((rows, span), F32)
        for cut in range(SEND_CUTS):
            lead = jnp.where(slot == iota((rows, tokens), 0) - cut * capacity, gate, 0.0)
            total += nn(lead.astype(BF16), grad[:, cut * span : (cut + 1) * span])
        out[...] = total.astype(BF16)


def hidden_kernel(inputs, w_gate, w_up, u_out, v_out, h_out, gate_buf, up_buf, sems):
    width = inputs.shape[1]
    step = width // W_CHUNKS
    copies = []
    for k in range(W_CHUNKS):
        part = pl.ds(k * step, step)
        for n, (src, dst) in enumerate(((w_gate, gate_buf), (w_up, up_buf))):
            copy = pltpu.make_async_copy(src.at[part], dst.at[part], sems.at[n, k])
            copy.start()
            copies.append(copy)
    a = jnp.zeros(u_out.shape, F32)
    b = jnp.zeros(u_out.shape, F32)
    for k in range(W_CHUNKS):
        left = inputs[:, k * step : (k + 1) * step]
        copies[2 * k].wait()
        a += nn(left, gate_buf[k * step : (k + 1) * step, :])
        copies[2 * k + 1].wait()
        b += nn(left, up_buf[k * step : (k + 1) * step, :])
    s = jax.nn.sigmoid(a)
    u = a * s
    u_out[...] = u
    v_out[...] = b * s * (1.0 + a * (1.0 - s))
    h_out[...] = u * b


def project_kernel(group, capacity, n_dp, *refs):
    received = refs[:group]
    w_down, u_in, v_in, h_in, inputs = refs[group : group + 5]
    sends = refs[group + 5 : -6]
    da_out, db_out, gate_out, down_buf, rows_buf, sems = refs[-6:]
    rows, width = inputs.shape
    hidden = u_in.shape[1]
    span = width // SEND_CUTS
    me = lax.axis_index("expert")
    copies = []
    for cut in range(SEND_CUTS):
        part = pl.ds(cut * span, span)
        copy = pltpu.make_async_copy(w_down.at[:, part], down_buf.at[:, part], sems.at[cut])
        copy.start()
        copies.append(copy)
    packed = SEND_CUTS * capacity
    every = jnp.concatenate([ref[...] for ref in received], axis=0)
    to = iota((rows, group * packed), 0)
    at = iota((rows, group * packed), 1)
    source = (at // packed) ^ me
    within = at % packed
    match = (to // capacity == source) & (to % capacity == within % capacity)
    projected = jnp.zeros((rows, hidden), F32)
    for cut in range(SEND_CUTS):
        select = (match & (within // capacity == cut)).astype(F32).astype(BF16)
        piece = nn(select, every).astype(BF16)
        rows_buf[:, cut * span : (cut + 1) * span] = piece
        copies[cut].wait()
        projected += nt(piece, down_buf[:, cut * span : (cut + 1) * span])
    da = (projected * v_in[...]).astype(BF16)
    db = (projected * u_in[...]).astype(BF16)
    hid = h_in[...]
    da_out[...] = da
    db_out[...] = db
    gate = jnp.sum(hid * projected, axis=1, keepdims=True)
    lane = iota((rows, GATE_LANES), 1)
    gate_out[...] = jnp.where(lane == me // (group // EXPERTS_W), gate, 0.0).astype(BF16)
    hid = hid.astype(BF16)
    if n_dp != PAIRED:
        sends[0][...] = rows_buf[...]
        sends[1][...] = hid
        return
    pair = 2 * (width // n_dp)
    chip = lax.axis_index("dp") // 2
    for m, send in enumerate(sends):
        start = pl.multiple_of((chip ^ m) * pair, 128)
        send[:, 0:pair] = inputs[:, pl.ds(start, pair)]
        send[:, pair : 2 * pair] = rows_buf[:, pl.ds(start, pair)]
        send[:, 2 * pair : 2 * pair + hidden] = da
        send[:, 2 * pair + hidden : 2 * pair + 2 * hidden] = db
        send[:, 2 * pair + 2 * hidden :] = hid


def input_kernel(group, capacity, da, db, gate, w_gate, w_up, *refs):
    outs = refs[:group]
    gate_buf, up_buf, sems = refs[group:]
    rows = da.shape[0]
    width = w_gate.shape[0]
    span = width // BACK_CUTS
    step = width // W_CHUNKS
    per = W_CHUNKS // BACK_CUTS
    me = lax.axis_index("expert")
    copies = []
    for k in range(W_CHUNKS):
        part = pl.ds(k * step, step)
        for n, (src, dst) in enumerate(((w_gate, gate_buf), (w_up, up_buf))):
            copy = pltpu.make_async_copy(src.at[part], dst.at[part], sems.at[n, k])
            copy.start()
            copies.append(copy)
    packed = BACK_CUTS * capacity
    to = iota((group * packed, rows), 0)
    at = iota((group * packed, rows), 1)
    target = (to // packed) ^ me
    within = to % packed
    match = (at // capacity == target) & (at % capacity == within % capacity)
    selects = [
        (match & (within // capacity == cut)).astype(F32).astype(BF16) for cut in range(BACK_CUTS)
    ]
    total = [jnp.zeros((group * packed, step), F32) for _ in range(per)]
    for k in range(W_CHUNKS):
        copies[2 * k].wait()
        part = nt(da[...], gate_buf[k * step : (k + 1) * step, :])
        copies[2 * k + 1].wait()
        part += nt(db[...], up_buf[k * step : (k + 1) * step, :])
        total[k % per] += nn(selects[k // per], part.astype(BF16))
    gates = nn(selects[0], gate[...])
    for n, out in enumerate(outs):
        for q in range(per):
            out[:, q * step : (q + 1) * step] = total[q][n * packed : (n + 1) * packed].astype(BF16)
        out[:, span:] = gates[n * packed : (n + 1) * packed].astype(BF16)


def weight_kernel(block, hidden, *refs):
    buffers, out = refs[:-1], refs[-1]
    start = pl.multiple_of((lax.axis_index("dp") % 2) * block, 128)
    inputs = jnp.concatenate([ref[:, pl.ds(start, block)] for ref in buffers], axis=0)
    rows = jnp.concatenate([ref[:, pl.ds(start + 2 * block, block)] for ref in buffers], axis=0)
    base = 4 * block
    for n, left in ((0, inputs), (1, inputs), (2, rows)):
        right = jnp.concatenate(
            [ref[:, base + n * hidden : base + (n + 1) * hidden] for ref in buffers], axis=0
        )
        out[n] = tn(left, right)


def combine_kernel(group, capacity, *refs):
    backs = refs[:group]
    routes, levels, slots, input_out, gate_out = refs[group:]
    tokens, width = input_out.shape
    span = width // BACK_CUTS
    packed = BACK_CUTS * capacity
    shards = group // EXPERTS_W
    me = lax.axis_index("expert")
    every = jnp.concatenate([ref[...] for ref in backs], axis=0)
    row = iota((group * packed, tokens), 0)
    expert = ((row // packed) ^ me) // shards
    within = row % packed
    slot = jnp.where(expert == 0, slots[0:1, :], slots[1:2, :])
    match = within % capacity == slot
    for cut in range(BACK_CUTS):
        pick = (match & (within // capacity == cut)).astype(F32).astype(BF16)
        total = tn(pick, every[:, 0:span])
        input_out[:, cut * span : (cut + 1) * span] = total.astype(BF16)
        if cut == 0:
            gates = tn(every[:, span:], pick)
    for k in range(2):
        route = routes[k : k + 1, :]
        value = jnp.where(route == 0, gates[0:1, :], jnp.where(route == 1, gates[1:2, :], 0.0))
        gate_out[k : k + 1, :] = value * (16.0 / levels[k : k + 1, :].astype(F32))


def swap(array, axis, size, mask):
    return lax.ppermute(array, axis, [(n, n ^ mask) for n in range(size)])


def plain_weights(inputs, grads, rights):
    inputs = lax.all_to_all(inputs, "dp", split_axis=1, concat_axis=0, tiled=True)
    grads = lax.all_to_all(grads, "dp", split_axis=1, concat_axis=0, tiled=True)
    rights = [lax.all_gather(right, "dp", axis=0, tiled=True) for right in rights]
    return jnp.stack([tn(inputs, rights[0]), tn(inputs, rights[1]), tn(grads, rights[2])])


def per_device(grad_out, routes, gate_levels, saved_inputs, w_gate, w_up, w_down):
    group = lax.axis_size("expert")
    n_dp = lax.axis_size("dp")
    shards = group // EXPERTS_W
    rows, width = saved_inputs.shape
    capacity = rows // group
    hidden = w_gate.shape[1]
    tokens = grad_out.shape[0]
    block = width // n_dp
    paired = n_dp == PAIRED
    routes = routes.T
    gate_levels = gate_levels.T
    shape = jax.ShapeDtypeStruct
    weight_bytes = w_gate.size * 2
    product = 2 * rows * width * hidden

    packed = shape((SEND_CUTS * capacity, width // SEND_CUTS), BF16)
    own, other, slots = call(
        functools.partial(pick_kernel, shards, capacity),
        (packed, packed, shape((8, tokens), jnp.int32)),
        (routes, gate_levels, grad_out),
        [VMEM] * 3,
        flops=4 * packed.size * tokens,
        moved=grad_out.size * 2,
        name="pick",
    )
    received = [own] + [
        swap(own if mask < shards else other, "expert", group, mask) for mask in range(1, group)
    ]
    part = shape((rows, hidden), F32)
    weights_scratch = [
        pltpu.VMEM((width, hidden), BF16),
        pltpu.VMEM((width, hidden), BF16),
        pltpu.SemaphoreType.DMA((2, W_CHUNKS)),
    ]
    u, v, h = call(
        hidden_kernel,
        (part,) * 3,
        (saved_inputs, w_gate, w_up),
        [VMEM, HBM, HBM],
        weights_scratch,
        flops=2 * product,
        moved=2 * weight_bytes,
        name="hidden",
    )
    half = shape((rows, hidden), BF16)
    chips = n_dp // 2 if paired else 0
    late = shape((rows, 4 * block + 3 * hidden), BF16)
    outward = (late,) * chips if paired else (shape((rows, width), BF16), half)
    *sends, da, db, gate = call(
        functools.partial(project_kernel, group, capacity, n_dp),
        outward + (half, half, shape((rows, GATE_LANES), BF16)),
        (*received, w_down, u, v, h, saved_inputs),
        [VMEM] * group + [HBM] + [VMEM] * 4,
        [
            pltpu.VMEM((hidden, width), BF16),
            pltpu.VMEM((rows, width), BF16),
            pltpu.SemaphoreType.DMA((SEND_CUTS,)),
        ],
        flops=product,
        moved=weight_bytes,
        name="project",
    )
    back = shape((BACK_CUTS * capacity, width // BACK_CUTS + GATE_LANES), BF16)
    returns = call(
        functools.partial(input_kernel, group, capacity),
        (back,) * group,
        (da, db, gate, w_gate, w_up),
        [VMEM] * 3 + [HBM] * 2,
        weights_scratch,
        flops=2 * product,
        moved=2 * weight_bytes,
        name="input",
    )
    backs = [returns[0]] + [swap(returns[n], "expert", group, n) for n in range(1, group)]
    if paired:
        buffers = [sends[0]] + [swap(sends[m], "dp", n_dp, 2 * m) for m in range(1, chips)]
        buffers += [swap(buffer, "dp", n_dp, 1) for buffer in buffers]
        weight_grad = call(
            functools.partial(weight_kernel, block, hidden),
            shape((3, block, hidden), F32),
            buffers,
            [VMEM] * (2 * chips),
            flops=6 * n_dp * rows * block * hidden,
            moved=2 * chips * late.size * 2,
            name="weight",
        )
    else:
        weight_grad = plain_weights(saved_inputs, sends[0], (da, db, sends[1]))
    input_grad, gate_grad = call(
        functools.partial(combine_kernel, group, capacity),
        (shape((tokens, width), BF16), shape((2, tokens), F32)),
        (*backs, routes, gate_levels, slots),
        [VMEM] * (group + 3),
        flops=2 * group * back.size * tokens,
        moved=2 * tokens * width,
        name="combine",
    )
    return input_grad, gate_grad.T, weight_grad.transpose(1, 0, 2)


def solution(mesh):
    in_specs = (
        P(("dp", "expert"), None),
        P(("dp", "expert"), None),
        P(("dp", "expert"), None),
        P(("dp", "expert"), None),
        P(None, "expert"),
        P(None, "expert"),
        P("expert", None),
    )
    out_specs = (P(("dp", "expert"), None), P(("dp", "expert"), None), P("dp", None, "expert"))
    return jax.shard_map(
        per_device, mesh=mesh, in_specs=in_specs, out_specs=out_specs, check_vma=False
    )
```

time: 253 us -> 60.8 us (0.24)
  waiting for transfers between devices: 174 us -> 23 us
  matrix products: 28.7 us -> 0 us
  Pallas kernels: 0 us -> 13.4 us
  between operations: 13.9 us -> 0.75 us
  other arithmetic: 6.89 us -> 0 us
  local copies, waits for them, and re-layouts: 12 us -> 7.53 us
    reduce_scatter x3 -> x0, waiting for transfers between devices: 156 us -> none  [the longest x1 65.5 us: per_device(): lax.psum_scatter(rows_product(saved_inputs, d_up), 'dp', scatter_dimensio...]
    dot_general x12 -> x0, matrix products: 28.7 us -> none  [the longest x3 13.2 us: rows_product(): lax.dot_general(left, right, (((0,), (0,)), ((), ())), preferred_element_...]
    ppermute x0 -> x13, waiting for transfers between devices: none -> 23 us  [swap(): return lax.ppermute(array, axis, [(n, n ^ mask) for n in range(size)])]
    all_to_all x4 -> x0, waiting for transfers between devices: 18 us -> none  [the longest x1 6.8 us: per_device(): lax.all_to_all(input_part.reshape(group, capacity, width), 'expert', spli...]
    all_to_all x4 -> x0, starting transfers between devices: 17.1 us -> none  [the longest x1 6.32 us: per_device(): lax.all_to_all(send_gate, 'expert', split_axis=0, concat_axis=0, tiled=True)]
    ppermute x0 -> x13, starting transfers between devices: none -> 15.9 us  [swap(): return lax.ppermute(array, axis, [(n, n ^ mask) for n in range(size)])]
    pallas_call x0 -> x6, Pallas kernels: none -> 13.4 us  [call(): pl.pallas_call(kernel, out_shape=outs, in_specs=specs, out_specs=jax.tree...]
    another operation x3 -> x0, other arithmetic: 3.97 us -> none  [the longest x1 3.17 us: per_device(): weight_grad = jnp.stack([gate_share, up_share, down_share], axis=1)]
  transfers between devices with their start and end apart: 7 -> 13, of which waited for: 7 -> 5; matrix products, arithmetic and copies ran while one was open for 10% -> 0% of each run, Pallas kernels for 0% -> 13%
where the time goes in v1:
time: 60.8 us; the launch traced here: 60.5 us
  waiting for transfers between devices  23 us (38%)
  starting transfers between devices  15.9 us (26%)
  Pallas kernels  13.4 us (22%)
  local copies, waits for them, and re-layouts  7.53 us (12%)
  between operations  0.75 us (1%)
    ppermute x13, waiting for transfers between devices, swap(): return lax.ppermute(array, axis, [(n, n ^ mask) for n in range(size)])  23 us
    ppermute x13, starting transfers between devices, swap(): return lax.ppermute(array, axis, [(n, n ^ mask) for n in range(size)])  15.9 us
    pallas_call x6, Pallas kernels, call(): pl.pallas_call(kernel, out_shape=outs, in_specs=specs, out_specs=jax.tree...  13.4 us
    unnamed x24, local copies, waits for them, and re-layouts  7.53 us
  transfers between devices with their start and end apart: 13, of which 5 were waited for; matrix products, arithmetic and copies ran while one was open for 0% of the time, Pallas kernels for 13%

profile of v1, /device:TPU:0, one launch (start us, length us, event | category | flops | bytes accessed | tf_op | source)
XLA Modules:
  0.0 60.5 jit_solution(15383243230698950206)
XLA Ops:
  0.6 0.0 copy-start.5
  0.6 1.4 %copy-done.5 = bf16[256,3072]{1,0:T(8,128)(2,1)S(1)} copy-done((bf16[256,3072]{1,0:T(8,128)(2,1)S(1)}, bf16[256,3072]{1,0:T(8,128)(2,1)}, u32[]{:S(2)}) %copy-start.5) | copy-done | bytes 1572888
  2.0 0.0 copy-start.8
  2.0 0.7 %copy-done.8 = s32[256,2]{0,1:T(2,128)S(1)} copy-done((s32[256,2]{0,1:T(2,128)S(1)}, s32[256,2]{0,1:T(2,128)}, u32[]{:S(2)}) %copy-start.8) | copy-done | bytes 2072
  2.7 0.0 copy-start.10
  2.7 0.7 %copy-done.10 = s32[256,2]{0,1:T(2,128)S(1)} copy-done((s32[256,2]{0,1:T(2,128)S(1)}, s32[256,2]{0,1:T(2,128)}, u32[]{:S(2)}) %copy-start.10) | copy-done | bytes 2072
  3.4 0.8 %pick.1 = (bf16[48,768]{1,0:T(8,128)(2,1)S(1)}, bf16[48,768]{1,0:T(8,128)(2,1)S(1)}, s32[8,256]{1,0:T(8,128)S(1)}) custom-call(s32[2,256]{1,0:T(2,128)S(1)} %bitcast.4, s32[2,256]{1,0:T(2,128)S(1)} %bitcast.6, bf16[256,3072]{1,0:T(8,128)(2,1)S(1)} %copy-done.5), custom_call_target="tpu_custom_call" | custom-call | flops 37748736 | bytes 1572864 | tf_op jit(solution)/shard_map/pick/pallas_call | solution.py:39
  4.2 3.1 %collective-permute-start = (bf16[48,768]{1,0:T(8,128)(2,1)S(1)}, bf16[48,768]{1,0:T(8,128)(2,1)S(1)}, u32[]{:S(2)}, u32[]{:S(2)}) collective-permute-start(bf16[48,768]{1,0:T(8,128)(2,1)S(1)} %get-tuple-element.22.refs_0_), channel_id=1, source_target_pairs={{0,1},{1,0},{2,3},{3,2},{4,5},{5,4},{6,7},{7,6},{8,9},{9,8},{10,11... | collective-permute-start | bytes 221192 | tf_op jit(solution)/shard_map/ppermute | solution.py:234
  7.3 2.6 %collective-permute-start.1 = (bf16[48,768]{1,0:T(8,128)(2,1)S(1)}, bf16[48,768]{1,0:T(8,128)(2,1)S(1)}, u32[]{:S(2)}, u32[]{:S(2)}) collective-permute-start(bf16[48,768]{1,0:T(8,128)(2,1)S(1)} %get-tuple-element.23), channel_id=1, source_target_pairs={{0,2},{1,3},{2,0},{3,1},{4,6},{5,7},{6,4},{7,5},{8,10},{9,11},{10,... | collective-permute-start | bytes 221192 | tf_op jit(solution)/shard_map/ppermute | solution.py:234
  9.9 0.0 collective-permute-start.2
  9.9 0.0 copy-start
  9.9 1.9 %copy-done = bf16[3072,512]{1,0:T(8,128)(2,1)S(1)} copy-done((bf16[3072,512]{1,0:T(8,128)(2,1)S(1)}, bf16[3072,512]{1,0:T(8,128)(2,1)}, u32[]{:S(2)}) %copy-start) | copy-done | bytes 3145752
  11.8 0.0 copy-start.2
  11.8 1.9 %copy-done.2 = bf16[3072,512]{1,0:T(8,128)(2,1)S(1)} copy-done((bf16[3072,512]{1,0:T(8,128)(2,1)S(1)}, bf16[3072,512]{1,0:T(8,128)(2,1)}, u32[]{:S(2)}) %copy-start.2) | copy-done | bytes 3145752
  13.7 0.0 copy-start.6
  13.7 1.0 %copy-done.6 = bf16[48,3072]{1,0:T(8,128)(2,1)S(1)} copy-done((bf16[48,3072]{1,0:T(8,128)(2,1)S(1)}, bf16[48,3072]{1,0:T(8,128)(2,1)}, u32[]{:S(2)}) %copy-start.6) | copy-done | bytes 294936
  14.6 0.0 copy-start.4
  14.6 0.0 copy-start.7
  14.6 0.0 copy-start.3
  14.6 2.0 %hidden.1 = (f32[48,512]{1,0:T(8,128)S(1)}, f32[48,512]{1,0:T(8,128)S(1)}, f32[48,512]{1,0:T(8,128)S(1)}) custom-call(bf16[48,3072]{1,0:T(8,128)(2,1)S(1)} %copy-done.6, bf16[3072,512]{1,0:T(8,128)(2,1)S(1)} %copy-done, bf16[3072,512]{1,0:T(8,128)(2,1)S(1)} %copy-done.2), custom_call_target="tpu_custom_call" | custom-call | flops 301989888 | bytes 6291456 | tf_op jit(solution)/shard_map/hidden/pallas_call | solution.py:39
  16.6 0.0 copy-start.1
  16.6 0.0 collective-permute-done.refs_1_
  16.6 0.0 collective-permute-done.1.refs_2_
  16.6 0.0 collective-permute-done.2.refs_3_
  16.6 0.0 copy-done.4
  16.7 0.0 copy-done.7
  16.7 2.4 %project.1 = (bf16[48,3072]{1,0:T(8,128)(2,1)S(1)}, bf16[48,3072]{1,0:T(8,128)(2,1)S(1)}, bf16[48,3072]{1,0:T(8,128)(2,1)S(1)}, bf16[48,3072]{1,0:T(8,128)(2,1)S...) custom-call(bf16[48,768]{1,0:T(8,128)(2,1)S(1)} %get-tuple-element.22.refs_0_, ...), custom_call_target="tpu_custom_call" | custom-call | flops 150994944 | bytes 3145728 | tf_op jit(solution)/shard_map/project/pallas_call | solution.py:39
  19.0 1.8 %collective-permute-start.6 = (bf16[48,3072]{1,0:T(8,128)(2,1)S(1)}, bf16[48,3072]{1,0:T(8,128)(2,1)S(1)}, u32[]{:S(2)}, u32[]{:S(2)}) collective-permute-start(bf16[48,3072]{1,0:T(8,128)(2,1)S(1)} %get-tuple-element.38), channel_id=1, source_target_pairs={{0,8},{4,12},{8,0},{12,4},{16,24},{20,28},{24,16},{28,20},{1,9},{5... | collective-permute-start | bytes 884744 | tf_op jit(solution)/shard_map/ppermute | solution.py:234
  20.8 1.5 %collective-permute-start.7 = (bf16[48,3072]{1,0:T(8,128)(2,1)S(1)}, bf16[48,3072]{1,0:T(8,128)(2,1)S(1)}, u32[]{:S(2)}, u32[]{:S(2)}) collective-permute-start(bf16[48,3072]{1,0:T(8,128)(2,1)S(1)} %get-tuple-element.39), channel_id=1, source_target_pairs={{0,16},{4,20},{8,24},{12,28},{16,0},{20,4},{24,8},{28,12},{1,17},{... | collective-permute-start | bytes 884744 | tf_op jit(solution)/shard_map/ppermute | solution.py:234
  22.3 0.3 collective-permute-start.8
  22.6 0.0 collective-permute-start.9
  22.6 6.5 %collective-permute-done.6.refs_1_ = bf16[48,3072]{1,0:T(8,128)(2,1)S(1)} collective-permute-done((bf16[48,3072]{1,0:T(8,128)(2,1)S(1)}, bf16[48,3072]{1,0:T(8,128)(2,1)S(1)}, u32[]{:S(2)}, u32[]{:S(2)}) %collective-permute-start.6) | collective-permute-done | bytes 294944 | tf_op jit(solution)/shard_map/ppermute | solution.py:234
  29.1 0.0 collective-permute-start.10
  29.1 5.8 %collective-permute-done.7.refs_2_ = bf16[48,3072]{1,0:T(8,128)(2,1)S(1)} collective-permute-done((bf16[48,3072]{1,0:T(8,128)(2,1)S(1)}, bf16[48,3072]{1,0:T(8,128)(2,1)S(1)}, u32[]{:S(2)}, u32[]{:S(2)}) %collective-permute-start.7) | collective-permute-done | bytes 294944 | tf_op jit(solution)/shard_map/ppermute | solution.py:234
  34.8 0.0 collective-permute-start.11
  34.8 0.0 collective-permute-done.8.refs_3_
  34.8 0.5 collective-permute-start.12
  35.3 0.0 copy-done.3
  35.4 0.0 copy-done.1
  35.4 0.0 copy-start.9
  35.4 0.0 copy-start.11
  35.4 4.1 %input.1 = (bf16[24,1664]{1,0:T(8,128)(2,1)S(1)}, bf16[24,1664]{1,0:T(8,128)(2,1)S(1)}, bf16[24,1664]{1,0:T(8,128)(2,1)S(1)}, bf16[24,1664]{1,0:T(8,128)(2,1)S(1)}) custom-call(bf16[48,512]{1,0:T(8,128)(2,1)S(1)} %get-tuple-element.27.da, bf16[48,512]{1,0:T(8,128)(2,1)S(1)} %get-tuple-element.28.db, bf16[48,128]{1,0:T(8,128)(2,1)S(1)} %get-tuple-element.29.gate, ...), custom_call_target="tpu_custom_call" | custom-call | flops 301989888 | bytes 6291456 | tf_op jit(solution)/shard_map/input/pallas_call | solution.py:39
  39.5 0.7 %collective-permute-start.3 = (bf16[24,1664]{1,0:T(8,128)(2,1)S(1)}, bf16[24,1664]{1,0:T(8,128)(2,1)S(1)}, u32[]{:S(2)}, u32[]{:S(2)}) collective-permute-start(bf16[24,1664]{1,0:T(8,128)(2,1)S(1)} %get-tuple-element.31), channel_id=1, source_target_pairs={{0,1},{1,0},{2,3},{3,2},{4,5},{5,4},{6,7},{7,6},{8,9},{9,8},{10,11... | collective-permute-start | bytes 239624 | tf_op jit(solution)/shard_map/ppermute | solution.py:234
  40.1 3.8 %collective-permute-done.3.refs_1_ = bf16[24,1664]{1,0:T(8,128)(2,1)S(1)} collective-permute-done((bf16[24,1664]{1,0:T(8,128)(2,1)S(1)}, bf16[24,1664]{1,0:T(8,128)(2,1)S(1)}, u32[]{:S(2)}, u32[]{:S(2)}) %collective-permute-start.3) | collective-permute-done | bytes 79904 | tf_op jit(solution)/shard_map/ppermute | solution.py:234
  43.9 2.3 %collective-permute-start.4 = (bf16[24,1664]{1,0:T(8,128)(2,1)S(1)}, bf16[24,1664]{1,0:T(8,128)(2,1)S(1)}, u32[]{:S(2)}, u32[]{:S(2)}) collective-permute-start(bf16[24,1664]{1,0:T(8,128)(2,1)S(1)} %get-tuple-element.32), channel_id=1, source_target_pairs={{0,2},{1,3},{2,0},{3,1},{4,6},{5,7},{6,4},{7,5},{8,10},{9,11},{10,... | collective-permute-start | bytes 239624 | tf_op jit(solution)/shard_map/ppermute | solution.py:234
  46.2 3.9 %collective-permute-done.4.refs_2_ = bf16[24,1664]{1,0:T(8,128)(2,1)S(1)} collective-permute-done((bf16[24,1664]{1,0:T(8,128)(2,1)S(1)}, bf16[24,1664]{1,0:T(8,128)(2,1)S(1)}, u32[]{:S(2)}, u32[]{:S(2)}) %collective-permute-start.4) | collective-permute-done | bytes 79904 | tf_op jit(solution)/shard_map/ppermute | solution.py:234
  50.1 3.2 %collective-permute-start.5 = (bf16[24,1664]{1,0:T(8,128)(2,1)S(1)}, bf16[24,1664]{1,0:T(8,128)(2,1)S(1)}, u32[]{:S(2)}, u32[]{:S(2)}) collective-permute-start(bf16[24,1664]{1,0:T(8,128)(2,1)S(1)} %get-tuple-element.33), channel_id=1, source_target_pairs={{0,3},{1,2},{2,1},{3,0},{4,7},{5,6},{6,5},{7,4},{8,11},{9,10},{10,... | collective-permute-start | bytes 239624 | tf_op jit(solution)/shard_map/ppermute | solution.py:234
  53.3 3.0 %collective-permute-done.5.refs_3_ = bf16[24,1664]{1,0:T(8,128)(2,1)S(1)} collective-permute-done((bf16[24,1664]{1,0:T(8,128)(2,1)S(1)}, bf16[24,1664]{1,0:T(8,128)(2,1)S(1)}, u32[]{:S(2)}, u32[]{:S(2)}) %collective-permute-start.5) | collective-permute-done | bytes 79904 | tf_op jit(solution)/shard_map/ppermute | solution.py:234
  56.3 0.0 copy-done.9
  56.3 0.0 copy-done.11
  56.3 1.9 %combine.1 = (bf16[256,3072]{1,0:T(8,128)(2,1)}, f32[2,256]{1,0:T(2,128)}) custom-call(bf16[24,1664]{1,0:T(8,128)(2,1)S(1)} %get-tuple-element.30.refs_0_, bf16[24,1664]{1,0:T(8,128)(2,1)S(1)} %collective-permute-done.3.refs_1_, bf16[24,1664]{1,0:T(8,128)(2,1)S(1)} %collective-permute-done.4.refs_2_, bf16[24,1664]{1,0:T(8,128)(2,1)S(1)} %collective-permute-done.5.refs_3_, ...), custom_call_target="tpu_custom_call" | custom-call | flops 81788928 | bytes 1572864 | tf_op jit(solution)/shard_map/combine/pallas_call | solution.py:39
  58.2 0.0 collective-permute-done.9.refs_4_
  58.2 0.0 collective-permute-done.10.refs_5_
  58.2 0.0 collective-permute-done.11.refs_6_
  58.2 0.0 collective-permute-done.12.refs_7_
  58.2 2.2 %weight.1 = f32[3,384,512]{2,1,0:T(8,128)} custom-call(bf16[48,3072]{1,0:T(8,128)(2,1)S(1)} %get-tuple-element.37.refs_0_, bf16[48,3072]{1,0:T(8,128)(2,1)S(1)} %collective-permute-done.6.refs_1_, bf16[48,3072]{1,0:T(8,128)(2,1)S(1)} %collective-permute-done.7.refs_2_, bf16[48,3072]{1,0:T(8,128)(2,1)S(1)} %collective-permute-done.8.refs_3_, ...), custom_call_target="tpu_custom_call" | custom-call | flops 452984832 | bytes 2359296 | tf_op jit(solution)/shard_map/weight/pallas_call | solution.py:39
Async XLA Ops:
  0.6 1.4 %copy-start.5 = (bf16[256,3072]{1,0:T(8,128)(2,1)S(1)}, bf16[256,3072]{1,0:T(8,128)(2,1)}, u32[]{:S(2)}) copy-start(bf16[256,3072]{1,0:T(8,128)(2,1)} %grad.1) | copy-start | bytes 4718596
  2.0 0.7 %copy-start.8 = (s32[256,2]{0,1:T(2,128)S(1)}, s32[256,2]{0,1:T(2,128)}, u32[]{:S(2)}) copy-start(s32[256,2]{0,1:T(2,128)} %param.8) | copy-start | bytes 6148
  2.7 0.7 %copy-start.10 = (s32[256,2]{0,1:T(2,128)S(1)}, s32[256,2]{0,1:T(2,128)}, u32[]{:S(2)}) copy-start(s32[256,2]{0,1:T(2,128)} %param.9) | copy-start | bytes 6148
  4.2 12.4 %collective-permute-start = (bf16[48,768]{1,0:T(8,128)(2,1)S(1)}, bf16[48,768]{1,0:T(8,128)(2,1)S(1)}, u32[]{:S(2)}, u32[]{:S(2)}) collective-permute-start(bf16[48,768]{1,0:T(8,128)(2,1)S(1)} %get-tuple-element.22.refs_0_), channel_id=1, source_target_pairs={{0,1},{1,0},{2,3},{3,2},{4,5},{5,4},{6,7},{7,6},{8,9},{9,8},{10,11... | collective-permute-start | bytes 221192 | tf_op jit(solution)/shard_map/ppermute | solution.py:234
  7.3 9.3 %collective-permute-start.1 = (bf16[48,768]{1,0:T(8,128)(2,1)S(1)}, bf16[48,768]{1,0:T(8,128)(2,1)S(1)}, u32[]{:S(2)}, u32[]{:S(2)}) collective-permute-start(bf16[48,768]{1,0:T(8,128)(2,1)S(1)} %get-tuple-element.23), channel_id=1, source_target_pairs={{0,2},{1,3},{2,0},{3,1},{4,6},{5,7},{6,4},{7,5},{8,10},{9,11},{10,... | collective-permute-start | bytes 221192 | tf_op jit(solution)/shard_map/ppermute | solution.py:234
  9.9 6.8 %collective-permute-start.2 = (bf16[48,768]{1,0:T(8,128)(2,1)S(1)}, bf16[48,768]{1,0:T(8,128)(2,1)S(1)}, u32[]{:S(2)}, u32[]{:S(2)}) collective-permute-start(bf16[48,768]{1,0:T(8,128)(2,1)S(1)} %get-tuple-element.23), channel_id=1, source_target_pairs={{0,3},{1,2},{2,1},{3,0},{4,7},{5,6},{6,5},{7,4},{8,11},{9,10},{10,... | collective-permute-start | bytes 221192 | tf_op jit(solution)/shard_map/ppermute | solution.py:234
  9.9 1.9 %copy-start = (bf16[3072,512]{1,0:T(8,128)(2,1)S(1)}, bf16[3072,512]{1,0:T(8,128)(2,1)}, u32[]{:S(2)}) copy-start(bf16[3072,512]{1,0:T(8,128)(2,1)} %w_gate.3) | copy-start | bytes 9437188
  11.8 1.9 %copy-start.2 = (bf16[3072,512]{1,0:T(8,128)(2,1)S(1)}, bf16[3072,512]{1,0:T(8,128)(2,1)}, u32[]{:S(2)}) copy-start(bf16[3072,512]{1,0:T(8,128)(2,1)} %w_up.3) | copy-start | bytes 9437188
  13.7 1.0 %copy-start.6 = (bf16[48,3072]{1,0:T(8,128)(2,1)S(1)}, bf16[48,3072]{1,0:T(8,128)(2,1)}, u32[]{:S(2)}) copy-start(bf16[48,3072]{1,0:T(8,128)(2,1)} %refs_8_.1) | copy-start | bytes 884740
  14.6 2.0 %copy-start.4 = (bf16[512,3072]{1,0:T(8,128)(2,1)S(1)}, bf16[512,3072]{1,0:T(8,128)(2,1)}, u32[]{:S(2)}) copy-start(bf16[512,3072]{1,0:T(8,128)(2,1)} %refs_4_.1) | copy-start | bytes 9437188
  14.6 2.0 %copy-start.7 = (bf16[48,3072]{1,0:T(8,128)(2,1)S(1)}, bf16[48,3072]{1,0:T(8,128)(2,1)}, u32[]{:S(2)}) copy-start(bf16[48,3072]{1,0:T(8,128)(2,1)} %refs_8_.1) | copy-start | bytes 884740
  14.6 20.7 %copy-start.3 = (bf16[3072,512]{1,0:T(8,128)(2,1)S(1)}, bf16[3072,512]{1,0:T(8,128)(2,1)}, u32[]{:S(2)}) copy-start(bf16[3072,512]{1,0:T(8,128)(2,1)} %w_up.3) | copy-start | bytes 9437188
  16.6 18.8 %copy-start.1 = (bf16[3072,512]{1,0:T(8,128)(2,1)S(1)}, bf16[3072,512]{1,0:T(8,128)(2,1)}, u32[]{:S(2)}) copy-start(bf16[3072,512]{1,0:T(8,128)(2,1)} %w_gate.3) | copy-start | bytes 9437188
  19.0 10.0 %collective-permute-start.6 = (bf16[48,3072]{1,0:T(8,128)(2,1)S(1)}, bf16[48,3072]{1,0:T(8,128)(2,1)S(1)}, u32[]{:S(2)}, u32[]{:S(2)}) collective-permute-start(bf16[48,3072]{1,0:T(8,128)(2,1)S(1)} %get-tuple-element.38), channel_id=1, source_target_pairs={{0,8},{4,12},{8,0},{12,4},{16,24},{20,28},{24,16},{28,20},{1,9},{5... | collective-permute-start | bytes 884744 | tf_op jit(solution)/shard_map/ppermute | solution.py:234
  20.8 14.0 %collective-permute-start.7 = (bf16[48,3072]{1,0:T(8,128)(2,1)S(1)}, bf16[48,3072]{1,0:T(8,128)(2,1)S(1)}, u32[]{:S(2)}, u32[]{:S(2)}) collective-permute-start(bf16[48,3072]{1,0:T(8,128)(2,1)S(1)} %get-tuple-element.39), channel_id=1, source_target_pairs={{0,16},{4,20},{8,24},{12,28},{16,0},{20,4},{24,8},{28,12},{1,17},{... | collective-permute-start | bytes 884744 | tf_op jit(solution)/shard_map/ppermute | solution.py:234
  22.3 12.5 %collective-permute-start.8 = (bf16[48,3072]{1,0:T(8,128)(2,1)S(1)}, bf16[48,3072]{1,0:T(8,128)(2,1)S(1)}, u32[]{:S(2)}, u32[]{:S(2)}) collective-permute-start(bf16[48,3072]{1,0:T(8,128)(2,1)S(1)} %get-tuple-element.40), channel_id=1, source_target_pairs={{0,24},{4,28},{8,16},{12,20},{16,8},{20,12},{24,0},{28,4},{1,25},{... | collective-permute-start | bytes 884744 | tf_op jit(solution)/shard_map/ppermute | solution.py:234
  22.6 35.6 %collective-permute-start.9 = (bf16[48,3072]{1,0:T(8,128)(2,1)S(1)}, bf16[48,3072]{1,0:T(8,128)(2,1)S(1)}, u32[]{:S(2)}, u32[]{:S(2)}) collective-permute-start(bf16[48,3072]{1,0:T(8,128)(2,1)S(1)} %get-tuple-element.37.refs_0_), channel_id=1, source_target_pairs={{0,4},{4,0},{8,12},{12,8},{16,20},{20,16},{24,28},{28,24},{1,5},{5... | collective-permute-start | bytes 884744 | tf_op jit(solution)/shard_map/ppermute | solution.py:234
  29.1 29.2 %collective-permute-start.10 = (bf16[48,3072]{1,0:T(8,128)(2,1)S(1)}, bf16[48,3072]{1,0:T(8,128)(2,1)S(1)}, u32[]{:S(2)}, u32[]{:S(2)}) collective-permute-start(bf16[48,3072]{1,0:T(8,128)(2,1)S(1)} %collective-permute-done.6.refs_1_), channel_id=1, source_target_pairs={{0,4},{4,0},{8,12},{12,8},{16,20},{20,16},{24,28},{28,24},{1,5},{5... | collective-permute-start | bytes 884744 | tf_op jit(solution)/shard_map/ppermute | solution.py:234
  34.8 23.4 %collective-permute-start.11 = (bf16[48,3072]{1,0:T(8,128)(2,1)S(1)}, bf16[48,3072]{1,0:T(8,128)(2,1)S(1)}, u32[]{:S(2)}, u32[]{:S(2)}) collective-permute-start(bf16[48,3072]{1,0:T(8,128)(2,1)S(1)} %collective-permute-done.7.refs_2_), channel_id=1, source_target_pairs={{0,4},{4,0},{8,12},{12,8},{16,20},{20,16},{24,28},{28,24},{1,5},{5... | collective-permute-start | bytes 884744 | tf_op jit(solution)/shard_map/ppermute | solution.py:234
  34.8 23.4 %collective-permute-start.12 = (bf16[48,3072]{1,0:T(8,128)(2,1)S(1)}, bf16[48,3072]{1,0:T(8,128)(2,1)S(1)}, u32[]{:S(2)}, u32[]{:S(2)}) collective-permute-start(bf16[48,3072]{1,0:T(8,128)(2,1)S(1)} %collective-permute-done.8.refs_3_), channel_id=1, source_target_pairs={{0,4},{4,0},{8,12},{12,8},{16,20},{20,16},{24,28},{28,24},{1,5},{5... | collective-permute-start | bytes 884744 | tf_op jit(solution)/shard_map/ppermute | solution.py:234
  35.4 21.0 %copy-start.9 = (s32[256,2]{0,1:T(2,128)S(1)}, s32[256,2]{0,1:T(2,128)}, u32[]{:S(2)}) copy-start(s32[256,2]{0,1:T(2,128)} %param.8) | copy-start | bytes 6148
  35.4 21.0 %copy-start.11 = (s32[256,2]{0,1:T(2,128)S(1)}, s32[256,2]{0,1:T(2,128)}, u32[]{:S(2)}) copy-start(s32[256,2]{0,1:T(2,128)} %param.9) | copy-start | bytes 6148
  39.5 4.5 %collective-permute-start.3 = (bf16[24,1664]{1,0:T(8,128)(2,1)S(1)}, bf16[24,1664]{1,0:T(8,128)(2,1)S(1)}, u32[]{:S(2)}, u32[]{:S(2)}) collective-permute-start(bf16[24,1664]{1,0:T(8,128)(2,1)S(1)} %get-tuple-element.31), channel_id=1, source_target_pairs={{0,1},{1,0},{2,3},{3,2},{4,5},{5,4},{6,7},{7,6},{8,9},{9,8},{10,11... | collective-permute-start | bytes 239624 | tf_op jit(solution)/shard_map/ppermute | solution.py:234
  43.9 6.2 %collective-permute-start.4 = (bf16[24,1664]{1,0:T(8,128)(2,1)S(1)}, bf16[24,1664]{1,0:T(8,128)(2,1)S(1)}, u32[]{:S(2)}, u32[]{:S(2)}) collective-permute-start(bf16[24,1664]{1,0:T(8,128)(2,1)S(1)} %get-tuple-element.32), channel_id=1, source_target_pairs={{0,2},{1,3},{2,0},{3,1},{4,6},{5,7},{6,4},{7,5},{8,10},{9,11},{10,... | collective-permute-start | bytes 239624 | tf_op jit(solution)/shard_map/ppermute | solution.py:234
  50.1 6.2 %collective-permute-start.5 = (bf16[24,1664]{1,0:T(8,128)(2,1)S(1)}, bf16[24,1664]{1,0:T(8,128)(2,1)S(1)}, u32[]{:S(2)}, u32[]{:S(2)}) collective-permute-start(bf16[24,1664]{1,0:T(8,128)(2,1)S(1)} %get-tuple-element.33), channel_id=1, source_target_pairs={{0,3},{1,2},{2,1},{3,0},{4,7},{5,6},{6,5},{7,4},{8,11},{9,10},{10,... | collective-permute-start | bytes 239624 | tf_op jit(solution)/shard_map/ppermute | solution.py:234

commit v2 on v1

v2 whole, which is shorter than its diff:
```python
import functools

import jax
import jax.numpy as jnp
from jax import lax
from jax.experimental import pallas as pl
from jax.experimental.pallas import tpu as pltpu
from jax.sharding import PartitionSpec as P

EXPERTS_W = 2
SEND_CUTS = 4
BACK_CUTS = 2
GATE_LANES = 128
W_CHUNKS = 4
PAIRED = 8
F32 = jnp.float32
BF16 = jnp.bfloat16
VMEM = pl.BlockSpec(memory_space=pltpu.VMEM)
HBM = pl.BlockSpec(memory_space=pltpu.HBM)


def nn(left, right):
    return lax.dot_general(left, right, (((1,), (0,)), ((), ())), preferred_element_type=F32)


def nt(left, right):
    return lax.dot_general(left, right, (((1,), (1,)), ((), ())), preferred_element_type=F32)


def tn(left, right):
    return lax.dot_general(left, right, (((0,), (0,)), ((), ())), preferred_element_type=F32)


def iota(shape, dim):
    return lax.broadcasted_iota(jnp.int32, shape, dim)


def call(kernel, outs, args, specs, scratch=(), vmem=24, name=None):
    return pl.pallas_call(
        kernel,
        out_shape=outs,
        in_specs=specs,
        out_specs=jax.tree.map(lambda _: VMEM, outs),
        scratch_shapes=scratch,
        compiler_params=pltpu.CompilerParams(vmem_limit_bytes=vmem * 1024 * 1024),
        cost_estimate=pl.CostEstimate(flops=0, bytes_accessed=0, transcendentals=0),
        name=name,
    )(*args)


def pick_kernel(
    shards, capacity, routes_hbm, levels_hbm, grad_hbm, own_out, other_out, slots_out,
    routes, levels, grad, sems,
):
    tokens, width = grad.shape
    span = width // SEND_CUTS
    rows = SEND_CUTS * capacity
    small = [
        pltpu.make_async_copy(routes_hbm, routes, sems.at[0]),
        pltpu.make_async_copy(levels_hbm, levels, sems.at[1]),
    ]
    large = [
        pltpu.make_async_copy(
            grad_hbm.at[:, pl.ds(cut * span, span)],
            grad.at[:, pl.ds(cut * span, span)],
            sems.at[2 + cut],
        )
        for cut in range(SEND_CUTS)
    ]
    for copy in small + large:
        copy.start()
    mine = lax.axis_index("expert") // shards
    upto = (iota((tokens, tokens), 0) <= iota((tokens, tokens), 1)).astype(BF16)
    for copy in small:
        copy.wait()
    first, second = routes[0:1, :], routes[1:2, :]
    found = jnp.zeros((8, tokens), F32)
    for expert in range(EXPERTS_W):
        hit = ((first == expert) | (second == expert)).astype(F32)
        found = jnp.where(iota((8, tokens), 0) == expert, hit, found)
    counted = nn(found.astype(BF16), upto)
    slots = jnp.where(found > 0, counted - 1.0, -4096.0).astype(jnp.int32)
    slots_out[...] = slots
    slot_of, gate_of = [], []
    for expert in (mine, 1 - mine):
        level = jnp.where(first == expert, levels[0:1, :], levels[1:2, :])
        slot_of.append(jnp.where(expert == 0, slots[0:1, :], slots[1:2, :]))
        gate_of.append(level.astype(F32) * (1.0 / 16.0))
    row = iota((2 * rows, tokens), 0)
    slot = jnp.where(row < rows, slot_of[0], slot_of[1])
    gate = jnp.where(row < rows, gate_of[0], gate_of[1])
    place = row % rows
    total = jnp.zeros((2 * rows, span), F32)
    for cut in range(SEND_CUTS):
        lead = jnp.where(slot == place - cut * capacity, gate, 0.0).astype(BF16)
        large[cut].wait()
        total += nn(lead, grad[:, cut * span : (cut + 1) * span])
    own_out[...] = total[:rows].astype(BF16)
    other_out[...] = total[rows:].astype(BF16)


def hidden_kernel(inputs, w_gate, w_up, u_out, v_out, h_out, gate_buf, up_buf, sems):
    width = inputs.shape[1]
    step = width // W_CHUNKS
    copies = []
    for k in range(W_CHUNKS):
        part = pl.ds(k * step, step)
        for n, (src, dst) in enumerate(((w_gate, gate_buf), (w_up, up_buf))):
            copy = pltpu.make_async_copy(src.at[part], dst.at[part], sems.at[n, k])
            copy.start()
            copies.append(copy)
    a = jnp.zeros(u_out.shape, F32)
    b = jnp.zeros(u_out.shape, F32)
    for k in range(W_CHUNKS):
        left = inputs[:, k * step : (k + 1) * step]
        copies[2 * k].wait()
        a += nn(left, gate_buf[k * step : (k + 1) * step, :])
        copies[2 * k + 1].wait()
        b += nn(left, up_buf[k * step : (k + 1) * step, :])
    s = jax.nn.sigmoid(a)
    u = a * s
    u_out[...] = u
    v_out[...] = b * s * (1.0 + a * (1.0 - s))
    h_out[...] = u * b


def project_kernel(group, capacity, n_dp, *refs):
    received = refs[:group]
    w_down, u_in, v_in, h_in, inputs = refs[group : group + 5]
    sends = refs[group + 5 : -4]
    da_out, db_out, gate_out, rows_buf = refs[-4:]
    rows, hidden = u_in.shape
    width = w_down.shape[1]
    span = width // SEND_CUTS
    me = lax.axis_index("expert")
    packed = SEND_CUTS * capacity
    every = jnp.concatenate([ref[...] for ref in received], axis=0)
    to = iota((rows, group * packed), 0)
    at = iota((rows, group * packed), 1)
    source = (at // packed) ^ me
    within = at % packed
    match = (to // capacity == source) & (to % capacity == within % capacity)
    projected = jnp.zeros((rows, hidden), F32)
    for cut in range(SEND_CUTS):
        select = (match & (within // capacity == cut)).astype(F32).astype(BF16)
        piece = nn(select, every).astype(BF16)
        rows_buf[:, cut * span : (cut + 1) * span] = piece
        projected += nt(piece, w_down[:, cut * span : (cut + 1) * span])
    da = (projected * v_in[...]).astype(BF16)
    db = (projected * u_in[...]).astype(BF16)
    h = h_in[...]
    da_out[...] = da
    db_out[...] = db
    gate = jnp.sum(h * projected, axis=1, keepdims=True)
    lane = iota((rows, GATE_LANES), 1)
    gate_out[...] = jnp.where(lane == me // (group // EXPERTS_W), gate, 0.0).astype(BF16)
    h = h.astype(BF16)
    if n_dp != PAIRED:
        sends[0][...] = rows_buf[...]
        sends[1][...] = h
        return
    pair = 2 * (width // n_dp)
    chip = lax.axis_index("dp") // 2
    for m, send in enumerate(sends):
        start = pl.multiple_of((chip ^ m) * pair, 128)
        send[:, 0:pair] = inputs[:, pl.ds(start, pair)]
        send[:, pair : 2 * pair] = rows_buf[:, pl.ds(start, pair)]
        for n, value in enumerate((da, db, h)):
            send[:, 2 * pair + n * hidden : 2 * pair + (n + 1) * hidden] = value


def input_kernel(group, capacity, da, db, gate, w_gate, w_up, *refs):
    outs = refs
    rows = da.shape[0]
    width = w_gate.shape[0]
    span = width // BACK_CUTS
    step = width // W_CHUNKS
    per = W_CHUNKS // BACK_CUTS
    me = lax.axis_index("expert")
    packed = BACK_CUTS * capacity
    to = iota((group * packed, rows), 0)
    at = iota((group * packed, rows), 1)
    target = (to // packed) ^ me
    within = to % packed
    match = (at // capacity == target) & (at % capacity == within % capacity)
    selects = [
        (match & (within // capacity == cut)).astype(F32).astype(BF16) for cut in range(BACK_CUTS)
    ]
    total = [jnp.zeros((group * packed, step), F32) for _ in range(per)]
    for k in range(W_CHUNKS):
        part = nt(da[...], w_gate[k * step : (k + 1) * step, :])
        part += nt(db[...], w_up[k * step : (k + 1) * step, :])
        total[k % per] += nn(selects[k // per], part.astype(BF16))
    gates = nn(selects[0], gate[...])
    for n, out in enumerate(outs):
        for q in range(per):
            out[:, q * step : (q + 1) * step] = total[q][n * packed : (n + 1) * packed].astype(BF16)
        out[:, span:] = gates[n * packed : (n + 1) * packed].astype(BF16)


def share_kernel(block, chips, *refs):
    buffers, out = refs[:chips], refs[-1]
    rows = buffers[0].shape[0]
    start = pl.multiple_of((1 - lax.axis_index("dp") % 2) * block, 128)
    for m, ref in enumerate(buffers):
        part = slice(m * rows, (m + 1) * rows)
        out[part, 0:block] = ref[:, pl.ds(start, block)]
        out[part, block : 2 * block] = ref[:, pl.ds(start + 2 * block, block)]
        out[part, 2 * block :] = ref[:, 4 * block :]


def weight_kernel(block, hidden, chips, *refs):
    buffers, shared, out = refs[:chips], refs[chips], refs[-1]
    start = pl.multiple_of((lax.axis_index("dp") % 2) * block, 128)
    lefts = [
        jnp.concatenate([ref[:, pl.ds(start + at, block)] for ref in buffers], axis=0)
        for at in (0, 2 * block)
    ]
    for n in range(3):
        at = 4 * block + n * hidden
        right = jnp.concatenate([ref[:, at : at + hidden] for ref in buffers], axis=0)
        total = tn(lefts[n // 2], right)
        left = shared[:, (n // 2) * block : (n // 2 + 1) * block]
        at -= 2 * block
        out[n] = total + tn(left, shared[:, at : at + hidden])


def combine_kernel(group, capacity, *refs):
    backs = refs[:group]
    routes, levels, slots, _, input_out, gate_out = refs[group:]
    tokens, width = input_out.shape
    span = width // BACK_CUTS
    packed = BACK_CUTS * capacity
    shards = group // EXPERTS_W
    me = lax.axis_index("expert")
    every = jnp.concatenate([ref[...] for ref in backs], axis=0)
    row = iota((group * packed, tokens), 0)
    expert = ((row // packed) ^ me) // shards
    within = row % packed
    slot = jnp.where(expert == 0, slots[0:1, :], slots[1:2, :])
    match = within % capacity == slot
    for cut in range(BACK_CUTS):
        pick = (match & (within // capacity == cut)).astype(F32).astype(BF16)
        total = tn(pick, every[:, 0:span])
        input_out[:, cut * span : (cut + 1) * span] = total.astype(BF16)
        if cut == 0:
            gates = tn(every[:, span:], pick)
    for k in range(2):
        route = routes[k : k + 1, :]
        value = jnp.where(route == 0, gates[0:1, :], jnp.where(route == 1, gates[1:2, :], 0.0))
        gate_out[k : k + 1, :] = value * (16.0 / levels[k : k + 1, :].astype(F32))


def swap(array, axis, size, mask):
    return lax.ppermute(array, axis, [(n, n ^ mask) for n in range(size)])


def plain_weights(inputs, grads, rights):
    inputs = lax.all_to_all(inputs, "dp", split_axis=1, concat_axis=0, tiled=True)
    grads = lax.all_to_all(grads, "dp", split_axis=1, concat_axis=0, tiled=True)
    rights = [lax.all_gather(right, "dp", axis=0, tiled=True) for right in rights]
    return jnp.stack([tn(inputs, rights[0]), tn(inputs, rights[1]), tn(grads, rights[2])])


def per_device(grad_out, routes, gate_levels, saved_inputs, w_gate, w_up, w_down):
    group = lax.axis_size("expert")
    n_dp = lax.axis_size("dp")
    shards = group // EXPERTS_W
    rows, width = saved_inputs.shape
    capacity = rows // group
    hidden = w_gate.shape[1]
    tokens = grad_out.shape[0]
    block = width // n_dp
    paired = n_dp == PAIRED
    routes = routes.T
    gate_levels = gate_levels.T
    shape = jax.ShapeDtypeStruct

    packed = shape((SEND_CUTS * capacity, width // SEND_CUTS), BF16)
    own, other, slots = call(
        functools.partial(pick_kernel, shards, capacity),
        (packed, packed, shape((8, tokens), jnp.int32)),
        (routes, gate_levels, grad_out),
        [HBM] * 3,
        [
            pltpu.VMEM(routes.shape, jnp.int32),
            pltpu.VMEM(routes.shape, jnp.int32),
            pltpu.VMEM(grad_out.shape, BF16),
            pltpu.SemaphoreType.DMA((2 + SEND_CUTS,)),
        ],
        vmem=60,
        name="pick",
    )
    received = [own] + [
        swap(own if mask < shards else other, "expert", group, mask) for mask in range(1, group)
    ]
    part = shape((rows, hidden), F32)
    chips = n_dp // 2 if paired else 1
    weight = shape((width, hidden), BF16)
    u, v, h, near_gate, near_up = call(
        hidden_kernel,
        (part,) * 3 + (weight,) * 2,
        (saved_inputs, w_gate, w_up),
        [VMEM, HBM, HBM],
        [pltpu.SemaphoreType.DMA((2, W_CHUNKS))],
        vmem=47,
        name="hidden",
    )
    half = shape((rows, hidden), BF16)
    late = shape((rows, 4 * block + 3 * hidden), BF16)
    outward = (late,) * chips if paired else (shape((rows, width), BF16), half)
    *sends, da, db, gate = call(
        functools.partial(project_kernel, group, capacity, n_dp),
        outward + (half, half, shape((rows, GATE_LANES), BF16)),
        (*received, w_down, u, v, h, saved_inputs),
        [VMEM] * (group + 5),
        [pltpu.VMEM((rows, width), BF16)],
        name="project",
    )
    back = shape((BACK_CUTS * capacity, width // BACK_CUTS + GATE_LANES), BF16)
    returns = call(
        functools.partial(input_kernel, group, capacity),
        (back,) * group,
        (da, db, gate, near_gate, near_up),
        [VMEM] * 5,
        name="input",
    )
    backs = [returns[0]] + [swap(returns[n], "expert", group, n) for n in range(1, group)]
    if paired:
        buffers = [sends[0]] + [swap(sends[m], "dp", n_dp, 2 * m) for m in range(1, chips)]
        sharing = call(
            functools.partial(share_kernel, block, chips),
            shape((chips * rows, 2 * block + 3 * hidden), BF16),
            (*buffers, *backs[1:]),
            [VMEM] * chips + [HBM] * (group - 1),
            name="share",
        )
        shared = swap(sharing, "dp", n_dp, 1)
        weight_grad = call(
            functools.partial(weight_kernel, block, hidden, chips),
            shape((3, block, hidden), F32),
            (*buffers, shared),
            [VMEM] * (chips + 1),
            name="weight",
        )
    else:
        sharing = returns[group - 1]
        weight_grad = plain_weights(saved_inputs, sends[0], (da, db, sends[1]))
    input_grad, gate_grad = call(
        functools.partial(combine_kernel, group, capacity),
        (shape((tokens, width), BF16), shape((2, tokens), F32)),
        (*backs, routes, gate_levels, slots, sharing),
        [VMEM] * (group + 3) + [HBM],
        name="combine",
    )
    return input_grad, gate_grad.T, weight_grad.transpose(1, 0, 2)


def solution(mesh):
    in_specs = (
        P(("dp", "expert"), None),
        P(("dp", "expert"), None),
        P(("dp", "expert"), None),
        P(("dp", "expert"), None),
        P(None, "expert"),
        P(None, "expert"),
        P("expert", None),
    )
    out_specs = (P(("dp", "expert"), None), P(("dp", "expert"), None), P("dp", None, "expert"))
    return jax.shard_map(
        per_device, mesh=mesh, in_specs=in_specs, out_specs=out_specs, check_vma=False
    )
```

time: 60.8 us -> 39.2 us (0.64)
  waiting for transfers between devices: 23 us -> 8.75 us
  local copies, waits for them, and re-layouts: 7.53 us -> 0.98 us
  starting transfers between devices: 15.9 us -> 14.7 us
    ppermute x13 -> x10, waiting for transfers between devices: 23 us -> 8.75 us  [swap(): return lax.ppermute(array, axis, [(n, n ^ mask) for n in range(size)])]
    unnamed x24 -> x12, local copies, waits for them, and re-layouts: 7.53 us -> 0.98 us
    ppermute x13 -> x10, starting transfers between devices: 15.9 us -> 14.7 us  [swap(): return lax.ppermute(array, axis, [(n, n ^ mask) for n in range(size)])]
    pallas_call x6 -> x7, Pallas kernels: 13.4 us -> 13.8 us  [call(): pl.pallas_call(kernel, out_shape=outs, in_specs=specs, out_specs=jax.tree...]
  transfers between devices with their start and end apart: 13 -> 10, of which waited for: 5 -> 6; matrix products, arithmetic and copies ran while one was open for 0% -> 0% of each run, Pallas kernels for 13% -> 20%
where the time goes in v2:
time: 39.2 us; the launch traced here: 39 us
  starting transfers between devices  14.7 us (38%)
  Pallas kernels  13.8 us (35%)
  waiting for transfers between devices  8.75 us (22%)
  local copies, waits for them, and re-layouts  0.98 us (2%)
  between operations  0.73 us (2%)
    ppermute x10, starting transfers between devices, swap(): return lax.ppermute(array, axis, [(n, n ^ mask) for n in range(size)])  14.7 us
    pallas_call x7, Pallas kernels, call(): pl.pallas_call(kernel, out_shape=outs, in_specs=specs, out_specs=jax.tree...  13.8 us
    ppermute x10, waiting for transfers between devices, swap(): return lax.ppermute(array, axis, [(n, n ^ mask) for n in range(size)])  8.75 us
    unnamed x12, local copies, waits for them, and re-layouts  0.98 us
  transfers between devices with their start and end apart: 10, of which 6 were waited for; matrix products, arithmetic and copies ran while one was open for 0% of the time, Pallas kernels for 20%

profile of v2, /device:TPU:0, one launch (start us, length us, event | category | flops | bytes accessed | tf_op | source)
XLA Modules:
  0.0 39.0 jit_solution(9150166892675073908)
XLA Ops:
  0.6 2.5 %pick.1 = (bf16[48,768]{1,0:T(8,128)(2,1)}, bf16[48,768]{1,0:T(8,128)(2,1)}, s32[8,256]{1,0:T(8,128)}) custom-call(s32[2,256]{1,0:T(2,128)} %bitcast.4, s32[2,256]{1,0:T(2,128)} %bitcast.6, bf16[256,3072]{1,0:T(8,128)(2,1)} %grad_hbm.1), custom_call_target="tpu_custom_call" | custom-call | tf_op jit(solution)/shard_map/pick/pallas_call | solution.py:39
  3.1 3.1 %collective-permute-start = (bf16[48,768]{1,0:T(8,128)(2,1)}, bf16[48,768]{1,0:T(8,128)(2,1)S(1)}, u32[]{:S(2)}, u32[]{:S(2)}) collective-permute-start(bf16[48,768]{1,0:T(8,128)(2,1)} %get-tuple-element.24.refs_0_), channel_id=1, source_target_pairs={{0,1},{1,0},{2,3},{3,2},{4,5},{5,4},{6,7},{7,6},{8,9},{9,8},{10,11... | collective-permute-start | bytes 221192 | tf_op jit(solution)/shard_map/ppermute | solution.py:255
  6.2 0.0 copy-start
  6.2 2.5 %collective-permute-start.2 = (bf16[48,768]{1,0:T(8,128)(2,1)}, bf16[48,768]{1,0:T(8,128)(2,1)S(1)}, u32[]{:S(2)}, u32[]{:S(2)}) collective-permute-start(bf16[48,768]{1,0:T(8,128)(2,1)} %get-tuple-element.25), channel_id=1, source_target_pairs={{0,3},{1,2},{2,1},{3,0},{4,7},{5,6},{6,5},{7,4},{8,11},{9,10},{10,... | collective-permute-start | bytes 221192 | tf_op jit(solution)/shard_map/ppermute | solution.py:255
  8.7 0.1 collective-permute-start.1
  8.8 0.0 copy-start.1
  8.8 1.0 %copy-done.1 = bf16[48,3072]{1,0:T(8,128)(2,1)S(1)} copy-done((bf16[48,3072]{1,0:T(8,128)(2,1)S(1)}, bf16[48,3072]{1,0:T(8,128)(2,1)}, u32[]{:S(2)}) %copy-start.1) | copy-done | bytes 294936
  9.7 0.0 copy-start.2
  9.8 3.2 %hidden.1 = (f32[48,512]{1,0:T(8,128)S(1)}, f32[48,512]{1,0:T(8,128)S(1)}, f32[48,512]{1,0:T(8,128)S(1)}, bf16[3072,512]{1,0:T(8,128)(2,1)S(1)}, bf16[3072,512]{1,0:T(8,128)(2,1)S(1)}) custom-call(bf16[48,3072]{1,0:T(8,128)(2,1)S(1)} %copy-done.1, bf16[3072,512]{1,0:T(8,128)(2,1)} %w_gate.1, bf16[3072,512]{1,0:T(8,128)(2,1)} %w_up.1), custom_call_target="tpu_custom_call" | custom-call | tf_op jit(solution)/shard_map/hidden/pallas_call | solution.py:39
  12.9 0.0 collective-permute-done.refs_1_
  12.9 0.7 %collective-permute-done.2.refs_3_ = bf16[48,768]{1,0:T(8,128)(2,1)S(1)} collective-permute-done((bf16[48,768]{1,0:T(8,128)(2,1)}, bf16[48,768]{1,0:T(8,128)(2,1)S(1)}, u32[]{:S(2)}, u32[]{:S(2)}) %collective-permute-start.2) | collective-permute-done | bytes 73760 | tf_op jit(solution)/shard_map/ppermute | solution.py:255
  13.6 2.3 %collective-permute-done.1.refs_2_ = bf16[48,768]{1,0:T(8,128)(2,1)S(1)} collective-permute-done((bf16[48,768]{1,0:T(8,128)(2,1)}, bf16[48,768]{1,0:T(8,128)(2,1)S(1)}, u32[]{:S(2)}, u32[]{:S(2)}) %collective-permute-start.1) | collective-permute-done | bytes 73760 | tf_op jit(solution)/shard_map/ppermute | solution.py:255
  15.9 0.0 copy-done
  15.9 0.0 copy-done.2
  15.9 1.4 %project.1 = (bf16[48,3072]{1,0:T(8,128)(2,1)S(1)}, bf16[48,3072]{1,0:T(8,128)(2,1)S(1)}, bf16[48,3072]{1,0:T(8,128)(2,1)S(1)}, bf16[48,3072]{1,0:T(8,128)(2,1)S...) custom-call(bf16[48,768]{1,0:T(8,128)(2,1)S(1)} %copy-done.2, ...), custom_call_target="tpu_custom_call" | custom-call | tf_op jit(solution)/shard_map/project/pallas_call | solution.py:39
  17.4 1.5 %collective-permute-start.6 = (bf16[48,3072]{1,0:T(8,128)(2,1)S(1)}, bf16[48,3072]{1,0:T(8,128)(2,1)S(1)}, u32[]{:S(2)}, u32[]{:S(2)}) collective-permute-start(bf16[48,3072]{1,0:T(8,128)(2,1)S(1)} %get-tuple-element.40), channel_id=1, source_target_pairs={{0,8},{4,12},{8,0},{12,4},{16,24},{20,28},{24,16},{28,20},{1,9},{5... | collective-permute-start | bytes 884744 | tf_op jit(solution)/shard_map/ppermute | solution.py:255
  18.9 1.5 %collective-permute-start.7 = (bf16[48,3072]{1,0:T(8,128)(2,1)S(1)}, bf16[48,3072]{1,0:T(8,128)(2,1)S(1)}, u32[]{:S(2)}, u32[]{:S(2)}) collective-permute-start(bf16[48,3072]{1,0:T(8,128)(2,1)S(1)} %get-tuple-element.41), channel_id=1, source_target_pairs={{0,16},{4,20},{8,24},{12,28},{16,0},{20,4},{24,8},{28,12},{1,17},{... | collective-permute-start | bytes 884744 | tf_op jit(solution)/shard_map/ppermute | solution.py:255
  20.4 0.5 %collective-permute-start.8 = (bf16[48,3072]{1,0:T(8,128)(2,1)S(1)}, bf16[48,3072]{1,0:T(8,128)(2,1)S(1)}, u32[]{:S(2)}, u32[]{:S(2)}) collective-permute-start(bf16[48,3072]{1,0:T(8,128)(2,1)S(1)} %get-tuple-element.42), channel_id=1, source_target_pairs={{0,24},{4,28},{8,16},{12,20},{16,8},{20,12},{24,0},{28,4},{1,25},{... | collective-permute-start | bytes 884744 | tf_op jit(solution)/shard_map/ppermute | solution.py:255
  20.9 0.0 copy-start.3
  20.9 0.0 copy-start.4
  20.9 0.0 copy-start.5
  20.9 2.6 %input.1 = (bf16[24,1664]{1,0:T(8,128)(2,1)S(1)}, bf16[24,1664]{1,0:T(8,128)(2,1)S(1)}, bf16[24,1664]{1,0:T(8,128)(2,1)S(1)}, bf16[24,1664]{1,0:T(8,128)(2,1)S(1)}) custom-call(bf16[48,512]{1,0:T(8,128)(2,1)S(1)} %get-tuple-element.29.da, bf16[48,512]{1,0:T(8,128)(2,1)S(1)} %get-tuple-element.30.db, bf16[48,128]{1,0:T(8,128)(2,1)S(1)} %get-tuple-element.31.gate, ...), custom_call_target="tpu_custom_call" | custom-call | tf_op jit(solution)/shard_map/input/pallas_call | solution.py:39
  23.5 0.1 collective-permute-start.3
  23.6 3.0 %collective-permute-start.4 = (bf16[24,1664]{1,0:T(8,128)(2,1)S(1)}, bf16[24,1664]{1,0:T(8,128)(2,1)S(1)}, u32[]{:S(2)}, u32[]{:S(2)}) collective-permute-start(bf16[24,1664]{1,0:T(8,128)(2,1)S(1)} %get-tuple-element.36), channel_id=1, source_target_pairs={{0,2},{1,3},{2,0},{3,1},{4,6},{5,7},{6,4},{7,5},{8,10},{9,11},{10,... | collective-permute-start | bytes 239624 | tf_op jit(solution)/shard_map/ppermute | solution.py:255
  26.5 1.4 %collective-permute-done.3.refs_4_.refs_1_ = bf16[24,1664]{1,0:T(8,128)(2,1)S(1)} collective-permute-done((bf16[24,1664]{1,0:T(8,128)(2,1)S(1)}, bf16[24,1664]{1,0:T(8,128)(2,1)S(1)}, u32[]{:S(2)}, u32[]{:S(2)}) %collective-permute-start.3) | collective-permute-done | bytes 79904 | tf_op jit(solution)/shard_map/ppermute | solution.py:255
  28.0 2.4 %collective-permute-start.5 = (bf16[24,1664]{1,0:T(8,128)(2,1)S(1)}, bf16[24,1664]{1,0:T(8,128)(2,1)S(1)}, u32[]{:S(2)}, u32[]{:S(2)}) collective-permute-start(bf16[24,1664]{1,0:T(8,128)(2,1)S(1)} %get-tuple-element.37), channel_id=1, source_target_pairs={{0,3},{1,2},{2,1},{3,0},{4,7},{5,6},{6,5},{7,4},{8,11},{9,10},{10,... | collective-permute-start | bytes 239624 | tf_op jit(solution)/shard_map/ppermute | solution.py:255
  30.4 1.2 %collective-permute-done.4.refs_5_.refs_2_ = bf16[24,1664]{1,0:T(8,128)(2,1)S(1)} collective-permute-done((bf16[24,1664]{1,0:T(8,128)(2,1)S(1)}, bf16[24,1664]{1,0:T(8,128)(2,1)S(1)}, u32[]{:S(2)}, u32[]{:S(2)}) %collective-permute-start.4) | collective-permute-done | bytes 79904 | tf_op jit(solution)/shard_map/ppermute | solution.py:255
  31.7 2.5 %collective-permute-done.5.refs_6_.refs_3_ = bf16[24,1664]{1,0:T(8,128)(2,1)S(1)} collective-permute-done((bf16[24,1664]{1,0:T(8,128)(2,1)S(1)}, bf16[24,1664]{1,0:T(8,128)(2,1)S(1)}, u32[]{:S(2)}, u32[]{:S(2)}) %collective-permute-start.5) | collective-permute-done | bytes 79904 | tf_op jit(solution)/shard_map/ppermute | solution.py:255
  34.2 0.0 collective-permute-done.6.refs_1_
  34.2 0.0 collective-permute-done.7.refs_2_
  34.2 0.0 collective-permute-done.8.refs_3_
  34.2 0.1 share.1.refs_7_
  34.3 0.1 collective-permute-start.9
  34.4 0.0 copy-done.3
  34.4 0.0 copy-done.4
  34.4 0.0 copy-done.5
  34.4 1.9 %combine.1 = (bf16[256,3072]{1,0:T(8,128)(2,1)}, f32[2,256]{1,0:T(2,128)}) custom-call(bf16[24,1664]{1,0:T(8,128)(2,1)S(1)} %get-tuple-element.34.refs_0_, bf16[24,1664]{1,0:T(8,128)(2,1)S(1)} %collective-permute-done.3.refs_4_.refs_1_, bf16[24,1664]{1,0:T(8,128)(2,1)S(1)} %collective-permute-done.4.refs_5_.refs_2_, ...), custom_call_target="tpu_custom_call" | custom-call | tf_op jit(solution)/shard_map/combine/pallas_call | solution.py:39
  36.3 0.5 %collective-permute-done.9.refs_4_ = bf16[192,2304]{1,0:T(8,128)(2,1)S(1)} collective-permute-done((bf16[192,2304]{1,0:T(8,128)(2,1)S(1)}, bf16[192,2304]{1,0:T(8,128)(2,1)S(1)}, u32[]{:S(2)}, u32[]{:S(2)}) %collective-permute-start.9) | collective-permute-done | bytes 884768 | tf_op jit(solution)/shard_map/ppermute | solution.py:255
  36.8 2.2 %weight.1 = f32[3,384,512]{2,1,0:T(8,128)} custom-call(bf16[48,3072]{1,0:T(8,128)(2,1)S(1)} %get-tuple-element.39.refs_0_, bf16[48,3072]{1,0:T(8,128)(2,1)S(1)} %collective-permute-done.6.refs_1_, bf16[48,3072]{1,0:T(8,128)(2,1)S(1)} %collective-permute-done.7.refs_2_, bf16[48,3072]{1,0:T(8,128)(2,1)S(1)} %collective-permute-done.8.refs_3_, ...), custom_call_target="tpu_custom_call" | custom-call | tf_op jit(solution)/shard_map/weight/pallas_call | solution.py:39
Async XLA Ops:
  3.1 9.8 %collective-permute-start = (bf16[48,768]{1,0:T(8,128)(2,1)}, bf16[48,768]{1,0:T(8,128)(2,1)S(1)}, u32[]{:S(2)}, u32[]{:S(2)}) collective-permute-start(bf16[48,768]{1,0:T(8,128)(2,1)} %get-tuple-element.24.refs_0_), channel_id=1, source_target_pairs={{0,1},{1,0},{2,3},{3,2},{4,5},{5,4},{6,7},{7,6},{8,9},{9,8},{10,11... | collective-permute-start | bytes 221192 | tf_op jit(solution)/shard_map/ppermute | solution.py:255
  6.2 9.8 %copy-start = (bf16[512,3072]{1,0:T(8,128)(2,1)S(1)}, bf16[512,3072]{1,0:T(8,128)(2,1)}, u32[]{:S(2)}) copy-start(bf16[512,3072]{1,0:T(8,128)(2,1)} %refs_4_.1) | copy-start | bytes 9437188
  6.2 7.4 %collective-permute-start.2 = (bf16[48,768]{1,0:T(8,128)(2,1)}, bf16[48,768]{1,0:T(8,128)(2,1)S(1)}, u32[]{:S(2)}, u32[]{:S(2)}) collective-permute-start(bf16[48,768]{1,0:T(8,128)(2,1)} %get-tuple-element.25), channel_id=1, source_target_pairs={{0,3},{1,2},{2,1},{3,0},{4,7},{5,6},{6,5},{7,4},{8,11},{9,10},{10,... | collective-permute-start | bytes 221192 | tf_op jit(solution)/shard_map/ppermute | solution.py:255
  8.7 7.3 %collective-permute-start.1 = (bf16[48,768]{1,0:T(8,128)(2,1)}, bf16[48,768]{1,0:T(8,128)(2,1)S(1)}, u32[]{:S(2)}, u32[]{:S(2)}) collective-permute-start(bf16[48,768]{1,0:T(8,128)(2,1)} %get-tuple-element.25), channel_id=1, source_target_pairs={{0,2},{1,3},{2,0},{3,1},{4,6},{5,7},{6,4},{7,5},{8,10},{9,11},{10,... | collective-permute-start | bytes 221192 | tf_op jit(solution)/shard_map/ppermute | solution.py:255
  8.8 1.0 %copy-start.1 = (bf16[48,3072]{1,0:T(8,128)(2,1)S(1)}, bf16[48,3072]{1,0:T(8,128)(2,1)}, u32[]{:S(2)}) copy-start(bf16[48,3072]{1,0:T(8,128)(2,1)} %refs_8_.1) | copy-start | bytes 884740
  9.7 6.2 %copy-start.2 = (bf16[48,768]{1,0:T(8,128)(2,1)S(1)}, bf16[48,768]{1,0:T(8,128)(2,1)}, u32[]{:S(2)}) copy-start(bf16[48,768]{1,0:T(8,128)(2,1)} %get-tuple-element.24.refs_0_) | copy-start | bytes 221188
  17.4 16.8 %collective-permute-start.6 = (bf16[48,3072]{1,0:T(8,128)(2,1)S(1)}, bf16[48,3072]{1,0:T(8,128)(2,1)S(1)}, u32[]{:S(2)}, u32[]{:S(2)}) collective-permute-start(bf16[48,3072]{1,0:T(8,128)(2,1)S(1)} %get-tuple-element.40), channel_id=1, source_target_pairs={{0,8},{4,12},{8,0},{12,4},{16,24},{20,28},{24,16},{28,20},{1,9},{5... | collective-permute-start | bytes 884744 | tf_op jit(solution)/shard_map/ppermute | solution.py:255
  18.9 15.3 %collective-permute-start.7 = (bf16[48,3072]{1,0:T(8,128)(2,1)S(1)}, bf16[48,3072]{1,0:T(8,128)(2,1)S(1)}, u32[]{:S(2)}, u32[]{:S(2)}) collective-permute-start(bf16[48,3072]{1,0:T(8,128)(2,1)S(1)} %get-tuple-element.41), channel_id=1, source_target_pairs={{0,16},{4,20},{8,24},{12,28},{16,0},{20,4},{24,8},{28,12},{1,17},{... | collective-permute-start | bytes 884744 | tf_op jit(solution)/shard_map/ppermute | solution.py:255
  20.4 13.8 %collective-permute-start.8 = (bf16[48,3072]{1,0:T(8,128)(2,1)S(1)}, bf16[48,3072]{1,0:T(8,128)(2,1)S(1)}, u32[]{:S(2)}, u32[]{:S(2)}) collective-permute-start(bf16[48,3072]{1,0:T(8,128)(2,1)S(1)} %get-tuple-element.42), channel_id=1, source_target_pairs={{0,24},{4,28},{8,16},{12,20},{16,8},{20,12},{24,0},{28,4},{1,25},{... | collective-permute-start | bytes 884744 | tf_op jit(solution)/shard_map/ppermute | solution.py:255
  20.9 13.5 %copy-start.3 = (s32[8,256]{1,0:T(8,128)S(1)}, s32[8,256]{1,0:T(8,128)}, u32[]{:S(2)}) copy-start(s32[8,256]{1,0:T(8,128)} %get-tuple-element.38.refs_6_) | copy-start | bytes 24580
  20.9 13.5 %copy-start.4 = (s32[256,2]{0,1:T(2,128)S(1)}, s32[256,2]{0,1:T(2,128)}, u32[]{:S(2)}) copy-start(s32[256,2]{0,1:T(2,128)} %param.8) | copy-start | bytes 6148
  20.9 13.5 %copy-start.5 = (s32[256,2]{0,1:T(2,128)S(1)}, s32[256,2]{0,1:T(2,128)}, u32[]{:S(2)}) copy-start(s32[256,2]{0,1:T(2,128)} %param.9) | copy-start | bytes 6148
  23.5 4.5 %collective-permute-start.3 = (bf16[24,1664]{1,0:T(8,128)(2,1)S(1)}, bf16[24,1664]{1,0:T(8,128)(2,1)S(1)}, u32[]{:S(2)}, u32[]{:S(2)}) collective-permute-start(bf16[24,1664]{1,0:T(8,128)(2,1)S(1)} %get-tuple-element.35), channel_id=1, source_target_pairs={{0,1},{1,0},{2,3},{3,2},{4,5},{5,4},{6,7},{7,6},{8,9},{9,8},{10,11... | collective-permute-start | bytes 239624 | tf_op jit(solution)/shard_map/ppermute | solution.py:255
  23.6 8.1 %collective-permute-start.4 = (bf16[24,1664]{1,0:T(8,128)(2,1)S(1)}, bf16[24,1664]{1,0:T(8,128)(2,1)S(1)}, u32[]{:S(2)}, u32[]{:S(2)}) collective-permute-start(bf16[24,1664]{1,0:T(8,128)(2,1)S(1)} %get-tuple-element.36), channel_id=1, source_target_pairs={{0,2},{1,3},{2,0},{3,1},{4,6},{5,7},{6,4},{7,5},{8,10},{9,11},{10,... | collective-permute-start | bytes 239624 | tf_op jit(solution)/shard_map/ppermute | solution.py:255
  28.0 6.2 %collective-permute-start.5 = (bf16[24,1664]{1,0:T(8,128)(2,1)S(1)}, bf16[24,1664]{1,0:T(8,128)(2,1)S(1)}, u32[]{:S(2)}, u32[]{:S(2)}) collective-permute-start(bf16[24,1664]{1,0:T(8,128)(2,1)S(1)} %get-tuple-element.37), channel_id=1, source_target_pairs={{0,3},{1,2},{2,1},{3,0},{4,7},{5,6},{6,5},{7,4},{8,11},{9,10},{10,... | collective-permute-start | bytes 239624 | tf_op jit(solution)/shard_map/ppermute | solution.py:255
  34.3 2.5 %collective-permute-start.9 = (bf16[192,2304]{1,0:T(8,128)(2,1)S(1)}, bf16[192,2304]{1,0:T(8,128)(2,1)S(1)}, u32[]{:S(2)}, u32[]{:S(2)}) collective-permute-start(bf16[192,2304]{1,0:T(8,128)(2,1)S(1)} %share.1.refs_7_), channel_id=1, source_target_pairs={{0,4},{4,0},{8,12},{12,8},{16,20},{20,16},{24,28},{28,24},{1,5},{5... | collective-permute-start | bytes 2654216 | tf_op jit(solution)/shard_map/ppermute | solution.py:255

commit v3 on v2

--- a/solution.py
+++ b/solution.py
@@ -12,11 +12,14 @@
 BACK_CUTS = 2
 GATE_LANES = 128
 W_CHUNKS = 4
+EARLY = (1, 2, 3)
+DISPATCH_ORDER = (0, 3, 2, 1)
 PAIRED = 8
 F32 = jnp.float32
 BF16 = jnp.bfloat16
 VMEM = pl.BlockSpec(memory_space=pltpu.VMEM)
 HBM = pl.BlockSpec(memory_space=pltpu.HBM)
+UNUSED = pl.BlockSpec(memory_space=pl.ANY)
 
 
 def nn(left, right):
@@ -35,17 +38,36 @@
     return lax.broadcasted_iota(jnp.int32, shape, dim)
 
 
-def call(kernel, outs, args, specs, scratch=(), vmem=24, name=None):
+def call(kernel, outs, args, specs, scratch=(), near=True, out_specs=None, name=None):
+    args = [
+        pltpu.with_memory_space_constraint(arg, pltpu.HBM) if spec is HBM else arg
+        for arg, spec in zip(args, specs)
+    ]
+    if near:
+        outs = jax.tree.map(lambda out: pltpu.VMEM(out.shape, out.dtype), outs)
     return pl.pallas_call(
         kernel,
         out_shape=outs,
         in_specs=specs,
-        out_specs=jax.tree.map(lambda _: VMEM, outs),
+        out_specs=out_specs or jax.tree.map(lambda _: VMEM, outs),
         scratch_shapes=scratch,
-        compiler_params=pltpu.CompilerParams(vmem_limit_bytes=vmem * 1024 * 1024),
+        compiler_params=pltpu.CompilerParams(vmem_limit_bytes=24 * 1024 * 1024),
         cost_estimate=pl.CostEstimate(flops=0, bytes_accessed=0, transcendentals=0),
         name=name,
     )(*args)
+
+
+def order(count):
+    return DISPATCH_ORDER if count == 4 else range(count)
+
+
+def arrange(arrays):
+    return [arrays[mask] for mask in order(len(arrays))]
+
+
+def restore(refs):
+    places = list(order(len(refs)))
+    return [refs[places.index(mask)] for mask in range(len(refs))]
 
 
 def pick_kernel(
@@ -99,7 +121,11 @@
     other_out[...] = total[rows:].astype(BF16)
 
 
-def hidden_kernel(inputs, w_gate, w_up, u_out, v_out, h_out, gate_buf, up_buf, sems):
+def hidden_kernel(
+    inputs_hbm, w_gate, w_up, u_out, v_out, h_out, inputs, gate_buf, up_buf, sems
+):
+    first = pltpu.make_async_copy(inputs_hbm, inputs, sems.at[2, 0])
+    first.start()
     width = inputs.shape[1]
     step = width // W_CHUNKS
     copies = []
@@ -109,6 +135,7 @@
             copy = pltpu.make_async_copy(src.at[part], dst.at[part], sems.at[n, k])
             copy.start()
             copies.append(copy)
+    first.wait()
     a = jnp.zeros(u_out.shape, F32)
     b = jnp.zeros(u_out.shape, F32)
     for k in range(W_CHUNKS):
@@ -125,7 +152,7 @@
 
 
 def project_kernel(group, capacity, n_dp, *refs):
-    received = refs[:group]
+    received = restore(refs[:group])
     w_down, u_in, v_in, h_in, inputs = refs[group : group + 5]
     sends = refs[group + 5 : -4]
     da_out, db_out, gate_out, rows_buf = refs[-4:]
@@ -170,7 +197,7 @@
 
 
 def input_kernel(group, capacity, da, db, gate, w_gate, w_up, *refs):
-    outs = refs
+    outs = refs[-group:]
     rows = da.shape[0]
     width = w_gate.shape[0]
     span = width // BACK_CUTS
@@ -210,7 +237,7 @@
 
 
 def weight_kernel(block, hidden, chips, *refs):
-    buffers, shared, out = refs[:chips], refs[chips], refs[-1]
+    buffers, out = refs[:chips], refs[-1]
     start = pl.multiple_of((lax.axis_index("dp") % 2) * block, 128)
     lefts = [
         jnp.concatenate([ref[:, pl.ds(start + at, block)] for ref in buffers], axis=0)
@@ -219,16 +246,25 @@
     for n in range(3):
         at = 4 * block + n * hidden
         right = jnp.concatenate([ref[:, at : at + hidden] for ref in buffers], axis=0)
-        total = tn(lefts[n // 2], right)
+        out[n] = tn(lefts[n // 2], right)
+
+
+def finish_kernel(block, hidden, partial, shared, out_hbm, buf, sems):
+    copies = []
+    for n in range(3):
         left = shared[:, (n // 2) * block : (n // 2 + 1) * block]
-        at -= 2 * block
-        out[n] = total + tn(left, shared[:, at : at + hidden])
+        at = 2 * block + n * hidden
+        buf[n] = partial[n] + tn(left, shared[:, at : at + hidden])
+        copies.append(pltpu.make_async_copy(buf.at[n], out_hbm.at[n], sems.at[n]))
+        copies[-1].start()
+    for copy in copies:
+        copy.wait()
 
 
 def combine_kernel(group, capacity, *refs):
     backs = refs[:group]
-    routes, levels, slots, _, input_out, gate_out = refs[group:]
-    tokens, width = input_out.shape
+    routes, levels, slots, _, input_hbm, gate_out, input_buf, sems = refs[group:]
+    tokens, width = input_buf.shape
     span = width // BACK_CUTS
     packed = BACK_CUTS * capacity
     shards = group // EXPERTS_W
@@ -239,20 +275,35 @@
     within = row % packed
     slot = jnp.where(expert == 0, slots[0:1, :], slots[1:2, :])
     match = within % capacity == slot
+    copies = []
     for cut in range(BACK_CUTS):
         pick = (match & (within // capacity == cut)).astype(F32).astype(BF16)
-        total = tn(pick, every[:, 0:span])
-        input_out[:, cut * span : (cut + 1) * span] = total.astype(BF16)
+        half = span // 2
+        for at in (0, half):
+            part = pl.ds(cut * span + at, half)
+            input_buf[:, part] = tn(pick, every[:, at : at + half]).astype(BF16)
+            copies.append(
+                pltpu.make_async_copy(
+                    input_buf.at[:, part], input_hbm.at[:, part], sems.at[len(copies)]
+                )
+            )
+            copies[-1].start()
         if cut == 0:
             gates = tn(every[:, span:], pick)
     for k in range(2):
         route = routes[k : k + 1, :]
         value = jnp.where(route == 0, gates[0:1, :], jnp.where(route == 1, gates[1:2, :], 0.0))
         gate_out[k : k + 1, :] = value * (16.0 / levels[k : k + 1, :].astype(F32))
+    for copy in copies:
+        copy.wait()
 
 
 def swap(array, axis, size, mask):
     return lax.ppermute(array, axis, [(n, n ^ mask) for n in range(size)])
+
+
+def far_first(group):
+    return [*range(group // 2, group), *range(1, group // 2)]
 
 
 def plain_weights(inputs, grads, rights):
@@ -288,31 +339,29 @@
             pltpu.VMEM(grad_out.shape, BF16),
             pltpu.SemaphoreType.DMA((2 + SEND_CUTS,)),
         ],
-        vmem=60,
         name="pick",
     )
-    received = [own] + [
-        swap(own if mask < shards else other, "expert", group, mask) for mask in range(1, group)
-    ]
+    received = [own] + [None] * (group - 1)
+    for mask in far_first(group):
+        received[mask] = swap(own if mask < shards else other, "expert", group, mask)
     part = shape((rows, hidden), F32)
-    chips = n_dp // 2 if paired else 1
     weight = shape((width, hidden), BF16)
-    u, v, h, near_gate, near_up = call(
+    u, v, h, near_inputs, near_gate, near_up = call(
         hidden_kernel,
-        (part,) * 3 + (weight,) * 2,
+        (part,) * 3 + (shape((rows, width), BF16),) + (weight,) * 2,
         (saved_inputs, w_gate, w_up),
-        [VMEM, HBM, HBM],
-        [pltpu.SemaphoreType.DMA((2, W_CHUNKS))],
-        vmem=47,
+        [HBM] * 3,
+        [pltpu.SemaphoreType.DMA((3, W_CHUNKS))],
         name="hidden",
     )
     half = shape((rows, hidden), BF16)
+    chips = n_dp // 2 if paired else 0
     late = shape((rows, 4 * block + 3 * hidden), BF16)
     outward = (late,) * chips if paired else (shape((rows, width), BF16), half)
     *sends, da, db, gate = call(
         functools.partial(project_kernel, group, capacity, n_dp),
         outward + (half, half, shape((rows, GATE_LANES), BF16)),
-        (*received, w_down, u, v, h, saved_inputs),
+        (*arrange(received), w_down, u, v, h, near_inputs),
         [VMEM] * (group + 5),
         [pltpu.VMEM((rows, width), BF16)],
         name="project",
@@ -325,32 +374,48 @@
         [VMEM] * 5,
         name="input",
     )
-    backs = [returns[0]] + [swap(returns[n], "expert", group, n) for n in range(1, group)]
+    backs = [returns[0]] + [None] * (group - 1)
+    for mask in far_first(group):
+        backs[mask] = swap(returns[mask], "expert", group, mask)
     if paired:
         buffers = [sends[0]] + [swap(sends[m], "dp", n_dp, 2 * m) for m in range(1, chips)]
         sharing = call(
             functools.partial(share_kernel, block, chips),
             shape((chips * rows, 2 * block + 3 * hidden), BF16),
-            (*buffers, *backs[1:]),
-            [VMEM] * chips + [HBM] * (group - 1),
+            (*buffers, *[backs[mask] for mask in EARLY]),
+            [VMEM] * chips + [UNUSED] * len(EARLY),
             name="share",
         )
         shared = swap(sharing, "dp", n_dp, 1)
-        weight_grad = call(
+        block_shape = shape((3, block, hidden), F32)
+        partial = call(
             functools.partial(weight_kernel, block, hidden, chips),
-            shape((3, block, hidden), F32),
-            (*buffers, shared),
-            [VMEM] * (chips + 1),
+            block_shape,
+            buffers,
+            [VMEM] * chips,
             name="weight",
         )
+        weight_grad = call(
+            functools.partial(finish_kernel, block, hidden),
+            block_shape,
+            (partial, shared),
+            [VMEM] * 2,
+            [pltpu.VMEM(block_shape.shape, F32), pltpu.SemaphoreType.DMA((3,))],
+            near=False,
+            out_specs=HBM,
+            name="finish",
+        )
     else:
-        sharing = returns[group - 1]
+        sharing = returns[0]
         weight_grad = plain_weights(saved_inputs, sends[0], (da, db, sends[1]))
     input_grad, gate_grad = call(
         functools.partial(combine_kernel, group, capacity),
         (shape((tokens, width), BF16), shape((2, tokens), F32)),
         (*backs, routes, gate_levels, slots, sharing),
-        [VMEM] * (group + 3) + [HBM],
+        [VMEM] * (group + 3) + [UNUSED],
+        [pltpu.VMEM((tokens, width), BF16), pltpu.SemaphoreType.DMA((2 * BACK_CUTS,))],
+        near=False,
+        out_specs=(HBM, VMEM),
         name="combine",
     )
     return input_grad, gate_grad.T, weight_grad.transpose(1, 0, 2)

time: 39.2 us -> 37.5 us (0.957)
  local copies, waits for them, and re-layouts: 0.98 us -> 0.02 us
  waiting for transfers between devices: 8.75 us -> 8.32 us
    unnamed x12 -> x6, local copies, waits for them, and re-layouts: 0.98 us -> 0.02 us
    ppermute x10, waiting for transfers between devices: 8.75 us -> 8.32 us  [swap(): return lax.ppermute(array, axis, [(n, n ^ mask) for n in range(size)])]
    pallas_call x7 -> x8, Pallas kernels: 13.8 us -> 13.5 us  [call(): pl.pallas_call(kernel, out_shape=outs, in_specs=specs, out_specs=out_spec...]
  transfers between devices with their start and end apart: 10 -> 10, of which waited for: 6 -> 5; matrix products, arithmetic and copies ran while one was open for 0% -> 0% of each run, Pallas kernels for 20% -> 23%
where the time goes in v3:
time: 37.5 us; the launch traced here: 37.3 us
  starting transfers between devices  14.6 us (39%)
  Pallas kernels  13.5 us (36%)
  waiting for transfers between devices  8.32 us (22%)
  between operations  0.74 us (2%)
    ppermute x10, starting transfers between devices, swap(): return lax.ppermute(array, axis, [(n, n ^ mask) for n in range(size)])  14.6 us
    pallas_call x8, Pallas kernels, call(): pl.pallas_call(kernel, out_shape=outs, in_specs=specs, out_specs=out_spec...  13.5 us
    ppermute x10, waiting for transfers between devices, swap(): return lax.ppermute(array, axis, [(n, n ^ mask) for n in range(size)])  8.32 us
  transfers between devices with their start and end apart: 10, of which 5 were waited for; matrix products, arithmetic and copies ran while one was open for 0% of the time, Pallas kernels for 23%

profile of v3, /device:TPU:0, one launch (start us, length us, event | category | flops | bytes accessed | tf_op | source)
XLA Modules:
  0.0 37.3 jit_solution(11279527848934673639)
XLA Ops:
  0.6 1.8 %pick.1 = (bf16[48,768]{1,0:T(8,128)(2,1)S(1)}, bf16[48,768]{1,0:T(8,128)(2,1)S(1)}, s32[8,256]{1,0:T(8,128)S(1)}) custom-call(s32[2,256]{1,0:T(2,128)} %bitcast.4, s32[2,256]{1,0:T(2,128)} %bitcast.6, bf16[256,3072]{1,0:T(8,128)(2,1)} %grad_hbm.1), custom_call_target="tpu_custom_call" | custom-call | tf_op jit(solution)/shard_map/pick/pallas_call | solution.py:48
  2.4 3.1 %collective-permute-start.2 = (bf16[48,768]{1,0:T(8,128)(2,1)S(1)}, bf16[48,768]{1,0:T(8,128)(2,1)S(1)}, u32[]{:S(2)}, u32[]{:S(2)}) collective-permute-start(bf16[48,768]{1,0:T(8,128)(2,1)S(1)} %get-tuple-element.25.refs_0_), channel_id=1, source_target_pairs={{0,1},{1,0},{2,3},{3,2},{4,5},{5,4},{6,7},{7,6},{8,9},{9,8},{10,11... | collective-permute-start | bytes 221192 | tf_op jit(solution)/shard_map/ppermute | solution.py:302
  5.5 0.0 copy-start
  5.5 2.6 %collective-permute-start.1 = (bf16[48,768]{1,0:T(8,128)(2,1)S(1)}, bf16[48,768]{1,0:T(8,128)(2,1)S(1)}, u32[]{:S(2)}, u32[]{:S(2)}) collective-permute-start(bf16[48,768]{1,0:T(8,128)(2,1)S(1)} %get-tuple-element.26), channel_id=1, source_target_pairs={{0,2},{1,3},{2,0},{3,1},{4,6},{5,7},{6,4},{7,5},{8,10},{9,11},{10,... | collective-permute-start | bytes 221192 | tf_op jit(solution)/shard_map/ppermute | solution.py:302
  8.1 0.0 collective-permute-start
  8.1 3.3 %hidden.1 = (f32[48,512]{1,0:T(8,128)S(1)}, f32[48,512]{1,0:T(8,128)S(1)}, f32[48,512]{1,0:T(8,128)S(1)}, bf16[48,3072]{1,0:T(8,128)(2,1)S(1)}, bf16[3072,512]{1...) custom-call(bf16[48,3072]{1,0:T(8,128)(2,1)} %inputs_hbm.1, bf16[3072,512]{1,0:T(8,128)(2,1)} %w_gate.1, bf16[3072,512]{1,0:T(8,128)(2,1)} %w_up.1), custom_call_target="tpu_custom_call" | custom-call | tf_op jit(solution)/shard_map/hidden/pallas_call | solution.py:48
  11.4 0.0 collective-permute-done.2.refs_3_
  11.4 1.9 %collective-permute-done.1.refs_2_ = bf16[48,768]{1,0:T(8,128)(2,1)S(1)} collective-permute-done((bf16[48,768]{1,0:T(8,128)(2,1)S(1)}, bf16[48,768]{1,0:T(8,128)(2,1)S(1)}, u32[]{:S(2)}, u32[]{:S(2)}) %collective-permute-start.1) | collective-permute-done | bytes 73760 | tf_op jit(solution)/shard_map/ppermute | solution.py:302
  13.3 1.1 %collective-permute-done.refs_1_ = bf16[48,768]{1,0:T(8,128)(2,1)S(1)} collective-permute-done((bf16[48,768]{1,0:T(8,128)(2,1)S(1)}, bf16[48,768]{1,0:T(8,128)(2,1)S(1)}, u32[]{:S(2)}, u32[]{:S(2)}) %collective-permute-start) | collective-permute-done | bytes 73760 | tf_op jit(solution)/shard_map/ppermute | solution.py:302
  14.4 0.0 copy-done
  14.4 1.4 %project.1 = (bf16[48,3072]{1,0:T(8,128)(2,1)S(1)}, bf16[48,3072]{1,0:T(8,128)(2,1)S(1)}, bf16[48,3072]{1,0:T(8,128)(2,1)S(1)}, bf16[48,3072]{1,0:T(8,128)(2,1)S...) custom-call(bf16[48,768]{1,0:T(8,128)(2,1)S(1)} %get-tuple-element.25.refs_0_, ...), custom_call_target="tpu_custom_call" | custom-call | tf_op jit(solution)/shard_map/project/pallas_call | solution.py:48
  15.8 1.5 %collective-permute-start.6 = (bf16[48,3072]{1,0:T(8,128)(2,1)S(1)}, bf16[48,3072]{1,0:T(8,128)(2,1)S(1)}, u32[]{:S(2)}, u32[]{:S(2)}) collective-permute-start(bf16[48,3072]{1,0:T(8,128)(2,1)S(1)} %get-tuple-element.42), channel_id=1, source_target_pairs={{0,8},{4,12},{8,0},{12,4},{16,24},{20,28},{24,16},{28,20},{1,9},{5... | collective-permute-start | bytes 884744 | tf_op jit(solution)/shard_map/ppermute | solution.py:302
  17.3 1.5 %collective-permute-start.7 = (bf16[48,3072]{1,0:T(8,128)(2,1)S(1)}, bf16[48,3072]{1,0:T(8,128)(2,1)S(1)}, u32[]{:S(2)}, u32[]{:S(2)}) collective-permute-start(bf16[48,3072]{1,0:T(8,128)(2,1)S(1)} %get-tuple-element.43), channel_id=1, source_target_pairs={{0,16},{4,20},{8,24},{12,28},{16,0},{20,4},{24,8},{28,12},{1,17},{... | collective-permute-start | bytes 884744 | tf_op jit(solution)/shard_map/ppermute | solution.py:302
  18.8 0.5 %collective-permute-start.8 = (bf16[48,3072]{1,0:T(8,128)(2,1)S(1)}, bf16[48,3072]{1,0:T(8,128)(2,1)S(1)}, u32[]{:S(2)}, u32[]{:S(2)}) collective-permute-start(bf16[48,3072]{1,0:T(8,128)(2,1)S(1)} %get-tuple-element.44), channel_id=1, source_target_pairs={{0,24},{4,28},{8,16},{12,20},{16,8},{20,12},{24,0},{28,4},{1,25},{... | collective-permute-start | bytes 884744 | tf_op jit(solution)/shard_map/ppermute | solution.py:302
  19.3 2.6 %input.1 = (bf16[24,1664]{1,0:T(8,128)(2,1)S(1)}, bf16[24,1664]{1,0:T(8,128)(2,1)S(1)}, bf16[24,1664]{1,0:T(8,128)(2,1)S(1)}, bf16[24,1664]{1,0:T(8,128)(2,1)S(1)}) custom-call(bf16[48,512]{1,0:T(8,128)(2,1)S(1)} %get-tuple-element.31.da, bf16[48,512]{1,0:T(8,128)(2,1)S(1)} %get-tuple-element.32.db, bf16[48,128]{1,0:T(8,128)(2,1)S(1)} %get-tuple-element.33.gate, ...), custom_call_target="tpu_custom_call" | custom-call | tf_op jit(solution)/shard_map/input/pallas_call | solution.py:48
  21.9 0.0 copy-start.1
  21.9 0.0 copy-start.2
  21.9 1.2 %collective-permute-start.3 = (bf16[24,1664]{1,0:T(8,128)(2,1)S(1)}, bf16[24,1664]{1,0:T(8,128)(2,1)S(1)}, u32[]{:S(2)}, u32[]{:S(2)}) collective-permute-start(bf16[24,1664]{1,0:T(8,128)(2,1)S(1)} %get-tuple-element.37), channel_id=1, source_target_pairs={{0,1},{1,0},{2,3},{3,2},{4,5},{5,4},{6,7},{7,6},{8,9},{9,8},{10,11... | collective-permute-start | bytes 239624 | tf_op jit(solution)/shard_map/ppermute | solution.py:302
  23.1 1.7 %collective-permute-start.4 = (bf16[24,1664]{1,0:T(8,128)(2,1)S(1)}, bf16[24,1664]{1,0:T(8,128)(2,1)S(1)}, u32[]{:S(2)}, u32[]{:S(2)}) collective-permute-start(bf16[24,1664]{1,0:T(8,128)(2,1)S(1)} %get-tuple-element.38), channel_id=1, source_target_pairs={{0,2},{1,3},{2,0},{3,1},{4,6},{5,7},{6,4},{7,5},{8,10},{9,11},{10,... | collective-permute-start | bytes 239624 | tf_op jit(solution)/shard_map/ppermute | solution.py:302
  24.8 1.6 %collective-permute-done.3.refs_4_.refs_1_ = bf16[24,1664]{1,0:T(8,128)(2,1)S(1)} collective-permute-done((bf16[24,1664]{1,0:T(8,128)(2,1)S(1)}, bf16[24,1664]{1,0:T(8,128)(2,1)S(1)}, u32[]{:S(2)}, u32[]{:S(2)}) %collective-permute-start.3) | collective-permute-done | bytes 79904 | tf_op jit(solution)/shard_map/ppermute | solution.py:302
  26.4 2.5 %collective-permute-start.5 = (bf16[24,1664]{1,0:T(8,128)(2,1)S(1)}, bf16[24,1664]{1,0:T(8,128)(2,1)S(1)}, u32[]{:S(2)}, u32[]{:S(2)}) collective-permute-start(bf16[24,1664]{1,0:T(8,128)(2,1)S(1)} %get-tuple-element.39), channel_id=1, source_target_pairs={{0,3},{1,2},{2,1},{3,0},{4,7},{5,6},{6,5},{7,4},{8,11},{9,10},{10,... | collective-permute-start | bytes 239624 | tf_op jit(solution)/shard_map/ppermute | solution.py:302
  29.0 1.0 %collective-permute-done.4.refs_5_.refs_2_ = bf16[24,1664]{1,0:T(8,128)(2,1)S(1)} collective-permute-done((bf16[24,1664]{1,0:T(8,128)(2,1)S(1)}, bf16[24,1664]{1,0:T(8,128)(2,1)S(1)}, u32[]{:S(2)}, u32[]{:S(2)}) %collective-permute-start.4) | collective-permute-done | bytes 79904 | tf_op jit(solution)/shard_map/ppermute | solution.py:302
  29.9 2.7 %collective-permute-done.5.refs_6_.refs_3_ = bf16[24,1664]{1,0:T(8,128)(2,1)S(1)} collective-permute-done((bf16[24,1664]{1,0:T(8,128)(2,1)S(1)}, bf16[24,1664]{1,0:T(8,128)(2,1)S(1)}, u32[]{:S(2)}, u32[]{:S(2)}) %collective-permute-start.5) | collective-permute-done | bytes 79904 | tf_op jit(solution)/shard_map/ppermute | solution.py:302
  32.7 0.0 collective-permute-done.6.refs_1_
  32.7 0.0 collective-permute-done.7.refs_2_
  32.7 0.0 collective-permute-done.8.refs_3_
  32.7 0.1 share.1.refs_7_
  32.7 0.1 collective-permute-start.9
  32.8 0.5 %weight.1.partial = f32[3,384,512]{2,1,0:T(8,128)S(1)} custom-call(bf16[48,3072]{1,0:T(8,128)(2,1)S(1)} %get-tuple-element.41.refs_0_, bf16[48,3072]{1,0:T(8,128)(2,1)S(1)} %collective-permute-done.6.refs_1_, bf16[48,3072]{1,0:T(8,128)(2,1)S(1)} %collective-permute-done.7.refs_2_, bf16[48,3072]{1,0:T(8,128)(2,1)S(1)} %collective-permute-done.8.refs_3_), custom_call_target="tpu_custom_call" | custom-call | tf_op jit(solution)/shard_map/weight/pallas_call | solution.py:48
  33.3 0.0 copy-done.1
  33.3 0.0 copy-done.2
  33.4 2.2 %combine.1 = (bf16[256,3072]{1,0:T(8,128)(2,1)}, f32[2,256]{1,0:T(2,128)}) custom-call(bf16[24,1664]{1,0:T(8,128)(2,1)S(1)} %get-tuple-element.36.refs_0_, bf16[24,1664]{1,0:T(8,128)(2,1)S(1)} %collective-permute-done.3.refs_4_.refs_1_, bf16[24,1664]{1,0:T(8,128)(2,1)S(1)} %collective-permute-done.4.refs_5_.refs_2_, ...), custom_call_target="tpu_custom_call" | custom-call | tf_op jit(solution)/shard_map/combine/pallas_call | solution.py:48
  35.5 0.0 collective-permute-done.9.shared
  35.5 1.7 %finish.1 = f32[3,384,512]{2,1,0:T(8,128)} custom-call(f32[3,384,512]{2,1,0:T(8,128)S(1)} %weight.1.partial, bf16[192,2304]{1,0:T(8,128)(2,1)S(1)} %collective-permute-done.9.shared), custom_call_target="tpu_custom_call" | custom-call | tf_op jit(solution)/shard_map/finish/pallas_call | solution.py:48
Async XLA Ops:
  2.4 8.9 %collective-permute-start.2 = (bf16[48,768]{1,0:T(8,128)(2,1)S(1)}, bf16[48,768]{1,0:T(8,128)(2,1)S(1)}, u32[]{:S(2)}, u32[]{:S(2)}) collective-permute-start(bf16[48,768]{1,0:T(8,128)(2,1)S(1)} %get-tuple-element.25.refs_0_), channel_id=1, source_target_pairs={{0,1},{1,0},{2,3},{3,2},{4,5},{5,4},{6,7},{7,6},{8,9},{9,8},{10,11... | collective-permute-start | bytes 221192 | tf_op jit(solution)/shard_map/ppermute | solution.py:302
  5.5 8.9 %copy-start = (bf16[512,3072]{1,0:T(8,128)(2,1)S(1)}, bf16[512,3072]{1,0:T(8,128)(2,1)}, u32[]{:S(2)}) copy-start(bf16[512,3072]{1,0:T(8,128)(2,1)} %refs_4_.1) | copy-start | bytes 9437188
  5.5 7.8 %collective-permute-start.1 = (bf16[48,768]{1,0:T(8,128)(2,1)S(1)}, bf16[48,768]{1,0:T(8,128)(2,1)S(1)}, u32[]{:S(2)}, u32[]{:S(2)}) collective-permute-start(bf16[48,768]{1,0:T(8,128)(2,1)S(1)} %get-tuple-element.26), channel_id=1, source_target_pairs={{0,2},{1,3},{2,0},{3,1},{4,6},{5,7},{6,4},{7,5},{8,10},{9,11},{10,... | collective-permute-start | bytes 221192 | tf_op jit(solution)/shard_map/ppermute | solution.py:302
  8.1 6.3 %collective-permute-start = (bf16[48,768]{1,0:T(8,128)(2,1)S(1)}, bf16[48,768]{1,0:T(8,128)(2,1)S(1)}, u32[]{:S(2)}, u32[]{:S(2)}) collective-permute-start(bf16[48,768]{1,0:T(8,128)(2,1)S(1)} %get-tuple-element.26), channel_id=1, source_target_pairs={{0,3},{1,2},{2,1},{3,0},{4,7},{5,6},{6,5},{7,4},{8,11},{9,10},{10,... | collective-permute-start | bytes 221192 | tf_op jit(solution)/shard_map/ppermute | solution.py:302
  15.8 16.9 %collective-permute-start.6 = (bf16[48,3072]{1,0:T(8,128)(2,1)S(1)}, bf16[48,3072]{1,0:T(8,128)(2,1)S(1)}, u32[]{:S(2)}, u32[]{:S(2)}) collective-permute-start(bf16[48,3072]{1,0:T(8,128)(2,1)S(1)} %get-tuple-element.42), channel_id=1, source_target_pairs={{0,8},{4,12},{8,0},{12,4},{16,24},{20,28},{24,16},{28,20},{1,9},{5... | collective-permute-start | bytes 884744 | tf_op jit(solution)/shard_map/ppermute | solution.py:302
  17.3 15.3 %collective-permute-start.7 = (bf16[48,3072]{1,0:T(8,128)(2,1)S(1)}, bf16[48,3072]{1,0:T(8,128)(2,1)S(1)}, u32[]{:S(2)}, u32[]{:S(2)}) collective-permute-start(bf16[48,3072]{1,0:T(8,128)(2,1)S(1)} %get-tuple-element.43), channel_id=1, source_target_pairs={{0,16},{4,20},{8,24},{12,28},{16,0},{20,4},{24,8},{28,12},{1,17},{... | collective-permute-start | bytes 884744 | tf_op jit(solution)/shard_map/ppermute | solution.py:302
  18.8 13.8 %collective-permute-start.8 = (bf16[48,3072]{1,0:T(8,128)(2,1)S(1)}, bf16[48,3072]{1,0:T(8,128)(2,1)S(1)}, u32[]{:S(2)}, u32[]{:S(2)}) collective-permute-start(bf16[48,3072]{1,0:T(8,128)(2,1)S(1)} %get-tuple-element.44), channel_id=1, source_target_pairs={{0,24},{4,28},{8,16},{12,20},{16,8},{20,12},{24,0},{28,4},{1,25},{... | collective-permute-start | bytes 884744 | tf_op jit(solution)/shard_map/ppermute | solution.py:302
  21.9 11.4 %copy-start.1 = (s32[256,2]{0,1:T(2,128)S(1)}, s32[256,2]{0,1:T(2,128)}, u32[]{:S(2)}) copy-start(s32[256,2]{0,1:T(2,128)} %param.8) | copy-start | bytes 6148
  21.9 11.4 %copy-start.2 = (s32[256,2]{0,1:T(2,128)S(1)}, s32[256,2]{0,1:T(2,128)}, u32[]{:S(2)}) copy-start(s32[256,2]{0,1:T(2,128)} %param.9) | copy-start | bytes 6148
  21.9 4.5 %collective-permute-start.3 = (bf16[24,1664]{1,0:T(8,128)(2,1)S(1)}, bf16[24,1664]{1,0:T(8,128)(2,1)S(1)}, u32[]{:S(2)}, u32[]{:S(2)}) collective-permute-start(bf16[24,1664]{1,0:T(8,128)(2,1)S(1)} %get-tuple-element.37), channel_id=1, source_target_pairs={{0,1},{1,0},{2,3},{3,2},{4,5},{5,4},{6,7},{7,6},{8,9},{9,8},{10,11... | collective-permute-start | bytes 239624 | tf_op jit(solution)/shard_map/ppermute | solution.py:302
  23.1 6.8 %collective-permute-start.4 = (bf16[24,1664]{1,0:T(8,128)(2,1)S(1)}, bf16[24,1664]{1,0:T(8,128)(2,1)S(1)}, u32[]{:S(2)}, u32[]{:S(2)}) collective-permute-start(bf16[24,1664]{1,0:T(8,128)(2,1)S(1)} %get-tuple-element.38), channel_id=1, source_target_pairs={{0,2},{1,3},{2,0},{3,1},{4,6},{5,7},{6,4},{7,5},{8,10},{9,11},{10,... | collective-permute-start | bytes 239624 | tf_op jit(solution)/shard_map/ppermute | solution.py:302
  26.4 6.2 %collective-permute-start.5 = (bf16[24,1664]{1,0:T(8,128)(2,1)S(1)}, bf16[24,1664]{1,0:T(8,128)(2,1)S(1)}, u32[]{:S(2)}, u32[]{:S(2)}) collective-permute-start(bf16[24,1664]{1,0:T(8,128)(2,1)S(1)} %get-tuple-element.39), channel_id=1, source_target_pairs={{0,3},{1,2},{2,1},{3,0},{4,7},{5,6},{6,5},{7,4},{8,11},{9,10},{10,... | collective-permute-start | bytes 239624 | tf_op jit(solution)/shard_map/ppermute | solution.py:302
  32.7 2.8 %collective-permute-start.9 = (bf16[192,2304]{1,0:T(8,128)(2,1)S(1)}, bf16[192,2304]{1,0:T(8,128)(2,1)S(1)}, u32[]{:S(2)}, u32[]{:S(2)}) collective-permute-start(bf16[192,2304]{1,0:T(8,128)(2,1)S(1)} %share.1.refs_7_), channel_id=1, source_target_pairs={{0,4},{4,0},{8,12},{12,8},{16,20},{20,16},{24,28},{28,24},{1,5},{5... | collective-permute-start | bytes 2654216 | tf_op jit(solution)/shard_map/ppermute | solution.py:302

commit v4 on v3

--- a/solution.py
+++ b/solution.py
@@ -12,7 +12,8 @@
 BACK_CUTS = 2
 GATE_LANES = 128
 W_CHUNKS = 4
-EARLY = (1, 2, 3)
+LAST = 3
+HEAVY = 10**11
 DISPATCH_ORDER = (0, 3, 2, 1)
 PAIRED = 8
 F32 = jnp.float32
@@ -38,7 +39,7 @@
     return lax.broadcasted_iota(jnp.int32, shape, dim)
 
 
-def call(kernel, outs, args, specs, scratch=(), near=True, out_specs=None, name=None):
+def call(kernel, outs, args, specs, scratch=(), near=True, out_specs=None, flops=0, name=None):
     args = [
         pltpu.with_memory_space_constraint(arg, pltpu.HBM) if spec is HBM else arg
         for arg, spec in zip(args, specs)
@@ -52,7 +53,7 @@
         out_specs=out_specs or jax.tree.map(lambda _: VMEM, outs),
         scratch_shapes=scratch,
         compiler_params=pltpu.CompilerParams(vmem_limit_bytes=24 * 1024 * 1024),
-        cost_estimate=pl.CostEstimate(flops=0, bytes_accessed=0, transcendentals=0),
+        cost_estimate=pl.CostEstimate(flops=flops, bytes_accessed=0, transcendentals=0),
         name=name,
     )(*args)
 
@@ -121,9 +122,8 @@
     other_out[...] = total[rows:].astype(BF16)
 
 
-def hidden_kernel(
-    inputs_hbm, w_gate, w_up, u_out, v_out, h_out, inputs, gate_buf, up_buf, sems
-):
+def hidden_kernel(n_dp, inputs_hbm, w_gate, w_up, *refs):
+    ahead, (u_out, v_out, h_out, inputs, gate_buf, up_buf, sems) = refs[:-7], refs[-7:]
     first = pltpu.make_async_copy(inputs_hbm, inputs, sems.at[2, 0])
     first.start()
     width = inputs.shape[1]
@@ -148,7 +148,13 @@
     u = a * s
     u_out[...] = u
     v_out[...] = b * s * (1.0 + a * (1.0 - s))
-    h_out[...] = u * b
+    h = u * b
+    h_out[...] = h
+    pair = 2 * (width // n_dp)
+    for m, out in enumerate(ahead):
+        start = pl.multiple_of(((lax.axis_index("dp") // 2) ^ m) * pair, 128)
+        out[:, 0:pair] = inputs[:, pl.ds(start, pair)]
+        out[:, pair:] = h.astype(BF16)
 
 
 def project_kernel(group, capacity, n_dp, *refs):
@@ -190,10 +196,14 @@
     chip = lax.axis_index("dp") // 2
     for m, send in enumerate(sends):
         start = pl.multiple_of((chip ^ m) * pair, 128)
-        send[:, 0:pair] = inputs[:, pl.ds(start, pair)]
-        send[:, pair : 2 * pair] = rows_buf[:, pl.ds(start, pair)]
-        for n, value in enumerate((da, db, h)):
-            send[:, 2 * pair + n * hidden : 2 * pair + (n + 1) * hidden] = value
+        base = 0
+        if m == LAST:
+            send[:, 0:pair] = inputs[:, pl.ds(start, pair)]
+            send[:, pair : pair + hidden] = h
+            base = pair + hidden
+        send[:, base : base + pair] = rows_buf[:, pl.ds(start, pair)]
+        send[:, base + pair : base + pair + hidden] = da
+        send[:, base + pair + hidden :] = db
 
 
 def input_kernel(group, capacity, da, db, gate, w_gate, w_up, *refs):
@@ -225,36 +235,48 @@
         out[:, span:] = gates[n * packed : (n + 1) * packed].astype(BF16)
 
 
-def share_kernel(block, chips, *refs):
-    buffers, out = refs[:chips], refs[-1]
+def halves(columns, refs):
+    first = [(ref, 0) for ref in (*refs[:LAST], refs[-1])]
+    second = [(ref, 0) for ref in refs[LAST:-1]] + [(refs[-1], columns)]
+    return first, second
+
+
+def share_kernel(block, hidden, *refs):
+    buffers, out = refs[:-1], refs[-1]
     rows = buffers[0].shape[0]
-    start = pl.multiple_of((1 - lax.axis_index("dp") % 2) * block, 128)
-    for m, ref in enumerate(buffers):
+    start = (1 - lax.axis_index("dp") % 2) * block
+    first, second = halves(2 * block + hidden, buffers)
+    middle = block + hidden
+    for m in range(LAST + 1):
         part = slice(m * rows, (m + 1) * rows)
-        out[part, 0:block] = ref[:, pl.ds(start, block)]
-        out[part, block : 2 * block] = ref[:, pl.ds(start + 2 * block, block)]
-        out[part, 2 * block :] = ref[:, 4 * block :]
-
-
-def weight_kernel(block, hidden, chips, *refs):
-    buffers, out = refs[:chips], refs[-1]
-    start = pl.multiple_of((lax.axis_index("dp") % 2) * block, 128)
-    lefts = [
-        jnp.concatenate([ref[:, pl.ds(start + at, block)] for ref in buffers], axis=0)
-        for at in (0, 2 * block)
-    ]
-    for n in range(3):
-        at = 4 * block + n * hidden
-        right = jnp.concatenate([ref[:, at : at + hidden] for ref in buffers], axis=0)
-        out[n] = tn(lefts[n // 2], right)
+        for (ref, at), to, wide in ((first[m], 0, middle), (second[m], middle, middle + hidden)):
+            out[part, to : to + block] = ref[:, pl.ds(pl.multiple_of(at + start, 128), block)]
+            at += 2 * block
+            out[part, to + block : to + wide] = ref[:, at : at + wide - block]
+
+
+def weight_kernel(block, hidden, *refs):
+    buffers, out = refs[:-1], refs[-1]
+    start = (lax.axis_index("dp") % 2) * block
+    first, second = halves(2 * block + hidden, buffers)
+
+    def gather(side, skip, wide):
+        parts = [ref[:, pl.ds(pl.multiple_of(at + skip, 128), wide)] for ref, at in side]
+        return jnp.concatenate(parts, axis=0)
+
+    inputs, grads = gather(first, start, block), gather(second, start, block)
+    out[0] = tn(inputs, gather(second, 2 * block, hidden))
+    out[1] = tn(inputs, gather(second, 2 * block + hidden, hidden))
+    out[2] = tn(grads, gather(first, 2 * block, hidden))
 
 
 def finish_kernel(block, hidden, partial, shared, out_hbm, buf, sems):
+    middle = block + hidden
+    inputs, h = shared[:, 0:block], shared[:, block:middle]
+    grads, da = shared[:, middle : middle + block], shared[:, middle + block : 2 * middle]
     copies = []
-    for n in range(3):
-        left = shared[:, (n // 2) * block : (n // 2 + 1) * block]
-        at = 2 * block + n * hidden
-        buf[n] = partial[n] + tn(left, shared[:, at : at + hidden])
+    for n, (left, right) in enumerate(((inputs, da), (inputs, shared[:, 2 * middle :]), (grads, h))):
+        buf[n] = partial[n] + tn(left, right)
         copies.append(pltpu.make_async_copy(buf.at[n], out_hbm.at[n], sems.at[n]))
         copies[-1].start()
     for copy in copies:
@@ -263,7 +285,8 @@
 
 def combine_kernel(group, capacity, *refs):
     backs = refs[:group]
-    routes, levels, slots, _, input_hbm, gate_out, input_buf, sems = refs[group:]
+    routes, levels, slots = refs[group : group + 3]
+    input_hbm, gate_out, input_buf, sems = refs[-4:]
     tokens, width = input_buf.shape
     span = width // BACK_CUTS
     packed = BACK_CUTS * capacity
@@ -346,53 +369,60 @@
         received[mask] = swap(own if mask < shards else other, "expert", group, mask)
     part = shape((rows, hidden), F32)
     weight = shape((width, hidden), BF16)
-    u, v, h, near_inputs, near_gate, near_up = call(
-        hidden_kernel,
-        (part,) * 3 + (shape((rows, width), BF16),) + (weight,) * 2,
+    ahead = shape((rows, 2 * block + hidden), BF16)
+    *ahead, u, v, h, near_inputs, near_gate, near_up = call(
+        functools.partial(hidden_kernel, n_dp),
+        (ahead,) * (LAST * paired) + (part,) * 3 + (shape((rows, width), BF16),) + (weight,) * 2,
         (saved_inputs, w_gate, w_up),
         [HBM] * 3,
         [pltpu.SemaphoreType.DMA((3, W_CHUNKS))],
+        flops=HEAVY,
         name="hidden",
     )
     half = shape((rows, hidden), BF16)
-    chips = n_dp // 2 if paired else 0
-    late = shape((rows, 4 * block + 3 * hidden), BF16)
-    outward = (late,) * chips if paired else (shape((rows, width), BF16), half)
+    late = shape((rows, 2 * block + 2 * hidden), BF16)
+    full = shape((rows, 4 * block + 3 * hidden), BF16)
+    outward = (late,) * LAST + (full,) if paired else (shape((rows, width), BF16), half)
     *sends, da, db, gate = call(
         functools.partial(project_kernel, group, capacity, n_dp),
         outward + (half, half, shape((rows, GATE_LANES), BF16)),
         (*arrange(received), w_down, u, v, h, near_inputs),
         [VMEM] * (group + 5),
         [pltpu.VMEM((rows, width), BF16)],
+        flops=HEAVY,
         name="project",
     )
+    ahead = [swap(array, "dp", n_dp, 2 * m) if m > 0 else array for m, array in enumerate(ahead)]
     back = shape((BACK_CUTS * capacity, width // BACK_CUTS + GATE_LANES), BF16)
     returns = call(
         functools.partial(input_kernel, group, capacity),
         (back,) * group,
-        (da, db, gate, near_gate, near_up),
-        [VMEM] * 5,
+        (da, db, gate, near_gate, near_up, *ahead[1:]),
+        [VMEM] * 5 + [UNUSED] * len(ahead[1:]),
+        flops=HEAVY,
         name="input",
     )
     backs = [returns[0]] + [None] * (group - 1)
     for mask in far_first(group):
         backs[mask] = swap(returns[mask], "expert", group, mask)
     if paired:
-        buffers = [sends[0]] + [swap(sends[m], "dp", n_dp, 2 * m) for m in range(1, chips)]
+        buffers = ahead + [sends[0]]
+        buffers += [swap(sends[m], "dp", n_dp, 2 * m) for m in range(1, LAST + 1)]
         sharing = call(
-            functools.partial(share_kernel, block, chips),
-            shape((chips * rows, 2 * block + 3 * hidden), BF16),
-            (*buffers, *[backs[mask] for mask in EARLY]),
-            [VMEM] * chips + [UNUSED] * len(EARLY),
+            functools.partial(share_kernel, block, hidden),
+            shape(((LAST + 1) * rows, 2 * block + 3 * hidden), BF16),
+            buffers,
+            [VMEM] * len(buffers),
             name="share",
         )
         shared = swap(sharing, "dp", n_dp, 1)
         block_shape = shape((3, block, hidden), F32)
         partial = call(
-            functools.partial(weight_kernel, block, hidden, chips),
+            functools.partial(weight_kernel, block, hidden),
             block_shape,
             buffers,
-            [VMEM] * chips,
+            [VMEM] * len(buffers),
+            flops=HEAVY,
             name="weight",
         )
         weight_grad = call(
@@ -406,16 +436,17 @@
             name="finish",
         )
     else:
-        sharing = returns[0]
         weight_grad = plain_weights(saved_inputs, sends[0], (da, db, sends[1]))
+    after = [weight_grad] if paired else []
     input_grad, gate_grad = call(
         functools.partial(combine_kernel, group, capacity),
         (shape((tokens, width), BF16), shape((2, tokens), F32)),
-        (*backs, routes, gate_levels, slots, sharing),
-        [VMEM] * (group + 3) + [UNUSED],
+        (*backs, routes, gate_levels, slots, *after),
+        [VMEM] * (group + 3) + [HBM] * len(after),
         [pltpu.VMEM((tokens, width), BF16), pltpu.SemaphoreType.DMA((2 * BACK_CUTS,))],
         near=False,
         out_specs=(HBM, VMEM),
+        flops=HEAVY,
         name="combine",
     )
     return input_grad, gate_grad.T, weight_grad.transpose(1, 0, 2)

time: 37.5 us -> 34.7 us (0.925)
  waiting for transfers between devices: 8.32 us -> 3.22 us
  starting transfers between devices: 14.6 us -> 16.8 us
    ppermute x10 -> x12, waiting for transfers between devices: 8.32 us -> 3.22 us  [swap(): return lax.ppermute(array, axis, [(n, n ^ mask) for n in range(size)])]
    ppermute x10 -> x12, starting transfers between devices: 14.6 us -> 16.8 us  [swap(): return lax.ppermute(array, axis, [(n, n ^ mask) for n in range(size)])]
  transfers between devices with their start and end apart: 10 -> 12, of which waited for: 5 -> 2; matrix products, arithmetic and copies ran while one was open for 0% -> 0% of each run, Pallas kernels for 23% -> 28%
where the time goes in v4:
time: 34.7 us; the launch traced here: 34.5 us
  starting transfers between devices  16.8 us (48%)
  Pallas kernels  13.7 us (39%)
  waiting for transfers between devices  3.22 us (9%)
  between operations  0.75 us (2%)
    ppermute x12, starting transfers between devices, swap(): return lax.ppermute(array, axis, [(n, n ^ mask) for n in range(size)])  16.8 us
    pallas_call x8, Pallas kernels, call(): pl.pallas_call(kernel, out_shape=outs, in_specs=specs, out_specs=out_spec...  13.7 us
    ppermute x12, waiting for transfers between devices, swap(): return lax.ppermute(array, axis, [(n, n ^ mask) for n in range(size)])  3.22 us
  transfers between devices with their start and end apart: 12, of which 2 were waited for; matrix products, arithmetic and copies ran while one was open for 0% of the time, Pallas kernels for 28%

profile of v4, /device:TPU:0, one launch (start us, length us, event | category | flops | bytes accessed | tf_op | source)
XLA Modules:
  0.0 34.5 jit_solution(1501318316283506880)
XLA Ops:
  0.6 1.8 %pick.1 = (bf16[48,768]{1,0:T(8,128)(2,1)S(1)}, bf16[48,768]{1,0:T(8,128)(2,1)S(1)}, s32[8,256]{1,0:T(8,128)S(1)}) custom-call(s32[2,256]{1,0:T(2,128)} %bitcast.4, s32[2,256]{1,0:T(2,128)} %bitcast.6, bf16[256,3072]{1,0:T(8,128)(2,1)} %grad_hbm.1), custom_call_target="tpu_custom_call" | custom-call | tf_op jit(solution)/shard_map/pick/pallas_call | solution.py:49
  2.4 4.1 %collective-permute-start.1 = (bf16[48,768]{1,0:T(8,128)(2,1)S(1)}, bf16[48,768]{1,0:T(8,128)(2,1)S(1)}, u32[]{:S(2)}, u32[]{:S(2)}) collective-permute-start(bf16[48,768]{1,0:T(8,128)(2,1)S(1)} %get-tuple-element.29), channel_id=1, source_target_pairs={{0,2},{1,3},{2,0},{3,1},{4,6},{5,7},{6,4},{7,5},{8,10},{9,11},{10,... | collective-permute-start | bytes 221192 | tf_op jit(solution)/shard_map/ppermute | solution.py:325
  6.5 1.3 %collective-permute-start = (bf16[48,768]{1,0:T(8,128)(2,1)S(1)}, bf16[48,768]{1,0:T(8,128)(2,1)S(1)}, u32[]{:S(2)}, u32[]{:S(2)}) collective-permute-start(bf16[48,768]{1,0:T(8,128)(2,1)S(1)} %get-tuple-element.29), channel_id=1, source_target_pairs={{0,3},{1,2},{2,1},{3,0},{4,7},{5,6},{6,5},{7,4},{8,11},{9,10},{10,... | collective-permute-start | bytes 221192 | tf_op jit(solution)/shard_map/ppermute | solution.py:325
  7.9 0.0 copy-start.2
  7.9 0.2 collective-permute-start.2
  8.1 3.4 %hidden.1 = (bf16[48,1280]{1,0:T(8,128)(2,1)S(1)}, bf16[48,1280]{1,0:T(8,128)(2,1)S(1)}, bf16[48,1280]{1,0:T(8,128)(2,1)S(1)}, f32[48,512]{1,0:T(8,128)S(1)}, f3...) custom-call(bf16[48,3072]{1,0:T(8,128)(2,1)} %inputs_hbm.1, ...), custom_call_target="tpu_custom_call" | custom-call | flops 99999997952 | tf_op jit(solution)/shard_map/hidden/pallas_call | solution.py:49
  11.5 1.6 %collective-permute-start.3 = (bf16[48,1280]{1,0:T(8,128)(2,1)S(1)}, bf16[48,1280]{1,0:T(8,128)(2,1)S(1)}, u32[]{:S(2)}, u32[]{:S(2)}) collective-permute-start(bf16[48,1280]{1,0:T(8,128)(2,1)S(1)} %get-tuple-element.39), channel_id=1, source_target_pairs={{0,8},{4,12},{8,0},{12,4},{16,24},{20,28},{24,16},{28,20},{1,9},{5... | collective-permute-start | bytes 368648 | tf_op jit(solution)/shard_map/ppermute | solution.py:325
  13.1 1.5 %collective-permute-start.4 = (bf16[48,1280]{1,0:T(8,128)(2,1)S(1)}, bf16[48,1280]{1,0:T(8,128)(2,1)S(1)}, u32[]{:S(2)}, u32[]{:S(2)}) collective-permute-start(bf16[48,1280]{1,0:T(8,128)(2,1)S(1)} %get-tuple-element.40), channel_id=1, source_target_pairs={{0,16},{4,20},{8,24},{12,28},{16,0},{20,4},{24,8},{28,12},{1,17},{... | collective-permute-start | bytes 368648 | tf_op jit(solution)/shard_map/ppermute | solution.py:325
  14.6 0.0 collective-permute-done.2.refs_3_
  14.6 0.0 collective-permute-done.1.refs_2_
  14.6 0.0 collective-permute-done.refs_1_
  14.6 0.0 copy-done.2
  14.6 1.4 %project.1 = (bf16[48,1792]{1,0:T(8,128)(2,1)S(1)}, bf16[48,1792]{1,0:T(8,128)(2,1)S(1)}, bf16[48,1792]{1,0:T(8,128)(2,1)S(1)}, bf16[48,3072]{1,0:T(8,128)(2,1)S...) custom-call(bf16[48,768]{1,0:T(8,128)(2,1)S(1)} %get-tuple-element.28.refs_0_, ...), custom_call_target="tpu_custom_call" | custom-call | flops 99999997952 | tf_op jit(solution)/shard_map/project/pallas_call | solution.py:49
  16.1 0.6 %collective-permute-start.8 = (bf16[48,1792]{1,0:T(8,128)(2,1)S(1)}, bf16[48,1792]{1,0:T(8,128)(2,1)S(1)}, u32[]{:S(2)}, u32[]{:S(2)}) collective-permute-start(bf16[48,1792]{1,0:T(8,128)(2,1)S(1)} %get-tuple-element.48), channel_id=1, source_target_pairs={{0,8},{4,12},{8,0},{12,4},{16,24},{20,28},{24,16},{28,20},{1,9},{5... | collective-permute-start | bytes 516104 | tf_op jit(solution)/shard_map/ppermute | solution.py:325
  16.6 1.2 %collective-permute-start.9 = (bf16[48,1792]{1,0:T(8,128)(2,1)S(1)}, bf16[48,1792]{1,0:T(8,128)(2,1)S(1)}, u32[]{:S(2)}, u32[]{:S(2)}) collective-permute-start(bf16[48,1792]{1,0:T(8,128)(2,1)S(1)} %get-tuple-element.49), channel_id=1, source_target_pairs={{0,16},{4,20},{8,24},{12,28},{16,0},{20,4},{24,8},{28,12},{1,17},{... | collective-permute-start | bytes 516104 | tf_op jit(solution)/shard_map/ppermute | solution.py:325
  17.9 1.7 %collective-permute-start.10 = (bf16[48,3072]{1,0:T(8,128)(2,1)S(1)}, bf16[48,3072]{1,0:T(8,128)(2,1)S(1)}, u32[]{:S(2)}, u32[]{:S(2)}) collective-permute-start(bf16[48,3072]{1,0:T(8,128)(2,1)S(1)} %get-tuple-element.50), channel_id=1, source_target_pairs={{0,24},{4,28},{8,16},{12,20},{16,8},{20,12},{24,0},{28,4},{1,25},{... | collective-permute-start | bytes 884744 | tf_op jit(solution)/shard_map/ppermute | solution.py:325
  19.6 0.0 collective-permute-done.3.refs_0_.refs_1_
  19.6 0.0 collective-permute-done.4.refs_1_.refs_2_
  19.6 2.6 %input.1 = (bf16[24,1664]{1,0:T(8,128)(2,1)S(1)}, bf16[24,1664]{1,0:T(8,128)(2,1)S(1)}, bf16[24,1664]{1,0:T(8,128)(2,1)S(1)}, bf16[24,1664]{1,0:T(8,128)(2,1)S(1)}) custom-call(bf16[48,512]{1,0:T(8,128)(2,1)S(1)} %get-tuple-element.34.da, bf16[48,512]{1,0:T(8,128)(2,1)S(1)} %get-tuple-element.35.db, bf16[48,128]{1,0:T(8,128)(2,1)S(1)} %get-tuple-element.36.gate, ...), custom_call_target="tpu_custom_call" | custom-call | flops 99999997952 | tf_op jit(solution)/shard_map/input/pallas_call | solution.py:49
  22.2 1.7 %collective-permute-start.5 = (bf16[24,1664]{1,0:T(8,128)(2,1)S(1)}, bf16[24,1664]{1,0:T(8,128)(2,1)S(1)}, u32[]{:S(2)}, u32[]{:S(2)}) collective-permute-start(bf16[24,1664]{1,0:T(8,128)(2,1)S(1)} %get-tuple-element.42), channel_id=1, source_target_pairs={{0,1},{1,0},{2,3},{3,2},{4,5},{5,4},{6,7},{7,6},{8,9},{9,8},{10,11... | collective-permute-start | bytes 239624 | tf_op jit(solution)/shard_map/ppermute | solution.py:325
  23.9 2.0 %collective-permute-start.6 = (bf16[24,1664]{1,0:T(8,128)(2,1)S(1)}, bf16[24,1664]{1,0:T(8,128)(2,1)S(1)}, u32[]{:S(2)}, u32[]{:S(2)}) collective-permute-start(bf16[24,1664]{1,0:T(8,128)(2,1)S(1)} %get-tuple-element.43), channel_id=1, source_target_pairs={{0,2},{1,3},{2,0},{3,1},{4,6},{5,7},{6,4},{7,5},{8,10},{9,11},{10,... | collective-permute-start | bytes 239624 | tf_op jit(solution)/shard_map/ppermute | solution.py:325
  25.9 0.0 collective-permute-done.8.refs_4_
  25.9 0.8 %collective-permute-start.7 = (bf16[24,1664]{1,0:T(8,128)(2,1)S(1)}, bf16[24,1664]{1,0:T(8,128)(2,1)S(1)}, u32[]{:S(2)}, u32[]{:S(2)}) collective-permute-start(bf16[24,1664]{1,0:T(8,128)(2,1)S(1)} %get-tuple-element.44), channel_id=1, source_target_pairs={{0,3},{1,2},{2,1},{3,0},{4,7},{5,6},{6,5},{7,4},{8,11},{9,10},{10,... | collective-permute-start | bytes 239624 | tf_op jit(solution)/shard_map/ppermute | solution.py:325
  26.7 1.3 %collective-permute-done.9.refs_5_ = bf16[48,1792]{1,0:T(8,128)(2,1)S(1)} collective-permute-done((bf16[48,1792]{1,0:T(8,128)(2,1)S(1)}, bf16[48,1792]{1,0:T(8,128)(2,1)S(1)}, u32[]{:S(2)}, u32[]{:S(2)}) %collective-permute-start.9) | collective-permute-done | bytes 172064 | tf_op jit(solution)/shard_map/ppermute | solution.py:325
  28.0 0.0 collective-permute-done.10.refs_6_
  28.0 0.1 share.1
  28.1 0.1 collective-permute-start.11
  28.1 0.5 %weight.1.partial = f32[3,384,512]{2,1,0:T(8,128)S(1)} custom-call(bf16[48,1280]{1,0:T(8,128)(2,1)S(1)} %get-tuple-element.46.refs_0_, bf16[48,1280]{1,0:T(8,128)(2,1)S(1)} %collective-permute-done.3.refs_0_.refs_1_, bf16[48,1280]{1,0:T(8,128)(2,1)S(1)} %collective-permute-done.4.refs_1_.refs_2_, bf16[48,1792]{1,0:T(8,128)(2,1)S(1)} %get-tuple-element.47.refs_3_, ...), custom_call_target="tpu_custom_call" | custom-call | flops 99999997952 | tf_op jit(solution)/shard_map/weight/pallas_call | solution.py:49
  28.7 0.0 copy-start
  28.7 0.0 copy-start.1
  28.7 1.9 %collective-permute-done.11.shared = bf16[192,2304]{1,0:T(8,128)(2,1)S(1)} collective-permute-done((bf16[192,2304]{1,0:T(8,128)(2,1)S(1)}, bf16[192,2304]{1,0:T(8,128)(2,1)S(1)}, u32[]{:S(2)}, u32[]{:S(2)}) %collective-permute-start.11) | collective-permute-done | bytes 884768 | tf_op jit(solution)/shard_map/ppermute | solution.py:325
  30.6 1.7 %finish.1.refs_7_ = f32[3,384,512]{2,1,0:T(8,128)} custom-call(f32[3,384,512]{2,1,0:T(8,128)S(1)} %weight.1.partial, bf16[192,2304]{1,0:T(8,128)(2,1)S(1)} %collective-permute-done.11.shared), custom_call_target="tpu_custom_call" | custom-call | tf_op jit(solution)/shard_map/finish/pallas_call | solution.py:49
  32.3 0.0 collective-permute-done.5.refs_1_
  32.3 0.0 collective-permute-done.6.refs_2_
  32.3 0.0 collective-permute-done.7.refs_3_
  32.3 0.0 copy-done
  32.3 0.0 copy-done.1
  32.3 2.2 %combine.1 = (bf16[256,3072]{1,0:T(8,128)(2,1)}, f32[2,256]{1,0:T(2,128)}) custom-call(bf16[24,1664]{1,0:T(8,128)(2,1)S(1)} %get-tuple-element.41.refs_0_, bf16[24,1664]{1,0:T(8,128)(2,1)S(1)} %collective-permute-done.5.refs_1_, bf16[24,1664]{1,0:T(8,128)(2,1)S(1)} %collective-permute-done.6.refs_2_, bf16[24,1664]{1,0:T(8,128)(2,1)S(1)} %collective-permute-done.7.refs_3_, ...), custom_call_target="tpu_custom_call" | custom-call | flops 99999997952 | tf_op jit(solution)/shard_map/combine/pallas_call | solution.py:49
Async XLA Ops:
  2.4 12.2 %collective-permute-start.1 = (bf16[48,768]{1,0:T(8,128)(2,1)S(1)}, bf16[48,768]{1,0:T(8,128)(2,1)S(1)}, u32[]{:S(2)}, u32[]{:S(2)}) collective-permute-start(bf16[48,768]{1,0:T(8,128)(2,1)S(1)} %get-tuple-element.29), channel_id=1, source_target_pairs={{0,2},{1,3},{2,0},{3,1},{4,6},{5,7},{6,4},{7,5},{8,10},{9,11},{10,... | collective-permute-start | bytes 221192 | tf_op jit(solution)/shard_map/ppermute | solution.py:325
  6.5 8.1 %collective-permute-start = (bf16[48,768]{1,0:T(8,128)(2,1)S(1)}, bf16[48,768]{1,0:T(8,128)(2,1)S(1)}, u32[]{:S(2)}, u32[]{:S(2)}) collective-permute-start(bf16[48,768]{1,0:T(8,128)(2,1)S(1)} %get-tuple-element.29), channel_id=1, source_target_pairs={{0,3},{1,2},{2,1},{3,0},{4,7},{5,6},{6,5},{7,4},{8,11},{9,10},{10,... | collective-permute-start | bytes 221192 | tf_op jit(solution)/shard_map/ppermute | solution.py:325
  7.9 6.7 %copy-start.2 = (bf16[512,3072]{1,0:T(8,128)(2,1)S(1)}, bf16[512,3072]{1,0:T(8,128)(2,1)}, u32[]{:S(2)}) copy-start(bf16[512,3072]{1,0:T(8,128)(2,1)} %refs_4_.1) | copy-start | bytes 9437188
  7.9 6.7 %collective-permute-start.2 = (bf16[48,768]{1,0:T(8,128)(2,1)S(1)}, bf16[48,768]{1,0:T(8,128)(2,1)S(1)}, u32[]{:S(2)}, u32[]{:S(2)}) collective-permute-start(bf16[48,768]{1,0:T(8,128)(2,1)S(1)} %get-tuple-element.28.refs_0_), channel_id=1, source_target_pairs={{0,1},{1,0},{2,3},{3,2},{4,5},{5,4},{6,7},{7,6},{8,9},{9,8},{10,11... | collective-permute-start | bytes 221192 | tf_op jit(solution)/shard_map/ppermute | solution.py:325
  11.5 8.1 %collective-permute-start.3 = (bf16[48,1280]{1,0:T(8,128)(2,1)S(1)}, bf16[48,1280]{1,0:T(8,128)(2,1)S(1)}, u32[]{:S(2)}, u32[]{:S(2)}) collective-permute-start(bf16[48,1280]{1,0:T(8,128)(2,1)S(1)} %get-tuple-element.39), channel_id=1, source_target_pairs={{0,8},{4,12},{8,0},{12,4},{16,24},{20,28},{24,16},{28,20},{1,9},{5... | collective-permute-start | bytes 368648 | tf_op jit(solution)/shard_map/ppermute | solution.py:325
  13.1 6.5 %collective-permute-start.4 = (bf16[48,1280]{1,0:T(8,128)(2,1)S(1)}, bf16[48,1280]{1,0:T(8,128)(2,1)S(1)}, u32[]{:S(2)}, u32[]{:S(2)}) collective-permute-start(bf16[48,1280]{1,0:T(8,128)(2,1)S(1)} %get-tuple-element.40), channel_id=1, source_target_pairs={{0,16},{4,20},{8,24},{12,28},{16,0},{20,4},{24,8},{28,12},{1,17},{... | collective-permute-start | bytes 368648 | tf_op jit(solution)/shard_map/ppermute | solution.py:325
  16.1 9.8 %collective-permute-start.8 = (bf16[48,1792]{1,0:T(8,128)(2,1)S(1)}, bf16[48,1792]{1,0:T(8,128)(2,1)S(1)}, u32[]{:S(2)}, u32[]{:S(2)}) collective-permute-start(bf16[48,1792]{1,0:T(8,128)(2,1)S(1)} %get-tuple-element.48), channel_id=1, source_target_pairs={{0,8},{4,12},{8,0},{12,4},{16,24},{20,28},{24,16},{28,20},{1,9},{5... | collective-permute-start | bytes 516104 | tf_op jit(solution)/shard_map/ppermute | solution.py:325
  16.6 11.3 %collective-permute-start.9 = (bf16[48,1792]{1,0:T(8,128)(2,1)S(1)}, bf16[48,1792]{1,0:T(8,128)(2,1)S(1)}, u32[]{:S(2)}, u32[]{:S(2)}) collective-permute-start(bf16[48,1792]{1,0:T(8,128)(2,1)S(1)} %get-tuple-element.49), channel_id=1, source_target_pairs={{0,16},{4,20},{8,24},{12,28},{16,0},{20,4},{24,8},{28,12},{1,17},{... | collective-permute-start | bytes 516104 | tf_op jit(solution)/shard_map/ppermute | solution.py:325
  17.9 10.1 %collective-permute-start.10 = (bf16[48,3072]{1,0:T(8,128)(2,1)S(1)}, bf16[48,3072]{1,0:T(8,128)(2,1)S(1)}, u32[]{:S(2)}, u32[]{:S(2)}) collective-permute-start(bf16[48,3072]{1,0:T(8,128)(2,1)S(1)} %get-tuple-element.50), channel_id=1, source_target_pairs={{0,24},{4,28},{8,16},{12,20},{16,8},{20,12},{24,0},{28,4},{1,25},{... | collective-permute-start | bytes 884744 | tf_op jit(solution)/shard_map/ppermute | solution.py:325
  22.2 10.1 %collective-permute-start.5 = (bf16[24,1664]{1,0:T(8,128)(2,1)S(1)}, bf16[24,1664]{1,0:T(8,128)(2,1)S(1)}, u32[]{:S(2)}, u32[]{:S(2)}) collective-permute-start(bf16[24,1664]{1,0:T(8,128)(2,1)S(1)} %get-tuple-element.42), channel_id=1, source_target_pairs={{0,1},{1,0},{2,3},{3,2},{4,5},{5,4},{6,7},{7,6},{8,9},{9,8},{10,11... | collective-permute-start | bytes 239624 | tf_op jit(solution)/shard_map/ppermute | solution.py:325
  23.9 8.4 %collective-permute-start.6 = (bf16[24,1664]{1,0:T(8,128)(2,1)S(1)}, bf16[24,1664]{1,0:T(8,128)(2,1)S(1)}, u32[]{:S(2)}, u32[]{:S(2)}) collective-permute-start(bf16[24,1664]{1,0:T(8,128)(2,1)S(1)} %get-tuple-element.43), channel_id=1, source_target_pairs={{0,2},{1,3},{2,0},{3,1},{4,6},{5,7},{6,4},{7,5},{8,10},{9,11},{10,... | collective-permute-start | bytes 239624 | tf_op jit(solution)/shard_map/ppermute | solution.py:325
  25.9 6.4 %collective-permute-start.7 = (bf16[24,1664]{1,0:T(8,128)(2,1)S(1)}, bf16[24,1664]{1,0:T(8,128)(2,1)S(1)}, u32[]{:S(2)}, u32[]{:S(2)}) collective-permute-start(bf16[24,1664]{1,0:T(8,128)(2,1)S(1)} %get-tuple-element.44), channel_id=1, source_target_pairs={{0,3},{1,2},{2,1},{3,0},{4,7},{5,6},{6,5},{7,4},{8,11},{9,10},{10,... | collective-permute-start | bytes 239624 | tf_op jit(solution)/shard_map/ppermute | solution.py:325
  28.1 2.5 %collective-permute-start.11 = (bf16[192,2304]{1,0:T(8,128)(2,1)S(1)}, bf16[192,2304]{1,0:T(8,128)(2,1)S(1)}, u32[]{:S(2)}, u32[]{:S(2)}) collective-permute-start(bf16[192,2304]{1,0:T(8,128)(2,1)S(1)} %share.1), channel_id=1, source_target_pairs={{0,4},{4,0},{8,12},{12,8},{16,20},{20,16},{24,28},{28,24},{1,5},{5... | collective-permute-start | bytes 2654216 | tf_op jit(solution)/shard_map/ppermute | solution.py:325
  28.7 3.7 %copy-start = (s32[256,2]{0,1:T(2,128)S(1)}, s32[256,2]{0,1:T(2,128)}, u32[]{:S(2)}) copy-start(s32[256,2]{0,1:T(2,128)} %param.8) | copy-start | bytes 6148
  28.7 3.7 %copy-start.1 = (s32[256,2]{0,1:T(2,128)S(1)}, s32[256,2]{0,1:T(2,128)}, u32[]{:S(2)}) copy-start(s32[256,2]{0,1:T(2,128)} %param.9) | copy-start | bytes 6148

commit v5 on v4

--- a/solution.py
+++ b/solution.py
@@ -15,6 +15,7 @@
 LAST = 3
 HEAVY = 10**11
 DISPATCH_ORDER = (0, 3, 2, 1)
+RETURN_ORDER = (0, 3, 1, 2)
 PAIRED = 8
 F32 = jnp.float32
 BF16 = jnp.bfloat16
@@ -58,17 +59,14 @@
     )(*args)
 
 
-def order(count):
-    return DISPATCH_ORDER if count == 4 else range(count)
-
-
-def arrange(arrays):
-    return [arrays[mask] for mask in order(len(arrays))]
-
-
-def restore(refs):
-    places = list(order(len(refs)))
-    return [refs[places.index(mask)] for mask in range(len(refs))]
+def arrange(arrays, order):
+    return [arrays[mask] for mask in order] if len(arrays) == len(order) else arrays
+
+
+def restore(refs, order):
+    if len(refs) != len(order):
+        return refs
+    return [refs[order.index(mask)] for mask in range(len(refs))]
 
 
 def pick_kernel(
@@ -151,14 +149,14 @@
     h = u * b
     h_out[...] = h
     pair = 2 * (width // n_dp)
-    for m, out in enumerate(ahead):
-        start = pl.multiple_of(((lax.axis_index("dp") // 2) ^ m) * pair, 128)
+    for out in ahead:
+        start = pl.multiple_of(((lax.axis_index("dp") // 2) ^ LAST) * pair, 128)
         out[:, 0:pair] = inputs[:, pl.ds(start, pair)]
         out[:, pair:] = h.astype(BF16)
 
 
 def project_kernel(group, capacity, n_dp, *refs):
-    received = restore(refs[:group])
+    received = restore(refs[:group], DISPATCH_ORDER)
     w_down, u_in, v_in, h_in, inputs = refs[group : group + 5]
     sends = refs[group + 5 : -4]
     da_out, db_out, gate_out, rows_buf = refs[-4:]
@@ -197,7 +195,7 @@
     for m, send in enumerate(sends):
         start = pl.multiple_of((chip ^ m) * pair, 128)
         base = 0
-        if m == LAST:
+        if m < LAST:
             send[:, 0:pair] = inputs[:, pl.ds(start, pair)]
             send[:, pair : pair + hidden] = h
             base = pair + hidden
@@ -236,8 +234,8 @@
 
 
 def halves(columns, refs):
-    first = [(ref, 0) for ref in (*refs[:LAST], refs[-1])]
-    second = [(ref, 0) for ref in refs[LAST:-1]] + [(refs[-1], columns)]
+    first = [(ref, 0) for ref in refs[: LAST + 1]]
+    second = [(ref, columns) for ref in refs[:LAST]] + [(refs[-1], 0)]
     return first, second
 
 
@@ -270,7 +268,8 @@
     out[2] = tn(grads, gather(first, 2 * block, hidden))
 
 
-def finish_kernel(block, hidden, partial, shared, out_hbm, buf, sems):
+def finish_weights(hidden, partial, shared, out_hbm, buf, sems):
+    block = buf.shape[1]
     middle = block + hidden
     inputs, h = shared[:, 0:block], shared[:, block:middle]
     grads, da = shared[:, middle : middle + block], shared[:, middle + block : 2 * middle]
@@ -279,14 +278,19 @@
         buf[n] = partial[n] + tn(left, right)
         copies.append(pltpu.make_async_copy(buf.at[n], out_hbm.at[n], sems.at[n]))
         copies[-1].start()
-    for copy in copies:
-        copy.wait()
-
-
-def combine_kernel(group, capacity, *refs):
-    backs = refs[:group]
+    return copies
+
+
+def finish_kernel(group, capacity, hidden, *refs):
+    backs = restore(refs[:group], RETURN_ORDER)
     routes, levels, slots = refs[group : group + 3]
-    input_hbm, gate_out, input_buf, sems = refs[-4:]
+    copies = []
+    if hidden > 0:
+        partial, shared = refs[group + 3 : group + 5]
+        input_hbm, gate_out, weight_hbm, weight_buf, weight_sems, input_buf, sems = refs[-7:]
+        copies += finish_weights(hidden, partial, shared, weight_hbm, weight_buf, weight_sems)
+    else:
+        input_hbm, gate_out, input_buf, sems = refs[-4:]
     tokens, width = input_buf.shape
     span = width // BACK_CUTS
     packed = BACK_CUTS * capacity
@@ -298,19 +302,17 @@
     within = row % packed
     slot = jnp.where(expert == 0, slots[0:1, :], slots[1:2, :])
     match = within % capacity == slot
-    copies = []
     for cut in range(BACK_CUTS):
         pick = (match & (within // capacity == cut)).astype(F32).astype(BF16)
         half = span // 2
-        for at in (0, half):
-            part = pl.ds(cut * span + at, half)
-            input_buf[:, part] = tn(pick, every[:, at : at + half]).astype(BF16)
-            copies.append(
-                pltpu.make_async_copy(
-                    input_buf.at[:, part], input_hbm.at[:, part], sems.at[len(copies)]
-                )
+        for n in range(2):
+            part = pl.ds(cut * span + n * half, half)
+            input_buf[:, part] = tn(pick, every[:, n * half : (n + 1) * half]).astype(BF16)
+            copy = pltpu.make_async_copy(
+                input_buf.at[:, part], input_hbm.at[:, part], sems.at[2 * cut + n]
             )
-            copies[-1].start()
+            copy.start()
+            copies.append(copy)
         if cut == 0:
             gates = tn(every[:, span:], pick)
     for k in range(2):
@@ -372,7 +374,7 @@
     ahead = shape((rows, 2 * block + hidden), BF16)
     *ahead, u, v, h, near_inputs, near_gate, near_up = call(
         functools.partial(hidden_kernel, n_dp),
-        (ahead,) * (LAST * paired) + (part,) * 3 + (shape((rows, width), BF16),) + (weight,) * 2,
+        (ahead,) * paired + (part,) * 3 + (shape((rows, width), BF16),) + (weight,) * 2,
         (saved_inputs, w_gate, w_up),
         [HBM] * 3,
         [pltpu.SemaphoreType.DMA((3, W_CHUNKS))],
@@ -382,23 +384,23 @@
     half = shape((rows, hidden), BF16)
     late = shape((rows, 2 * block + 2 * hidden), BF16)
     full = shape((rows, 4 * block + 3 * hidden), BF16)
-    outward = (late,) * LAST + (full,) if paired else (shape((rows, width), BF16), half)
+    outward = (full,) * LAST + (late,) if paired else (shape((rows, width), BF16), half)
     *sends, da, db, gate = call(
         functools.partial(project_kernel, group, capacity, n_dp),
         outward + (half, half, shape((rows, GATE_LANES), BF16)),
-        (*arrange(received), w_down, u, v, h, near_inputs),
+        (*arrange(received, DISPATCH_ORDER), w_down, u, v, h, near_inputs),
         [VMEM] * (group + 5),
         [pltpu.VMEM((rows, width), BF16)],
         flops=HEAVY,
         name="project",
     )
-    ahead = [swap(array, "dp", n_dp, 2 * m) if m > 0 else array for m, array in enumerate(ahead)]
+    ahead = [swap(array, "dp", n_dp, 2 * LAST) for array in ahead]
     back = shape((BACK_CUTS * capacity, width // BACK_CUTS + GATE_LANES), BF16)
     returns = call(
         functools.partial(input_kernel, group, capacity),
         (back,) * group,
-        (da, db, gate, near_gate, near_up, *ahead[1:]),
-        [VMEM] * 5 + [UNUSED] * len(ahead[1:]),
+        (da, db, gate, near_gate, near_up, *ahead),
+        [VMEM] * 5 + [UNUSED] * len(ahead),
         flops=HEAVY,
         name="input",
     )
@@ -406,8 +408,8 @@
     for mask in far_first(group):
         backs[mask] = swap(returns[mask], "expert", group, mask)
     if paired:
-        buffers = ahead + [sends[0]]
-        buffers += [swap(sends[m], "dp", n_dp, 2 * m) for m in range(1, LAST + 1)]
+        got = [sends[0]] + [swap(sends[m], "dp", n_dp, 2 * m) for m in range(1, LAST + 1)]
+        buffers = got[:LAST] + ahead + got[LAST:]
         sharing = call(
             functools.partial(share_kernel, block, hidden),
             shape(((LAST + 1) * rows, 2 * block + 3 * hidden), BF16),
@@ -425,30 +427,29 @@
             flops=HEAVY,
             name="weight",
         )
-        weight_grad = call(
-            functools.partial(finish_kernel, block, hidden),
-            block_shape,
-            (partial, shared),
-            [VMEM] * 2,
-            [pltpu.VMEM(block_shape.shape, F32), pltpu.SemaphoreType.DMA((3,))],
-            near=False,
-            out_specs=HBM,
-            name="finish",
-        )
+        extra = (partial, shared)
+    else:
+        extra = ()
+    finished = (shape((tokens, width), BF16), shape((2, tokens), F32))
+    scratch = [pltpu.VMEM((tokens, width), BF16), pltpu.SemaphoreType.DMA((2 * BACK_CUTS,))]
+    if paired:
+        finished += (block_shape,)
+        scratch = [pltpu.VMEM(block_shape.shape, F32), pltpu.SemaphoreType.DMA((3,))] + scratch
+    input_grad, gate_grad, *weight_grad = call(
+        functools.partial(finish_kernel, group, capacity, hidden if paired else 0),
+        finished,
+        (*arrange(backs, RETURN_ORDER), routes, gate_levels, slots, *extra),
+        [VMEM] * (group + 3 + len(extra)),
+        scratch,
+        near=False,
+        out_specs=(HBM, VMEM, HBM)[: len(finished)],
+        flops=HEAVY,
+        name="finish",
+    )
+    if paired:
+        (weight_grad,) = weight_grad
     else:
         weight_grad = plain_weights(saved_inputs, sends[0], (da, db, sends[1]))
-    after = [weight_grad] if paired else []
-    input_grad, gate_grad = call(
-        functools.partial(combine_kernel, group, capacity),
-        (shape((tokens, width), BF16), shape((2, tokens), F32)),
-        (*backs, routes, gate_levels, slots, *after),
-        [VMEM] * (group + 3) + [HBM] * len(after),
-        [pltpu.VMEM((tokens, width), BF16), pltpu.SemaphoreType.DMA((2 * BACK_CUTS,))],
-        near=False,
-        out_specs=(HBM, VMEM),
-        flops=HEAVY,
-        name="combine",
-    )
     return input_grad, gate_grad.T, weight_grad.transpose(1, 0, 2)
 
 

time: 34.7 us -> 33.8 us (0.974)
  Pallas kernels: 13.7 us -> 12.6 us
  waiting for transfers between devices: 3.22 us -> 3.7 us
    pallas_call x8 -> x7, Pallas kernels: 13.7 us -> 12.6 us  [call(): pl.pallas_call(kernel, out_shape=outs, in_specs=specs, out_specs=out_spec...]
    ppermute x12 -> x11, waiting for transfers between devices: 3.22 us -> 3.7 us  [swap(): return lax.ppermute(array, axis, [(n, n ^ mask) for n in range(size)])]
    ppermute x12 -> x11, starting transfers between devices: 16.8 us -> 16.6 us  [swap(): return lax.ppermute(array, axis, [(n, n ^ mask) for n in range(size)])]
  transfers between devices with their start and end apart: 12 -> 11, of which waited for: 2 -> 4; matrix products, arithmetic and copies ran while one was open for 0% -> 0% of each run, Pallas kernels for 28% -> 24%
where the time goes in v5:
time: 33.8 us; the launch traced here: 33.6 us
  starting transfers between devices  16.6 us (49%)
  Pallas kernels  12.6 us (37%)
  waiting for transfers between devices  3.7 us (11%)
  between operations  0.72 us (2%)
    ppermute x11, starting transfers between devices, swap(): return lax.ppermute(array, axis, [(n, n ^ mask) for n in range(size)])  16.6 us
    pallas_call x7, Pallas kernels, call(): pl.pallas_call(kernel, out_shape=outs, in_specs=specs, out_specs=out_spec...  12.6 us
    ppermute x11, waiting for transfers between devices, swap(): return lax.ppermute(array, axis, [(n, n ^ mask) for n in range(size)])  3.7 us
  transfers between devices with their start and end apart: 11, of which 4 were waited for; matrix products, arithmetic and copies ran while one was open for 0% of the time, Pallas kernels for 24%

profile of v5, /device:TPU:0, one launch (start us, length us, event | category | flops | bytes accessed | tf_op | source)
XLA Modules:
  0.0 33.6 jit_solution(4705944177986864494)
XLA Ops:
  0.6 1.8 %pick.1 = (bf16[48,768]{1,0:T(8,128)(2,1)S(1)}, bf16[48,768]{1,0:T(8,128)(2,1)S(1)}, s32[8,256]{1,0:T(8,128)S(1)}) custom-call(s32[2,256]{1,0:T(2,128)} %bitcast.4, s32[2,256]{1,0:T(2,128)} %bitcast.6, bf16[256,3072]{1,0:T(8,128)(2,1)} %grad_hbm.1), custom_call_target="tpu_custom_call" | custom-call | tf_op jit(solution)/shard_map/pick/pallas_call | solution.py:50
  2.4 4.1 %collective-permute-start.1 = (bf16[48,768]{1,0:T(8,128)(2,1)S(1)}, bf16[48,768]{1,0:T(8,128)(2,1)S(1)}, u32[]{:S(2)}, u32[]{:S(2)}) collective-permute-start(bf16[48,768]{1,0:T(8,128)(2,1)S(1)} %get-tuple-element.28), channel_id=1, source_target_pairs={{0,2},{1,3},{2,0},{3,1},{4,6},{5,7},{6,4},{7,5},{8,10},{9,11},{10,... | collective-permute-start | bytes 221192 | tf_op jit(solution)/shard_map/ppermute | solution.py:327
  6.5 1.3 %collective-permute-start = (bf16[48,768]{1,0:T(8,128)(2,1)S(1)}, bf16[48,768]{1,0:T(8,128)(2,1)S(1)}, u32[]{:S(2)}, u32[]{:S(2)}) collective-permute-start(bf16[48,768]{1,0:T(8,128)(2,1)S(1)} %get-tuple-element.28), channel_id=1, source_target_pairs={{0,3},{1,2},{2,1},{3,0},{4,7},{5,6},{6,5},{7,4},{8,11},{9,10},{10,... | collective-permute-start | bytes 221192 | tf_op jit(solution)/shard_map/ppermute | solution.py:327
  7.9 0.0 copy-start.2
  7.9 0.2 collective-permute-start.2
  8.1 3.4 %hidden.1 = (bf16[48,1280]{1,0:T(8,128)(2,1)S(1)}, f32[48,512]{1,0:T(8,128)S(1)}, f32[48,512]{1,0:T(8,128)S(1)}, f32[48,512]{1,0:T(8,128)S(1)}, bf16[48,3072]{1,...) custom-call(bf16[48,3072]{1,0:T(8,128)(2,1)} %inputs_hbm.1, bf16[3072,512]{1,0:T(8,128)(2,1)} %w_gate.1, ...), custom_call_target="tpu_custom_call" | custom-call | flops 99999997952 | tf_op jit(solution)/shard_map/hidden/pallas_call | solution.py:50
  11.5 2.5 %collective-permute-start.3 = (bf16[48,1280]{1,0:T(8,128)(2,1)S(1)}, bf16[48,1280]{1,0:T(8,128)(2,1)S(1)}, u32[]{:S(2)}, u32[]{:S(2)}) collective-permute-start(bf16[48,1280]{1,0:T(8,128)(2,1)S(1)} %get-tuple-element.38), channel_id=1, source_target_pairs={{0,24},{4,28},{8,16},{12,20},{16,8},{20,12},{24,0},{28,4},{1,25},{... | collective-permute-start | bytes 368648 | tf_op jit(solution)/shard_map/ppermute | solution.py:327
  14.0 0.0 collective-permute-done.2.refs_3_
  14.0 0.0 collective-permute-done.1.refs_2_
  14.0 0.0 collective-permute-done.refs_1_
  14.1 0.0 copy-done.2
  14.1 1.4 %project.1 = (bf16[48,3072]{1,0:T(8,128)(2,1)S(1)}, bf16[48,3072]{1,0:T(8,128)(2,1)S(1)}, bf16[48,3072]{1,0:T(8,128)(2,1)S(1)}, bf16[48,1792]{1,0:T(8,128)(2,1)S...) custom-call(bf16[48,768]{1,0:T(8,128)(2,1)S(1)} %get-tuple-element.27.refs_0_, ...), custom_call_target="tpu_custom_call" | custom-call | flops 99999997952 | tf_op jit(solution)/shard_map/project/pallas_call | solution.py:50
  15.5 1.8 %collective-permute-start.9 = (bf16[48,1792]{1,0:T(8,128)(2,1)S(1)}, bf16[48,1792]{1,0:T(8,128)(2,1)S(1)}, u32[]{:S(2)}, u32[]{:S(2)}) collective-permute-start(bf16[48,1792]{1,0:T(8,128)(2,1)S(1)} %get-tuple-element.47), channel_id=1, source_target_pairs={{0,24},{4,28},{8,16},{12,20},{16,8},{20,12},{24,0},{28,4},{1,25},{... | collective-permute-start | bytes 516104 | tf_op jit(solution)/shard_map/ppermute | solution.py:327
  17.3 0.5 %collective-permute-start.7 = (bf16[48,3072]{1,0:T(8,128)(2,1)S(1)}, bf16[48,3072]{1,0:T(8,128)(2,1)S(1)}, u32[]{:S(2)}, u32[]{:S(2)}) collective-permute-start(bf16[48,3072]{1,0:T(8,128)(2,1)S(1)} %get-tuple-element.45), channel_id=1, source_target_pairs={{0,8},{4,12},{8,0},{12,4},{16,24},{20,28},{24,16},{28,20},{1,9},{5... | collective-permute-start | bytes 884744 | tf_op jit(solution)/shard_map/ppermute | solution.py:327
  17.8 1.2 %collective-permute-start.8 = (bf16[48,3072]{1,0:T(8,128)(2,1)S(1)}, bf16[48,3072]{1,0:T(8,128)(2,1)S(1)}, u32[]{:S(2)}, u32[]{:S(2)}) collective-permute-start(bf16[48,3072]{1,0:T(8,128)(2,1)S(1)} %get-tuple-element.46), channel_id=1, source_target_pairs={{0,16},{4,20},{8,24},{12,28},{16,0},{20,4},{24,8},{28,12},{1,17},{... | collective-permute-start | bytes 884744 | tf_op jit(solution)/shard_map/ppermute | solution.py:327
  19.0 0.0 collective-permute-done.3.refs_0_.refs_3_
  19.0 2.6 %input.1 = (bf16[24,1664]{1,0:T(8,128)(2,1)S(1)}, bf16[24,1664]{1,0:T(8,128)(2,1)S(1)}, bf16[24,1664]{1,0:T(8,128)(2,1)S(1)}, bf16[24,1664]{1,0:T(8,128)(2,1)S(1)}) custom-call(bf16[48,512]{1,0:T(8,128)(2,1)S(1)} %get-tuple-element.33.da, bf16[48,512]{1,0:T(8,128)(2,1)S(1)} %get-tuple-element.34.db, bf16[48,128]{1,0:T(8,128)(2,1)S(1)} %get-tuple-element.35.gate, ...), custom_call_target="tpu_custom_call" | custom-call | flops 99999997952 | tf_op jit(solution)/shard_map/input/pallas_call | solution.py:50
  21.6 3.1 %collective-permute-start.4 = (bf16[24,1664]{1,0:T(8,128)(2,1)S(1)}, bf16[24,1664]{1,0:T(8,128)(2,1)S(1)}, u32[]{:S(2)}, u32[]{:S(2)}) collective-permute-start(bf16[24,1664]{1,0:T(8,128)(2,1)S(1)} %get-tuple-element.40), channel_id=1, source_target_pairs={{0,3},{1,2},{2,1},{3,0},{4,7},{5,6},{6,5},{7,4},{8,11},{9,10},{10,... | collective-permute-start | bytes 239624 | tf_op jit(solution)/shard_map/ppermute | solution.py:327
  24.7 0.2 collective-permute-start.5
  24.9 0.0 collective-permute-done.9.refs_4_
  24.9 1.5 %collective-permute-start.6 = (bf16[24,1664]{1,0:T(8,128)(2,1)S(1)}, bf16[24,1664]{1,0:T(8,128)(2,1)S(1)}, u32[]{:S(2)}, u32[]{:S(2)}) collective-permute-start(bf16[24,1664]{1,0:T(8,128)(2,1)S(1)} %get-tuple-element.42), channel_id=1, source_target_pairs={{0,2},{1,3},{2,0},{3,1},{4,6},{5,7},{6,4},{7,5},{8,10},{9,11},{10,... | collective-permute-start | bytes 239624 | tf_op jit(solution)/shard_map/ppermute | solution.py:327
  26.4 1.0 %collective-permute-done.7.refs_1_ = bf16[48,3072]{1,0:T(8,128)(2,1)S(1)} collective-permute-done((bf16[48,3072]{1,0:T(8,128)(2,1)S(1)}, bf16[48,3072]{1,0:T(8,128)(2,1)S(1)}, u32[]{:S(2)}, u32[]{:S(2)}) %collective-permute-start.7) | collective-permute-done | bytes 294944 | tf_op jit(solution)/shard_map/ppermute | solution.py:327
  27.4 0.6 %collective-permute-done.8.refs_2_ = bf16[48,3072]{1,0:T(8,128)(2,1)S(1)} collective-permute-done((bf16[48,3072]{1,0:T(8,128)(2,1)S(1)}, bf16[48,3072]{1,0:T(8,128)(2,1)S(1)}, u32[]{:S(2)}, u32[]{:S(2)}) %collective-permute-start.8) | collective-permute-done | bytes 294944 | tf_op jit(solution)/shard_map/ppermute | solution.py:327
  28.0 0.1 share.1
  28.1 0.0 copy-start
  28.1 0.0 copy-start.1
  28.1 0.1 collective-permute-start.10
  28.2 0.5 %weight.1.refs_7_ = f32[3,384,512]{2,1,0:T(8,128)S(1)} custom-call(bf16[48,3072]{1,0:T(8,128)(2,1)S(1)} %get-tuple-element.44.refs_0_, bf16[48,3072]{1,0:T(8,128)(2,1)S(1)} %collective-permute-done.7.refs_1_, bf16[48,3072]{1,0:T(8,128)(2,1)S(1)} %collective-permute-done.8.refs_2_, bf16[48,1280]{1,0:T(8,128)(2,1)S(1)} %collective-permute-done.3.refs_0_.refs_3_, ...), custom_call_target="tpu_custom_call" | custom-call | flops 99999997952 | tf_op jit(solution)/shard_map/weight/pallas_call | solution.py:50
  28.7 0.1 collective-permute-done.4.refs_1_
  28.8 1.9 %collective-permute-done.5.refs_2_ = bf16[24,1664]{1,0:T(8,128)(2,1)S(1)} collective-permute-done((bf16[24,1664]{1,0:T(8,128)(2,1)S(1)}, bf16[24,1664]{1,0:T(8,128)(2,1)S(1)}, u32[]{:S(2)}, u32[]{:S(2)}) %collective-permute-start.5) | collective-permute-done | bytes 79904 | tf_op jit(solution)/shard_map/ppermute | solution.py:327
  30.8 0.0 collective-permute-done.6.refs_3_
  30.8 0.0 collective-permute-done.10.refs_8_
  30.8 0.0 copy-done
  30.8 0.0 copy-done.1
  30.8 2.8 %finish.1 = (bf16[256,3072]{1,0:T(8,128)(2,1)}, f32[2,256]{1,0:T(2,128)}, f32[3,384,512]{2,1,0:T(8,128)}) custom-call(bf16[24,1664]{1,0:T(8,128)(2,1)S(1)} %get-tuple-element.39.refs_0_, bf16[24,1664]{1,0:T(8,128)(2,1)S(1)} %collective-permute-done.4.refs_1_, bf16[24,1664]{1,0:T(8,128)(2,1)S(1)} %collective-permute-done.5.refs_2_, ...), custom_call_target="tpu_custom_call" | custom-call | flops 99999997952 | tf_op jit(solution)/shard_map/finish/pallas_call | solution.py:50
Async XLA Ops:
  2.4 11.6 %collective-permute-start.1 = (bf16[48,768]{1,0:T(8,128)(2,1)S(1)}, bf16[48,768]{1,0:T(8,128)(2,1)S(1)}, u32[]{:S(2)}, u32[]{:S(2)}) collective-permute-start(bf16[48,768]{1,0:T(8,128)(2,1)S(1)} %get-tuple-element.28), channel_id=1, source_target_pairs={{0,2},{1,3},{2,0},{3,1},{4,6},{5,7},{6,4},{7,5},{8,10},{9,11},{10,... | collective-permute-start | bytes 221192 | tf_op jit(solution)/shard_map/ppermute | solution.py:327
  6.5 7.5 %collective-permute-start = (bf16[48,768]{1,0:T(8,128)(2,1)S(1)}, bf16[48,768]{1,0:T(8,128)(2,1)S(1)}, u32[]{:S(2)}, u32[]{:S(2)}) collective-permute-start(bf16[48,768]{1,0:T(8,128)(2,1)S(1)} %get-tuple-element.28), channel_id=1, source_target_pairs={{0,3},{1,2},{2,1},{3,0},{4,7},{5,6},{6,5},{7,4},{8,11},{9,10},{10,... | collective-permute-start | bytes 221192 | tf_op jit(solution)/shard_map/ppermute | solution.py:327
  7.9 6.2 %copy-start.2 = (bf16[512,3072]{1,0:T(8,128)(2,1)S(1)}, bf16[512,3072]{1,0:T(8,128)(2,1)}, u32[]{:S(2)}) copy-start(bf16[512,3072]{1,0:T(8,128)(2,1)} %refs_4_.1) | copy-start | bytes 9437188
  7.9 6.2 %collective-permute-start.2 = (bf16[48,768]{1,0:T(8,128)(2,1)S(1)}, bf16[48,768]{1,0:T(8,128)(2,1)S(1)}, u32[]{:S(2)}, u32[]{:S(2)}) collective-permute-start(bf16[48,768]{1,0:T(8,128)(2,1)S(1)} %get-tuple-element.27.refs_0_), channel_id=1, source_target_pairs={{0,1},{1,0},{2,3},{3,2},{4,5},{5,4},{6,7},{7,6},{8,9},{9,8},{10,11... | collective-permute-start | bytes 221192 | tf_op jit(solution)/shard_map/ppermute | solution.py:327
  11.5 7.5 %collective-permute-start.3 = (bf16[48,1280]{1,0:T(8,128)(2,1)S(1)}, bf16[48,1280]{1,0:T(8,128)(2,1)S(1)}, u32[]{:S(2)}, u32[]{:S(2)}) collective-permute-start(bf16[48,1280]{1,0:T(8,128)(2,1)S(1)} %get-tuple-element.38), channel_id=1, source_target_pairs={{0,24},{4,28},{8,16},{12,20},{16,8},{20,12},{24,0},{28,4},{1,25},{... | collective-permute-start | bytes 368648 | tf_op jit(solution)/shard_map/ppermute | solution.py:327
  15.5 9.4 %collective-permute-start.9 = (bf16[48,1792]{1,0:T(8,128)(2,1)S(1)}, bf16[48,1792]{1,0:T(8,128)(2,1)S(1)}, u32[]{:S(2)}, u32[]{:S(2)}) collective-permute-start(bf16[48,1792]{1,0:T(8,128)(2,1)S(1)} %get-tuple-element.47), channel_id=1, source_target_pairs={{0,24},{4,28},{8,16},{12,20},{16,8},{20,12},{24,0},{28,4},{1,25},{... | collective-permute-start | bytes 516104 | tf_op jit(solution)/shard_map/ppermute | solution.py:327
  17.3 10.1 %collective-permute-start.7 = (bf16[48,3072]{1,0:T(8,128)(2,1)S(1)}, bf16[48,3072]{1,0:T(8,128)(2,1)S(1)}, u32[]{:S(2)}, u32[]{:S(2)}) collective-permute-start(bf16[48,3072]{1,0:T(8,128)(2,1)S(1)} %get-tuple-element.45), channel_id=1, source_target_pairs={{0,8},{4,12},{8,0},{12,4},{16,24},{20,28},{24,16},{28,20},{1,9},{5... | collective-permute-start | bytes 884744 | tf_op jit(solution)/shard_map/ppermute | solution.py:327
  17.8 10.2 %collective-permute-start.8 = (bf16[48,3072]{1,0:T(8,128)(2,1)S(1)}, bf16[48,3072]{1,0:T(8,128)(2,1)S(1)}, u32[]{:S(2)}, u32[]{:S(2)}) collective-permute-start(bf16[48,3072]{1,0:T(8,128)(2,1)S(1)} %get-tuple-element.46), channel_id=1, source_target_pairs={{0,16},{4,20},{8,24},{12,28},{16,0},{20,4},{24,8},{28,12},{1,17},{... | collective-permute-start | bytes 884744 | tf_op jit(solution)/shard_map/ppermute | solution.py:327
  21.6 7.2 %collective-permute-start.4 = (bf16[24,1664]{1,0:T(8,128)(2,1)S(1)}, bf16[24,1664]{1,0:T(8,128)(2,1)S(1)}, u32[]{:S(2)}, u32[]{:S(2)}) collective-permute-start(bf16[24,1664]{1,0:T(8,128)(2,1)S(1)} %get-tuple-element.40), channel_id=1, source_target_pairs={{0,3},{1,2},{2,1},{3,0},{4,7},{5,6},{6,5},{7,4},{8,11},{9,10},{10,... | collective-permute-start | bytes 239624 | tf_op jit(solution)/shard_map/ppermute | solution.py:327
  24.7 6.1 %collective-permute-start.5 = (bf16[24,1664]{1,0:T(8,128)(2,1)S(1)}, bf16[24,1664]{1,0:T(8,128)(2,1)S(1)}, u32[]{:S(2)}, u32[]{:S(2)}) collective-permute-start(bf16[24,1664]{1,0:T(8,128)(2,1)S(1)} %get-tuple-element.41), channel_id=1, source_target_pairs={{0,1},{1,0},{2,3},{3,2},{4,5},{5,4},{6,7},{7,6},{8,9},{9,8},{10,11... | collective-permute-start | bytes 239624 | tf_op jit(solution)/shard_map/ppermute | solution.py:327
  24.9 5.9 %collective-permute-start.6 = (bf16[24,1664]{1,0:T(8,128)(2,1)S(1)}, bf16[24,1664]{1,0:T(8,128)(2,1)S(1)}, u32[]{:S(2)}, u32[]{:S(2)}) collective-permute-start(bf16[24,1664]{1,0:T(8,128)(2,1)S(1)} %get-tuple-element.42), channel_id=1, source_target_pairs={{0,2},{1,3},{2,0},{3,1},{4,6},{5,7},{6,4},{7,5},{8,10},{9,11},{10,... | collective-permute-start | bytes 239624 | tf_op jit(solution)/shard_map/ppermute | solution.py:327
  28.1 2.7 %copy-start = (s32[256,2]{0,1:T(2,128)S(1)}, s32[256,2]{0,1:T(2,128)}, u32[]{:S(2)}) copy-start(s32[256,2]{0,1:T(2,128)} %param.8) | copy-start | bytes 6148
  28.1 2.7 %copy-start.1 = (s32[256,2]{0,1:T(2,128)S(1)}, s32[256,2]{0,1:T(2,128)}, u32[]{:S(2)}) copy-start(s32[256,2]{0,1:T(2,128)} %param.9) | copy-start | bytes 6148
  28.1 2.7 %collective-permute-start.10 = (bf16[192,2304]{1,0:T(8,128)(2,1)S(1)}, bf16[192,2304]{1,0:T(8,128)(2,1)S(1)}, u32[]{:S(2)}, u32[]{:S(2)}) collective-permute-start(bf16[192,2304]{1,0:T(8,128)(2,1)S(1)} %share.1), channel_id=1, source_target_pairs={{0,4},{4,0},{8,12},{12,8},{16,20},{20,16},{24,28},{28,24},{1,5},{5... | collective-permute-start | bytes 2654216 | tf_op jit(solution)/shard_map/ppermute | solution.py:327

commit v6 on v5

--- a/solution.py
+++ b/solution.py
@@ -287,10 +287,11 @@
     copies = []
     if hidden > 0:
         partial, shared = refs[group + 3 : group + 5]
-        input_hbm, gate_out, weight_hbm, weight_buf, weight_sems, input_buf, sems = refs[-7:]
+        input_hbm, gate_hbm, weight_hbm, weight_buf, weight_sems = refs[-8:-3]
         copies += finish_weights(hidden, partial, shared, weight_hbm, weight_buf, weight_sems)
     else:
-        input_hbm, gate_out, input_buf, sems = refs[-4:]
+        input_hbm, gate_hbm = refs[-5:-3]
+    input_buf, gate_buf, sems = refs[-3:]
     tokens, width = input_buf.shape
     span = width // BACK_CUTS
     packed = BACK_CUTS * capacity
@@ -302,8 +303,17 @@
     within = row % packed
     slot = jnp.where(expert == 0, slots[0:1, :], slots[1:2, :])
     match = within % capacity == slot
-    for cut in range(BACK_CUTS):
-        pick = (match & (within // capacity == cut)).astype(F32).astype(BF16)
+    picks = [
+        (match & (within // capacity == cut)).astype(F32).astype(BF16) for cut in range(BACK_CUTS)
+    ]
+    gates = tn(every[:, span:], picks[0])
+    for k in range(2):
+        route = routes[k : k + 1, :]
+        value = jnp.where(route == 0, gates[0:1, :], jnp.where(route == 1, gates[1:2, :], 0.0))
+        gate_buf[k : k + 1, :] = value * (16.0 / levels[k : k + 1, :].astype(F32))
+    copies.append(pltpu.make_async_copy(gate_buf, gate_hbm, sems.at[2 * BACK_CUTS]))
+    copies[-1].start()
+    for cut, pick in enumerate(picks):
         half = span // 2
         for n in range(2):
             part = pl.ds(cut * span + n * half, half)
@@ -313,12 +323,6 @@
             )
             copy.start()
             copies.append(copy)
-        if cut == 0:
-            gates = tn(every[:, span:], pick)
-    for k in range(2):
-        route = routes[k : k + 1, :]
-        value = jnp.where(route == 0, gates[0:1, :], jnp.where(route == 1, gates[1:2, :], 0.0))
-        gate_out[k : k + 1, :] = value * (16.0 / levels[k : k + 1, :].astype(F32))
     for copy in copies:
         copy.wait()
 
@@ -431,7 +435,11 @@
     else:
         extra = ()
     finished = (shape((tokens, width), BF16), shape((2, tokens), F32))
-    scratch = [pltpu.VMEM((tokens, width), BF16), pltpu.SemaphoreType.DMA((2 * BACK_CUTS,))]
+    scratch = [
+        pltpu.VMEM((tokens, width), BF16),
+        pltpu.VMEM((2, tokens), F32),
+        pltpu.SemaphoreType.DMA((2 * BACK_CUTS + 1,)),
+    ]
     if paired:
         finished += (block_shape,)
         scratch = [pltpu.VMEM(block_shape.shape, F32), pltpu.SemaphoreType.DMA((3,))] + scratch
@@ -442,7 +450,7 @@
         [VMEM] * (group + 3 + len(extra)),
         scratch,
         near=False,
-        out_specs=(HBM, VMEM, HBM)[: len(finished)],
+        out_specs=(HBM,) * len(finished),
         flops=HEAVY,
         name="finish",
     )

time: 33.8 us -> 33.2 us (0.982)
  Pallas kernels: 12.6 us -> 12.1 us
    pallas_call x7, Pallas kernels: 12.6 us -> 12.1 us  [call(): pl.pallas_call(kernel, out_shape=outs, in_specs=specs, out_specs=out_spec...]
where the time goes in v6:
time: 33.2 us; the launch traced here: 33.1 us
  starting transfers between devices  16.6 us (50%)
  Pallas kernels  12.1 us (36%)
  waiting for transfers between devices  3.7 us (11%)
  between operations  0.72 us (2%)
    ppermute x11, starting transfers between devices, swap(): return lax.ppermute(array, axis, [(n, n ^ mask) for n in range(size)])  16.6 us
    pallas_call x7, Pallas kernels, call(): pl.pallas_call(kernel, out_shape=outs, in_specs=specs, out_specs=out_spec...  12.1 us
    ppermute x11, waiting for transfers between devices, swap(): return lax.ppermute(array, axis, [(n, n ^ mask) for n in range(size)])  3.7 us
  transfers between devices with their start and end apart: 11, of which 4 were waited for; matrix products, arithmetic and copies ran while one was open for 0% of the time, Pallas kernels for 24%

profile of v6, /device:TPU:0, one launch (start us, length us, event | category | flops | bytes accessed | tf_op | source)
XLA Modules:
  0.0 33.1 jit_solution(10977967645581765292)
XLA Ops:
  0.6 1.8 %pick.1 = (bf16[48,768]{1,0:T(8,128)(2,1)S(1)}, bf16[48,768]{1,0:T(8,128)(2,1)S(1)}, s32[8,256]{1,0:T(8,128)S(1)}) custom-call(s32[2,256]{1,0:T(2,128)} %bitcast.4, s32[2,256]{1,0:T(2,128)} %bitcast.6, bf16[256,3072]{1,0:T(8,128)(2,1)} %grad_hbm.1), custom_call_target="tpu_custom_call" | custom-call | tf_op jit(solution)/shard_map/pick/pallas_call | solution.py:50
  2.4 4.1 %collective-permute-start.1 = (bf16[48,768]{1,0:T(8,128)(2,1)S(1)}, bf16[48,768]{1,0:T(8,128)(2,1)S(1)}, u32[]{:S(2)}, u32[]{:S(2)}) collective-permute-start(bf16[48,768]{1,0:T(8,128)(2,1)S(1)} %get-tuple-element.28), channel_id=1, source_target_pairs={{0,2},{1,3},{2,0},{3,1},{4,6},{5,7},{6,4},{7,5},{8,10},{9,11},{10,... | collective-permute-start | bytes 221192 | tf_op jit(solution)/shard_map/ppermute | solution.py:331
  6.5 1.3 %collective-permute-start = (bf16[48,768]{1,0:T(8,128)(2,1)S(1)}, bf16[48,768]{1,0:T(8,128)(2,1)S(1)}, u32[]{:S(2)}, u32[]{:S(2)}) collective-permute-start(bf16[48,768]{1,0:T(8,128)(2,1)S(1)} %get-tuple-element.28), channel_id=1, source_target_pairs={{0,3},{1,2},{2,1},{3,0},{4,7},{5,6},{6,5},{7,4},{8,11},{9,10},{10,... | collective-permute-start | bytes 221192 | tf_op jit(solution)/shard_map/ppermute | solution.py:331
  7.9 0.0 copy-start.2
  7.9 0.2 collective-permute-start.2
  8.1 3.4 %hidden.1 = (bf16[48,1280]{1,0:T(8,128)(2,1)S(1)}, f32[48,512]{1,0:T(8,128)S(1)}, f32[48,512]{1,0:T(8,128)S(1)}, f32[48,512]{1,0:T(8,128)S(1)}, bf16[48,3072]{1,...) custom-call(bf16[48,3072]{1,0:T(8,128)(2,1)} %inputs_hbm.1, bf16[3072,512]{1,0:T(8,128)(2,1)} %w_gate.1, ...), custom_call_target="tpu_custom_call" | custom-call | flops 99999997952 | tf_op jit(solution)/shard_map/hidden/pallas_call | solution.py:50
  11.5 2.5 %collective-permute-start.3 = (bf16[48,1280]{1,0:T(8,128)(2,1)S(1)}, bf16[48,1280]{1,0:T(8,128)(2,1)S(1)}, u32[]{:S(2)}, u32[]{:S(2)}) collective-permute-start(bf16[48,1280]{1,0:T(8,128)(2,1)S(1)} %get-tuple-element.38), channel_id=1, source_target_pairs={{0,24},{4,28},{8,16},{12,20},{16,8},{20,12},{24,0},{28,4},{1,25},{... | collective-permute-start | bytes 368648 | tf_op jit(solution)/shard_map/ppermute | solution.py:331
  14.0 0.0 collective-permute-done.2.refs_3_
  14.0 0.0 collective-permute-done.1.refs_2_
  14.0 0.0 collective-permute-done.refs_1_
  14.1 0.0 copy-done.2
  14.1 1.4 %project.1 = (bf16[48,3072]{1,0:T(8,128)(2,1)S(1)}, bf16[48,3072]{1,0:T(8,128)(2,1)S(1)}, bf16[48,3072]{1,0:T(8,128)(2,1)S(1)}, bf16[48,1792]{1,0:T(8,128)(2,1)S...) custom-call(bf16[48,768]{1,0:T(8,128)(2,1)S(1)} %get-tuple-element.27.refs_0_, ...), custom_call_target="tpu_custom_call" | custom-call | flops 99999997952 | tf_op jit(solution)/shard_map/project/pallas_call | solution.py:50
  15.5 1.8 %collective-permute-start.9 = (bf16[48,1792]{1,0:T(8,128)(2,1)S(1)}, bf16[48,1792]{1,0:T(8,128)(2,1)S(1)}, u32[]{:S(2)}, u32[]{:S(2)}) collective-permute-start(bf16[48,1792]{1,0:T(8,128)(2,1)S(1)} %get-tuple-element.47), channel_id=1, source_target_pairs={{0,24},{4,28},{8,16},{12,20},{16,8},{20,12},{24,0},{28,4},{1,25},{... | collective-permute-start | bytes 516104 | tf_op jit(solution)/shard_map/ppermute | solution.py:331
  17.3 0.5 %collective-permute-start.7 = (bf16[48,3072]{1,0:T(8,128)(2,1)S(1)}, bf16[48,3072]{1,0:T(8,128)(2,1)S(1)}, u32[]{:S(2)}, u32[]{:S(2)}) collective-permute-start(bf16[48,3072]{1,0:T(8,128)(2,1)S(1)} %get-tuple-element.45), channel_id=1, source_target_pairs={{0,8},{4,12},{8,0},{12,4},{16,24},{20,28},{24,16},{28,20},{1,9},{5... | collective-permute-start | bytes 884744 | tf_op jit(solution)/shard_map/ppermute | solution.py:331
  17.8 1.2 %collective-permute-start.8 = (bf16[48,3072]{1,0:T(8,128)(2,1)S(1)}, bf16[48,3072]{1,0:T(8,128)(2,1)S(1)}, u32[]{:S(2)}, u32[]{:S(2)}) collective-permute-start(bf16[48,3072]{1,0:T(8,128)(2,1)S(1)} %get-tuple-element.46), channel_id=1, source_target_pairs={{0,16},{4,20},{8,24},{12,28},{16,0},{20,4},{24,8},{28,12},{1,17},{... | collective-permute-start | bytes 884744 | tf_op jit(solution)/shard_map/ppermute | solution.py:331
  19.0 0.0 collective-permute-done.3.refs_0_.refs_3_
  19.0 2.6 %input.1 = (bf16[24,1664]{1,0:T(8,128)(2,1)S(1)}, bf16[24,1664]{1,0:T(8,128)(2,1)S(1)}, bf16[24,1664]{1,0:T(8,128)(2,1)S(1)}, bf16[24,1664]{1,0:T(8,128)(2,1)S(1)}) custom-call(bf16[48,512]{1,0:T(8,128)(2,1)S(1)} %get-tuple-element.33.da, bf16[48,512]{1,0:T(8,128)(2,1)S(1)} %get-tuple-element.34.db, bf16[48,128]{1,0:T(8,128)(2,1)S(1)} %get-tuple-element.35.gate, ...), custom_call_target="tpu_custom_call" | custom-call | flops 99999997952 | tf_op jit(solution)/shard_map/input/pallas_call | solution.py:50
  21.6 3.1 %collective-permute-start.4 = (bf16[24,1664]{1,0:T(8,128)(2,1)S(1)}, bf16[24,1664]{1,0:T(8,128)(2,1)S(1)}, u32[]{:S(2)}, u32[]{:S(2)}) collective-permute-start(bf16[24,1664]{1,0:T(8,128)(2,1)S(1)} %get-tuple-element.40), channel_id=1, source_target_pairs={{0,3},{1,2},{2,1},{3,0},{4,7},{5,6},{6,5},{7,4},{8,11},{9,10},{10,... | collective-permute-start | bytes 239624 | tf_op jit(solution)/shard_map/ppermute | solution.py:331
  24.7 0.2 collective-permute-start.5
  24.9 0.0 collective-permute-done.9.refs_4_
  24.9 1.5 %collective-permute-start.6 = (bf16[24,1664]{1,0:T(8,128)(2,1)S(1)}, bf16[24,1664]{1,0:T(8,128)(2,1)S(1)}, u32[]{:S(2)}, u32[]{:S(2)}) collective-permute-start(bf16[24,1664]{1,0:T(8,128)(2,1)S(1)} %get-tuple-element.42), channel_id=1, source_target_pairs={{0,2},{1,3},{2,0},{3,1},{4,6},{5,7},{6,4},{7,5},{8,10},{9,11},{10,... | collective-permute-start | bytes 239624 | tf_op jit(solution)/shard_map/ppermute | solution.py:331
  26.4 1.0 %collective-permute-done.7.refs_1_ = bf16[48,3072]{1,0:T(8,128)(2,1)S(1)} collective-permute-done((bf16[48,3072]{1,0:T(8,128)(2,1)S(1)}, bf16[48,3072]{1,0:T(8,128)(2,1)S(1)}, u32[]{:S(2)}, u32[]{:S(2)}) %collective-permute-start.7) | collective-permute-done | bytes 294944 | tf_op jit(solution)/shard_map/ppermute | solution.py:331
  27.4 0.6 %collective-permute-done.8.refs_2_ = bf16[48,3072]{1,0:T(8,128)(2,1)S(1)} collective-permute-done((bf16[48,3072]{1,0:T(8,128)(2,1)S(1)}, bf16[48,3072]{1,0:T(8,128)(2,1)S(1)}, u32[]{:S(2)}, u32[]{:S(2)}) %collective-permute-start.8) | collective-permute-done | bytes 294944 | tf_op jit(solution)/shard_map/ppermute | solution.py:331
  28.0 0.1 share.1
  28.1 0.0 copy-start
  28.1 0.0 copy-start.1
  28.1 0.1 collective-permute-start.10
  28.2 0.5 %weight.1.refs_7_ = f32[3,384,512]{2,1,0:T(8,128)S(1)} custom-call(bf16[48,3072]{1,0:T(8,128)(2,1)S(1)} %get-tuple-element.44.refs_0_, bf16[48,3072]{1,0:T(8,128)(2,1)S(1)} %collective-permute-done.7.refs_1_, bf16[48,3072]{1,0:T(8,128)(2,1)S(1)} %collective-permute-done.8.refs_2_, bf16[48,1280]{1,0:T(8,128)(2,1)S(1)} %collective-permute-done.3.refs_0_.refs_3_, ...), custom_call_target="tpu_custom_call" | custom-call | flops 99999997952 | tf_op jit(solution)/shard_map/weight/pallas_call | solution.py:50
  28.7 0.1 collective-permute-done.4.refs_1_
  28.8 1.9 %collective-permute-done.5.refs_2_ = bf16[24,1664]{1,0:T(8,128)(2,1)S(1)} collective-permute-done((bf16[24,1664]{1,0:T(8,128)(2,1)S(1)}, bf16[24,1664]{1,0:T(8,128)(2,1)S(1)}, u32[]{:S(2)}, u32[]{:S(2)}) %collective-permute-start.5) | collective-permute-done | bytes 79904 | tf_op jit(solution)/shard_map/ppermute | solution.py:331
  30.8 0.0 collective-permute-done.6.refs_3_
  30.8 0.0 collective-permute-done.10.refs_8_
  30.8 0.0 copy-done
  30.8 0.0 copy-done.1
  30.8 2.3 %finish.1 = (bf16[256,3072]{1,0:T(8,128)(2,1)}, f32[2,256]{1,0:T(2,128)}, f32[3,384,512]{2,1,0:T(8,128)}) custom-call(bf16[24,1664]{1,0:T(8,128)(2,1)S(1)} %get-tuple-element.39.refs_0_, bf16[24,1664]{1,0:T(8,128)(2,1)S(1)} %collective-permute-done.4.refs_1_, bf16[24,1664]{1,0:T(8,128)(2,1)S(1)} %collective-permute-done.5.refs_2_, ...), custom_call_target="tpu_custom_call" | custom-call | flops 99999997952 | tf_op jit(solution)/shard_map/finish/pallas_call | solution.py:50
Async XLA Ops:
  2.4 11.6 %collective-permute-start.1 = (bf16[48,768]{1,0:T(8,128)(2,1)S(1)}, bf16[48,768]{1,0:T(8,128)(2,1)S(1)}, u32[]{:S(2)}, u32[]{:S(2)}) collective-permute-start(bf16[48,768]{1,0:T(8,128)(2,1)S(1)} %get-tuple-element.28), channel_id=1, source_target_pairs={{0,2},{1,3},{2,0},{3,1},{4,6},{5,7},{6,4},{7,5},{8,10},{9,11},{10,... | collective-permute-start | bytes 221192 | tf_op jit(solution)/shard_map/ppermute | solution.py:331
  6.5 7.5 %collective-permute-start = (bf16[48,768]{1,0:T(8,128)(2,1)S(1)}, bf16[48,768]{1,0:T(8,128)(2,1)S(1)}, u32[]{:S(2)}, u32[]{:S(2)}) collective-permute-start(bf16[48,768]{1,0:T(8,128)(2,1)S(1)} %get-tuple-element.28), channel_id=1, source_target_pairs={{0,3},{1,2},{2,1},{3,0},{4,7},{5,6},{6,5},{7,4},{8,11},{9,10},{10,... | collective-permute-start | bytes 221192 | tf_op jit(solution)/shard_map/ppermute | solution.py:331
  7.9 6.2 %copy-start.2 = (bf16[512,3072]{1,0:T(8,128)(2,1)S(1)}, bf16[512,3072]{1,0:T(8,128)(2,1)}, u32[]{:S(2)}) copy-start(bf16[512,3072]{1,0:T(8,128)(2,1)} %refs_4_.1) | copy-start | bytes 9437188
  7.9 6.2 %collective-permute-start.2 = (bf16[48,768]{1,0:T(8,128)(2,1)S(1)}, bf16[48,768]{1,0:T(8,128)(2,1)S(1)}, u32[]{:S(2)}, u32[]{:S(2)}) collective-permute-start(bf16[48,768]{1,0:T(8,128)(2,1)S(1)} %get-tuple-element.27.refs_0_), channel_id=1, source_target_pairs={{0,1},{1,0},{2,3},{3,2},{4,5},{5,4},{6,7},{7,6},{8,9},{9,8},{10,11... | collective-permute-start | bytes 221192 | tf_op jit(solution)/shard_map/ppermute | solution.py:331
  11.5 7.5 %collective-permute-start.3 = (bf16[48,1280]{1,0:T(8,128)(2,1)S(1)}, bf16[48,1280]{1,0:T(8,128)(2,1)S(1)}, u32[]{:S(2)}, u32[]{:S(2)}) collective-permute-start(bf16[48,1280]{1,0:T(8,128)(2,1)S(1)} %get-tuple-element.38), channel_id=1, source_target_pairs={{0,24},{4,28},{8,16},{12,20},{16,8},{20,12},{24,0},{28,4},{1,25},{... | collective-permute-start | bytes 368648 | tf_op jit(solution)/shard_map/ppermute | solution.py:331
  15.5 9.4 %collective-permute-start.9 = (bf16[48,1792]{1,0:T(8,128)(2,1)S(1)}, bf16[48,1792]{1,0:T(8,128)(2,1)S(1)}, u32[]{:S(2)}, u32[]{:S(2)}) collective-permute-start(bf16[48,1792]{1,0:T(8,128)(2,1)S(1)} %get-tuple-element.47), channel_id=1, source_target_pairs={{0,24},{4,28},{8,16},{12,20},{16,8},{20,12},{24,0},{28,4},{1,25},{... | collective-permute-start | bytes 516104 | tf_op jit(solution)/shard_map/ppermute | solution.py:331
  17.3 10.1 %collective-permute-start.7 = (bf16[48,3072]{1,0:T(8,128)(2,1)S(1)}, bf16[48,3072]{1,0:T(8,128)(2,1)S(1)}, u32[]{:S(2)}, u32[]{:S(2)}) collective-permute-start(bf16[48,3072]{1,0:T(8,128)(2,1)S(1)} %get-tuple-element.45), channel_id=1, source_target_pairs={{0,8},{4,12},{8,0},{12,4},{16,24},{20,28},{24,16},{28,20},{1,9},{5... | collective-permute-start | bytes 884744 | tf_op jit(solution)/shard_map/ppermute | solution.py:331
  17.8 10.2 %collective-permute-start.8 = (bf16[48,3072]{1,0:T(8,128)(2,1)S(1)}, bf16[48,3072]{1,0:T(8,128)(2,1)S(1)}, u32[]{:S(2)}, u32[]{:S(2)}) collective-permute-start(bf16[48,3072]{1,0:T(8,128)(2,1)S(1)} %get-tuple-element.46), channel_id=1, source_target_pairs={{0,16},{4,20},{8,24},{12,28},{16,0},{20,4},{24,8},{28,12},{1,17},{... | collective-permute-start | bytes 884744 | tf_op jit(solution)/shard_map/ppermute | solution.py:331
  21.6 7.2 %collective-permute-start.4 = (bf16[24,1664]{1,0:T(8,128)(2,1)S(1)}, bf16[24,1664]{1,0:T(8,128)(2,1)S(1)}, u32[]{:S(2)}, u32[]{:S(2)}) collective-permute-start(bf16[24,1664]{1,0:T(8,128)(2,1)S(1)} %get-tuple-element.40), channel_id=1, source_target_pairs={{0,3},{1,2},{2,1},{3,0},{4,7},{5,6},{6,5},{7,4},{8,11},{9,10},{10,... | collective-permute-start | bytes 239624 | tf_op jit(solution)/shard_map/ppermute | solution.py:331
  24.7 6.1 %collective-permute-start.5 = (bf16[24,1664]{1,0:T(8,128)(2,1)S(1)}, bf16[24,1664]{1,0:T(8,128)(2,1)S(1)}, u32[]{:S(2)}, u32[]{:S(2)}) collective-permute-start(bf16[24,1664]{1,0:T(8,128)(2,1)S(1)} %get-tuple-element.41), channel_id=1, source_target_pairs={{0,1},{1,0},{2,3},{3,2},{4,5},{5,4},{6,7},{7,6},{8,9},{9,8},{10,11... | collective-permute-start | bytes 239624 | tf_op jit(solution)/shard_map/ppermute | solution.py:331
  24.9 5.9 %collective-permute-start.6 = (bf16[24,1664]{1,0:T(8,128)(2,1)S(1)}, bf16[24,1664]{1,0:T(8,128)(2,1)S(1)}, u32[]{:S(2)}, u32[]{:S(2)}) collective-permute-start(bf16[24,1664]{1,0:T(8,128)(2,1)S(1)} %get-tuple-element.42), channel_id=1, source_target_pairs={{0,2},{1,3},{2,0},{3,1},{4,6},{5,7},{6,4},{7,5},{8,10},{9,11},{10,... | collective-permute-start | bytes 239624 | tf_op jit(solution)/shard_map/ppermute | solution.py:331
  28.1 2.7 %copy-start = (s32[256,2]{0,1:T(2,128)S(1)}, s32[256,2]{0,1:T(2,128)}, u32[]{:S(2)}) copy-start(s32[256,2]{0,1:T(2,128)} %param.8) | copy-start | bytes 6148
  28.1 2.7 %copy-start.1 = (s32[256,2]{0,1:T(2,128)S(1)}, s32[256,2]{0,1:T(2,128)}, u32[]{:S(2)}) copy-start(s32[256,2]{0,1:T(2,128)} %param.9) | copy-start | bytes 6148
  28.1 2.7 %collective-permute-start.10 = (bf16[192,2304]{1,0:T(8,128)(2,1)S(1)}, bf16[192,2304]{1,0:T(8,128)(2,1)S(1)}, u32[]{:S(2)}, u32[]{:S(2)}) collective-permute-start(bf16[192,2304]{1,0:T(8,128)(2,1)S(1)} %share.1), channel_id=1, source_target_pairs={{0,4},{4,0},{8,12},{12,8},{16,20},{20,16},{24,28},{28,24},{1,5},{5... | collective-permute-start | bytes 2654216 | tf_op jit(solution)/shard_map/ppermute | solution.py:331

commit v7 on v6

--- a/solution.py
+++ b/solution.py
@@ -40,7 +40,7 @@
     return lax.broadcasted_iota(jnp.int32, shape, dim)
 
 
-def call(kernel, outs, args, specs, scratch=(), near=True, out_specs=None, flops=0, name=None):
+def call(kernel, outs, args, specs, scratch=(), near=True, out_specs=None, aliases=None, flops=0, name=None):
     args = [
         pltpu.with_memory_space_constraint(arg, pltpu.HBM) if spec is HBM else arg
         for arg, spec in zip(args, specs)
@@ -53,6 +53,7 @@
         in_specs=specs,
         out_specs=out_specs or jax.tree.map(lambda _: VMEM, outs),
         scratch_shapes=scratch,
+        input_output_aliases=aliases or {},
         compiler_params=pltpu.CompilerParams(vmem_limit_bytes=24 * 1024 * 1024),
         cost_estimate=pl.CostEstimate(flops=flops, bytes_accessed=0, transcendentals=0),
         name=name,
@@ -120,39 +121,25 @@
     other_out[...] = total[rows:].astype(BF16)
 
 
-def hidden_kernel(n_dp, inputs_hbm, w_gate, w_up, *refs):
-    ahead, (u_out, v_out, h_out, inputs, gate_buf, up_buf, sems) = refs[:-7], refs[-7:]
-    first = pltpu.make_async_copy(inputs_hbm, inputs, sems.at[2, 0])
-    first.start()
-    width = inputs.shape[1]
-    step = width // W_CHUNKS
-    copies = []
-    for k in range(W_CHUNKS):
-        part = pl.ds(k * step, step)
-        for n, (src, dst) in enumerate(((w_gate, gate_buf), (w_up, up_buf))):
-            copy = pltpu.make_async_copy(src.at[part], dst.at[part], sems.at[n, k])
-            copy.start()
-            copies.append(copy)
-    first.wait()
-    a = jnp.zeros(u_out.shape, F32)
-    b = jnp.zeros(u_out.shape, F32)
-    for k in range(W_CHUNKS):
-        left = inputs[:, k * step : (k + 1) * step]
-        copies[2 * k].wait()
-        a += nn(left, gate_buf[k * step : (k + 1) * step, :])
-        copies[2 * k + 1].wait()
-        b += nn(left, up_buf[k * step : (k + 1) * step, :])
+def hidden_kernel(n_dp, inputs, w_gate, w_up, *refs):
+    ahead, (u_out, v_out, h_out) = refs[:-3], refs[-3:]
+    a = nn(inputs[...], w_gate[...])
+    b = nn(inputs[...], w_up[...])
     s = jax.nn.sigmoid(a)
     u = a * s
     u_out[...] = u
     v_out[...] = b * s * (1.0 + a * (1.0 - s))
     h = u * b
     h_out[...] = h
-    pair = 2 * (width // n_dp)
+    pair = 2 * (inputs.shape[1] // n_dp)
     for out in ahead:
         start = pl.multiple_of(((lax.axis_index("dp") // 2) ^ LAST) * pair, 128)
         out[:, 0:pair] = inputs[:, pl.ds(start, pair)]
         out[:, pair:] = h.astype(BF16)
+
+
+def pass_kernel(*refs):
+    pass
 
 
 def project_kernel(group, capacity, n_dp, *refs):
@@ -370,18 +357,25 @@
         ],
         name="pick",
     )
+    own, other = call(
+        pass_kernel,
+        (packed,) * 2,
+        (own, other),
+        [VMEM] * 2,
+        aliases={0: 0, 1: 1},
+        flops=HEAVY,
+        name="pass",
+    )
     received = [own] + [None] * (group - 1)
     for mask in far_first(group):
         received[mask] = swap(own if mask < shards else other, "expert", group, mask)
     part = shape((rows, hidden), F32)
-    weight = shape((width, hidden), BF16)
     ahead = shape((rows, 2 * block + hidden), BF16)
-    *ahead, u, v, h, near_inputs, near_gate, near_up = call(
+    *ahead, u, v, h = call(
         functools.partial(hidden_kernel, n_dp),
-        (ahead,) * paired + (part,) * 3 + (shape((rows, width), BF16),) + (weight,) * 2,
+        (ahead,) * paired + (part,) * 3,
         (saved_inputs, w_gate, w_up),
-        [HBM] * 3,
-        [pltpu.SemaphoreType.DMA((3, W_CHUNKS))],
+        [VMEM] * 3,
         flops=HEAVY,
         name="hidden",
     )
@@ -392,7 +386,7 @@
     *sends, da, db, gate = call(
         functools.partial(project_kernel, group, capacity, n_dp),
         outward + (half, half, shape((rows, GATE_LANES), BF16)),
-        (*arrange(received, DISPATCH_ORDER), w_down, u, v, h, near_inputs),
+        (*arrange(received, DISPATCH_ORDER), w_down, u, v, h, saved_inputs),
         [VMEM] * (group + 5),
         [pltpu.VMEM((rows, width), BF16)],
         flops=HEAVY,
@@ -403,7 +397,7 @@
     returns = call(
         functools.partial(input_kernel, group, capacity),
         (back,) * group,
-        (da, db, gate, near_gate, near_up, *ahead),
+        (da, db, gate, w_gate, w_up, *ahead),
         [VMEM] * 5 + [UNUSED] * len(ahead),
         flops=HEAVY,
         name="input",

time: 33.2 us -> 32.6 us (0.982)
  Pallas kernels: 12.1 us -> 9.87 us
  waiting for transfers between devices: 3.7 us -> 4.92 us
    pallas_call x7 -> x8, Pallas kernels: 12.1 us -> 9.87 us  [call(): pl.pallas_call(kernel, out_shape=outs, in_specs=specs, out_specs=out_spec...]
    ppermute x11, waiting for transfers between devices: 3.7 us -> 4.92 us  [swap(): return lax.ppermute(array, axis, [(n, n ^ mask) for n in range(size)])]
  transfers between devices with their start and end apart: 11 -> 11, of which waited for: 4 -> 3; matrix products, arithmetic and copies ran while one was open for 0% -> 0% of each run, Pallas kernels for 24% -> 18%
where the time goes in v7:
time: 32.6 us; the launch traced here: 32.5 us
  starting transfers between devices  16.9 us (52%)
  Pallas kernels  9.87 us (30%)
  waiting for transfers between devices  4.92 us (15%)
  between operations  0.75 us (2%)
    ppermute x11, starting transfers between devices, swap(): return lax.ppermute(array, axis, [(n, n ^ mask) for n in range(size)])  16.9 us
    pallas_call x8, Pallas kernels, call(): pl.pallas_call(kernel, out_shape=outs, in_specs=specs, out_specs=out_spec...  9.87 us
    ppermute x11, waiting for transfers between devices, swap(): return lax.ppermute(array, axis, [(n, n ^ mask) for n in range(size)])  4.92 us
  transfers between devices with their start and end apart: 11, of which 3 were waited for; matrix products, arithmetic and copies ran while one was open for 0% of the time, Pallas kernels for 18%

profile of v7, /device:TPU:0, one launch (start us, length us, event | category | flops | bytes accessed | tf_op | source)
XLA Modules:
  0.0 32.5 jit_solution(16136824489622522668)
XLA Ops:
  0.6 1.8 %pick.1 = (bf16[48,768]{1,0:T(8,128)(2,1)S(1)}, bf16[48,768]{1,0:T(8,128)(2,1)S(1)}, s32[8,256]{1,0:T(8,128)S(1)}) custom-call(s32[2,256]{1,0:T(2,128)} %bitcast.4, s32[2,256]{1,0:T(2,128)} %bitcast.6, bf16[256,3072]{1,0:T(8,128)(2,1)} %grad_hbm.1), custom_call_target="tpu_custom_call" | custom-call | tf_op jit(solution)/shard_map/pick/pallas_call | solution.py:50
  2.4 0.0 copy-start.3
  2.5 0.0 copy-start.4
  2.5 0.0 copy-start.5
  2.5 4.1 %collective-permute-start.1 = (bf16[48,768]{1,0:T(8,128)(2,1)S(1)}, bf16[48,768]{1,0:T(8,128)(2,1)S(1)}, u32[]{:S(2)}, u32[]{:S(2)}) collective-permute-start(bf16[48,768]{1,0:T(8,128)(2,1)S(1)} %get-tuple-element.29), channel_id=1, source_target_pairs={{0,2},{1,3},{2,0},{3,1},{4,6},{5,7},{6,4},{7,5},{8,10},{9,11},{10,... | collective-permute-start | bytes 221192 | tf_op jit(solution)/shard_map/ppermute | solution.py:318
  6.6 1.3 %collective-permute-start = (bf16[48,768]{1,0:T(8,128)(2,1)S(1)}, bf16[48,768]{1,0:T(8,128)(2,1)S(1)}, u32[]{:S(2)}, u32[]{:S(2)}) collective-permute-start(bf16[48,768]{1,0:T(8,128)(2,1)S(1)} %get-tuple-element.29), channel_id=1, source_target_pairs={{0,3},{1,2},{2,1},{3,0},{4,7},{5,6},{6,5},{7,4},{8,11},{9,10},{10,... | collective-permute-start | bytes 221192 | tf_op jit(solution)/shard_map/ppermute | solution.py:318
  7.9 0.0 copy-start.2
  7.9 0.2 collective-permute-start.2
  8.2 0.0 copy-done.3
  8.2 0.0 copy-done.4
  8.2 0.0 copy-done.5
  8.2 1.2 %hidden.1 = (bf16[48,1280]{1,0:T(8,128)(2,1)S(1)}, f32[48,512]{1,0:T(8,128)S(1)}, f32[48,512]{1,0:T(8,128)S(1)}, f32[48,512]{1,0:T(8,128)S(1)}) custom-call(bf16[48,3072]{1,0:T(8,128)(2,1)S(1)} %copy-done.5, bf16[3072,512]{1,0:T(8,128)(2,1)S(1)} %copy-done.3, bf16[3072,512]{1,0:T(8,128)(2,1)S(1)} %copy-done.4), custom_call_target="tpu_custom_call" | custom-call | flops 99999997952 | tf_op jit(solution)/shard_map/hidden/pallas_call | solution.py:50
  9.4 2.5 %collective-permute-start.3 = (bf16[48,1280]{1,0:T(8,128)(2,1)S(1)}, bf16[48,1280]{1,0:T(8,128)(2,1)S(1)}, u32[]{:S(2)}, u32[]{:S(2)}) collective-permute-start(bf16[48,1280]{1,0:T(8,128)(2,1)S(1)} %get-tuple-element.36), channel_id=1, source_target_pairs={{0,24},{4,28},{8,16},{12,20},{16,8},{20,12},{24,0},{28,4},{1,25},{... | collective-permute-start | bytes 368648 | tf_op jit(solution)/shard_map/ppermute | solution.py:318
  11.9 1.3 %collective-permute-done.2.refs_3_ = bf16[48,768]{1,0:T(8,128)(2,1)S(1)} collective-permute-done((bf16[48,768]{1,0:T(8,128)(2,1)S(1)}, bf16[48,768]{1,0:T(8,128)(2,1)S(1)}, u32[]{:S(2)}, u32[]{:S(2)}) %collective-permute-start.2) | collective-permute-done | bytes 73760 | tf_op jit(solution)/shard_map/ppermute | solution.py:318
  13.2 0.0 collective-permute-done.1.refs_2_
  13.2 0.0 collective-permute-done.refs_1_
  13.2 0.0 copy-done.2
  13.2 1.4 %project.1 = (bf16[48,3072]{1,0:T(8,128)(2,1)S(1)}, bf16[48,3072]{1,0:T(8,128)(2,1)S(1)}, bf16[48,3072]{1,0:T(8,128)(2,1)S(1)}, bf16[48,1792]{1,0:T(8,128)(2,1)S...) custom-call(bf16[48,768]{1,0:T(8,128)(2,1)S(1)} %get-tuple-element.28.refs_0_, ...), custom_call_target="tpu_custom_call" | custom-call | flops 99999997952 | tf_op jit(solution)/shard_map/project/pallas_call | solution.py:50
  14.7 2.7 %collective-permute-start.9 = (bf16[48,1792]{1,0:T(8,128)(2,1)S(1)}, bf16[48,1792]{1,0:T(8,128)(2,1)S(1)}, u32[]{:S(2)}, u32[]{:S(2)}) collective-permute-start(bf16[48,1792]{1,0:T(8,128)(2,1)S(1)} %get-tuple-element.45), channel_id=1, source_target_pairs={{0,24},{4,28},{8,16},{12,20},{16,8},{20,12},{24,0},{28,4},{1,25},{... | collective-permute-start | bytes 516104 | tf_op jit(solution)/shard_map/ppermute | solution.py:318
  17.3 0.5 %collective-permute-start.7 = (bf16[48,3072]{1,0:T(8,128)(2,1)S(1)}, bf16[48,3072]{1,0:T(8,128)(2,1)S(1)}, u32[]{:S(2)}, u32[]{:S(2)}) collective-permute-start(bf16[48,3072]{1,0:T(8,128)(2,1)S(1)} %get-tuple-element.43), channel_id=1, source_target_pairs={{0,8},{4,12},{8,0},{12,4},{16,24},{20,28},{24,16},{28,20},{1,9},{5... | collective-permute-start | bytes 884744 | tf_op jit(solution)/shard_map/ppermute | solution.py:318
  17.9 0.3 collective-permute-start.8
  18.2 0.0 collective-permute-done.3.refs_0_.refs_3_
  18.2 2.6 %input.1 = (bf16[24,1664]{1,0:T(8,128)(2,1)S(1)}, bf16[24,1664]{1,0:T(8,128)(2,1)S(1)}, bf16[24,1664]{1,0:T(8,128)(2,1)S(1)}, bf16[24,1664]{1,0:T(8,128)(2,1)S(1)}) custom-call(bf16[48,512]{1,0:T(8,128)(2,1)S(1)} %get-tuple-element.33.da, bf16[48,512]{1,0:T(8,128)(2,1)S(1)} %get-tuple-element.34.db, bf16[48,128]{1,0:T(8,128)(2,1)S(1)} %get-tuple-element.35.gate, ...), custom_call_target="tpu_custom_call" | custom-call | flops 99999997952 | tf_op jit(solution)/shard_map/input/pallas_call | solution.py:50
  20.8 3.4 %collective-permute-start.4 = (bf16[24,1664]{1,0:T(8,128)(2,1)S(1)}, bf16[24,1664]{1,0:T(8,128)(2,1)S(1)}, u32[]{:S(2)}, u32[]{:S(2)}) collective-permute-start(bf16[24,1664]{1,0:T(8,128)(2,1)S(1)} %get-tuple-element.38), channel_id=1, source_target_pairs={{0,3},{1,2},{2,1},{3,0},{4,7},{5,6},{6,5},{7,4},{8,11},{9,10},{10,... | collective-permute-start | bytes 239624 | tf_op jit(solution)/shard_map/ppermute | solution.py:318
  24.1 0.3 collective-permute-start.5
  24.5 0.0 collective-permute-done.9.refs_4_
  24.5 1.4 %collective-permute-start.6 = (bf16[24,1664]{1,0:T(8,128)(2,1)S(1)}, bf16[24,1664]{1,0:T(8,128)(2,1)S(1)}, u32[]{:S(2)}, u32[]{:S(2)}) collective-permute-start(bf16[24,1664]{1,0:T(8,128)(2,1)S(1)} %get-tuple-element.40), channel_id=1, source_target_pairs={{0,2},{1,3},{2,0},{3,1},{4,6},{5,7},{6,4},{7,5},{8,10},{9,11},{10,... | collective-permute-start | bytes 239624 | tf_op jit(solution)/shard_map/ppermute | solution.py:318
  25.9 1.1 %collective-permute-done.7.refs_1_ = bf16[48,3072]{1,0:T(8,128)(2,1)S(1)} collective-permute-done((bf16[48,3072]{1,0:T(8,128)(2,1)S(1)}, bf16[48,3072]{1,0:T(8,128)(2,1)S(1)}, u32[]{:S(2)}, u32[]{:S(2)}) %collective-permute-start.7) | collective-permute-done | bytes 294944 | tf_op jit(solution)/shard_map/ppermute | solution.py:318
  27.0 0.0 collective-permute-done.8.refs_2_
  27.0 0.1 share.1
  27.1 0.0 copy-start
  27.1 0.0 copy-start.1
  27.1 0.1 collective-permute-start.10
  27.2 0.5 %weight.1.refs_7_ = f32[3,384,512]{2,1,0:T(8,128)S(1)} custom-call(bf16[48,3072]{1,0:T(8,128)(2,1)S(1)} %get-tuple-element.42.refs_0_, bf16[48,3072]{1,0:T(8,128)(2,1)S(1)} %collective-permute-done.7.refs_1_, bf16[48,3072]{1,0:T(8,128)(2,1)S(1)} %collective-permute-done.8.refs_2_, bf16[48,1280]{1,0:T(8,128)(2,1)S(1)} %collective-permute-done.3.refs_0_.refs_3_, ...), custom_call_target="tpu_custom_call" | custom-call | flops 99999997952 | tf_op jit(solution)/shard_map/weight/pallas_call | solution.py:50
  27.7 0.0 collective-permute-done.4.refs_1_
  27.7 2.5 %collective-permute-done.5.refs_2_ = bf16[24,1664]{1,0:T(8,128)(2,1)S(1)} collective-permute-done((bf16[24,1664]{1,0:T(8,128)(2,1)S(1)}, bf16[24,1664]{1,0:T(8,128)(2,1)S(1)}, u32[]{:S(2)}, u32[]{:S(2)}) %collective-permute-start.5) | collective-permute-done | bytes 79904 | tf_op jit(solution)/shard_map/ppermute | solution.py:318
  30.2 0.0 collective-permute-done.6.refs_3_
  30.2 0.0 collective-permute-done.10.refs_8_
  30.2 0.0 copy-done
  30.2 0.0 copy-done.1
  30.2 2.3 %finish.1 = (bf16[256,3072]{1,0:T(8,128)(2,1)}, f32[2,256]{1,0:T(2,128)}, f32[3,384,512]{2,1,0:T(8,128)}) custom-call(bf16[24,1664]{1,0:T(8,128)(2,1)S(1)} %get-tuple-element.37.refs_0_, bf16[24,1664]{1,0:T(8,128)(2,1)S(1)} %collective-permute-done.4.refs_1_, bf16[24,1664]{1,0:T(8,128)(2,1)S(1)} %collective-permute-done.5.refs_2_, ...), custom_call_target="tpu_custom_call" | custom-call | flops 99999997952 | tf_op jit(solution)/shard_map/finish/pallas_call | solution.py:50
  (1 shorter events, 0.0 us)
Async XLA Ops:
  2.4 5.7 %copy-start.3 = (bf16[3072,512]{1,0:T(8,128)(2,1)S(1)}, bf16[3072,512]{1,0:T(8,128)(2,1)}, u32[]{:S(2)}) copy-start(bf16[3072,512]{1,0:T(8,128)(2,1)} %w_gate.3) | copy-start | bytes 9437188
  2.5 5.7 %copy-start.4 = (bf16[3072,512]{1,0:T(8,128)(2,1)S(1)}, bf16[3072,512]{1,0:T(8,128)(2,1)}, u32[]{:S(2)}) copy-start(bf16[3072,512]{1,0:T(8,128)(2,1)} %w_up.3) | copy-start | bytes 9437188
  2.5 5.7 %copy-start.5 = (bf16[48,3072]{1,0:T(8,128)(2,1)S(1)}, bf16[48,3072]{1,0:T(8,128)(2,1)}, u32[]{:S(2)}) copy-start(bf16[48,3072]{1,0:T(8,128)(2,1)} %refs_8_.1) | copy-start | bytes 884740
  2.5 10.7 %collective-permute-start.1 = (bf16[48,768]{1,0:T(8,128)(2,1)S(1)}, bf16[48,768]{1,0:T(8,128)(2,1)S(1)}, u32[]{:S(2)}, u32[]{:S(2)}) collective-permute-start(bf16[48,768]{1,0:T(8,128)(2,1)S(1)} %get-tuple-element.29), channel_id=1, source_target_pairs={{0,2},{1,3},{2,0},{3,1},{4,6},{5,7},{6,4},{7,5},{8,10},{9,11},{10,... | collective-permute-start | bytes 221192 | tf_op jit(solution)/shard_map/ppermute | solution.py:318
  6.6 6.6 %collective-permute-start = (bf16[48,768]{1,0:T(8,128)(2,1)S(1)}, bf16[48,768]{1,0:T(8,128)(2,1)S(1)}, u32[]{:S(2)}, u32[]{:S(2)}) collective-permute-start(bf16[48,768]{1,0:T(8,128)(2,1)S(1)} %get-tuple-element.29), channel_id=1, source_target_pairs={{0,3},{1,2},{2,1},{3,0},{4,7},{5,6},{6,5},{7,4},{8,11},{9,10},{10,... | collective-permute-start | bytes 221192 | tf_op jit(solution)/shard_map/ppermute | solution.py:318
  7.9 5.3 %copy-start.2 = (bf16[512,3072]{1,0:T(8,128)(2,1)S(1)}, bf16[512,3072]{1,0:T(8,128)(2,1)}, u32[]{:S(2)}) copy-start(bf16[512,3072]{1,0:T(8,128)(2,1)} %refs_4_.1) | copy-start | bytes 9437188
  7.9 5.3 %collective-permute-start.2 = (bf16[48,768]{1,0:T(8,128)(2,1)S(1)}, bf16[48,768]{1,0:T(8,128)(2,1)S(1)}, u32[]{:S(2)}, u32[]{:S(2)}) collective-permute-start(bf16[48,768]{1,0:T(8,128)(2,1)S(1)} %get-tuple-element.28.refs_0_), channel_id=1, source_target_pairs={{0,1},{1,0},{2,3},{3,2},{4,5},{5,4},{6,7},{7,6},{8,9},{9,8},{10,11... | collective-permute-start | bytes 221192 | tf_op jit(solution)/shard_map/ppermute | solution.py:318
  9.4 8.8 %collective-permute-start.3 = (bf16[48,1280]{1,0:T(8,128)(2,1)S(1)}, bf16[48,1280]{1,0:T(8,128)(2,1)S(1)}, u32[]{:S(2)}, u32[]{:S(2)}) collective-permute-start(bf16[48,1280]{1,0:T(8,128)(2,1)S(1)} %get-tuple-element.36), channel_id=1, source_target_pairs={{0,24},{4,28},{8,16},{12,20},{16,8},{20,12},{24,0},{28,4},{1,25},{... | collective-permute-start | bytes 368648 | tf_op jit(solution)/shard_map/ppermute | solution.py:318
  14.7 9.8 %collective-permute-start.9 = (bf16[48,1792]{1,0:T(8,128)(2,1)S(1)}, bf16[48,1792]{1,0:T(8,128)(2,1)S(1)}, u32[]{:S(2)}, u32[]{:S(2)}) collective-permute-start(bf16[48,1792]{1,0:T(8,128)(2,1)S(1)} %get-tuple-element.45), channel_id=1, source_target_pairs={{0,24},{4,28},{8,16},{12,20},{16,8},{20,12},{24,0},{28,4},{1,25},{... | collective-permute-start | bytes 516104 | tf_op jit(solution)/shard_map/ppermute | solution.py:318
  17.3 9.7 %collective-permute-start.7 = (bf16[48,3072]{1,0:T(8,128)(2,1)S(1)}, bf16[48,3072]{1,0:T(8,128)(2,1)S(1)}, u32[]{:S(2)}, u32[]{:S(2)}) collective-permute-start(bf16[48,3072]{1,0:T(8,128)(2,1)S(1)} %get-tuple-element.43), channel_id=1, source_target_pairs={{0,8},{4,12},{8,0},{12,4},{16,24},{20,28},{24,16},{28,20},{1,9},{5... | collective-permute-start | bytes 884744 | tf_op jit(solution)/shard_map/ppermute | solution.py:318
  17.9 9.1 %collective-permute-start.8 = (bf16[48,3072]{1,0:T(8,128)(2,1)S(1)}, bf16[48,3072]{1,0:T(8,128)(2,1)S(1)}, u32[]{:S(2)}, u32[]{:S(2)}) collective-permute-start(bf16[48,3072]{1,0:T(8,128)(2,1)S(1)} %get-tuple-element.44), channel_id=1, source_target_pairs={{0,16},{4,20},{8,24},{12,28},{16,0},{20,4},{24,8},{28,12},{1,17},{... | collective-permute-start | bytes 884744 | tf_op jit(solution)/shard_map/ppermute | solution.py:318
  20.8 6.9 %collective-permute-start.4 = (bf16[24,1664]{1,0:T(8,128)(2,1)S(1)}, bf16[24,1664]{1,0:T(8,128)(2,1)S(1)}, u32[]{:S(2)}, u32[]{:S(2)}) collective-permute-start(bf16[24,1664]{1,0:T(8,128)(2,1)S(1)} %get-tuple-element.38), channel_id=1, source_target_pairs={{0,3},{1,2},{2,1},{3,0},{4,7},{5,6},{6,5},{7,4},{8,11},{9,10},{10,... | collective-permute-start | bytes 239624 | tf_op jit(solution)/shard_map/ppermute | solution.py:318
  24.1 6.0 %collective-permute-start.5 = (bf16[24,1664]{1,0:T(8,128)(2,1)S(1)}, bf16[24,1664]{1,0:T(8,128)(2,1)S(1)}, u32[]{:S(2)}, u32[]{:S(2)}) collective-permute-start(bf16[24,1664]{1,0:T(8,128)(2,1)S(1)} %get-tuple-element.39), channel_id=1, source_target_pairs={{0,1},{1,0},{2,3},{3,2},{4,5},{5,4},{6,7},{7,6},{8,9},{9,8},{10,11... | collective-permute-start | bytes 239624 | tf_op jit(solution)/shard_map/ppermute | solution.py:318
  24.5 5.7 %collective-permute-start.6 = (bf16[24,1664]{1,0:T(8,128)(2,1)S(1)}, bf16[24,1664]{1,0:T(8,128)(2,1)S(1)}, u32[]{:S(2)}, u32[]{:S(2)}) collective-permute-start(bf16[24,1664]{1,0:T(8,128)(2,1)S(1)} %get-tuple-element.40), channel_id=1, source_target_pairs={{0,2},{1,3},{2,0},{3,1},{4,6},{5,7},{6,4},{7,5},{8,10},{9,11},{10,... | collective-permute-start | bytes 239624 | tf_op jit(solution)/shard_map/ppermute | solution.py:318
  27.1 3.1 %copy-start = (s32[256,2]{0,1:T(2,128)S(1)}, s32[256,2]{0,1:T(2,128)}, u32[]{:S(2)}) copy-start(s32[256,2]{0,1:T(2,128)} %param.8) | copy-start | bytes 6148
  27.1 3.1 %copy-start.1 = (s32[256,2]{0,1:T(2,128)S(1)}, s32[256,2]{0,1:T(2,128)}, u32[]{:S(2)}) copy-start(s32[256,2]{0,1:T(2,128)} %param.9) | copy-start | bytes 6148
  27.1 3.1 %collective-permute-start.10 = (bf16[192,2304]{1,0:T(8,128)(2,1)S(1)}, bf16[192,2304]{1,0:T(8,128)(2,1)S(1)}, u32[]{:S(2)}, u32[]{:S(2)}) collective-permute-start(bf16[192,2304]{1,0:T(8,128)(2,1)S(1)} %share.1), channel_id=1, source_target_pairs={{0,4},{4,0},{8,12},{12,8},{16,20},{20,16},{24,28},{28,24},{1,5},{5... | collective-permute-start | bytes 2654216 | tf_op jit(solution)/shard_map/ppermute | solution.py:318

commit v8 on v7

--- a/solution.py
+++ b/solution.py
@@ -12,10 +12,11 @@
 BACK_CUTS = 2
 GATE_LANES = 128
 W_CHUNKS = 4
+TURNED = 2
 LAST = 3
-HEAVY = 10**11
+HEAVY = 10**10
 DISPATCH_ORDER = (0, 3, 2, 1)
-RETURN_ORDER = (0, 3, 1, 2)
+RETURN_ORDER = (0, 3, 2, 1)
 PAIRED = 8
 F32 = jnp.float32
 BF16 = jnp.bfloat16
@@ -127,15 +128,26 @@
     b = nn(inputs[...], w_up[...])
     s = jax.nn.sigmoid(a)
     u = a * s
+    v = b * s * (1.0 + a * (1.0 - s))
     u_out[...] = u
-    v_out[...] = b * s * (1.0 + a * (1.0 - s))
+    v_out[...] = v
     h = u * b
     h_out[...] = h
     pair = 2 * (inputs.shape[1] // n_dp)
     for out in ahead:
         start = pl.multiple_of(((lax.axis_index("dp") // 2) ^ LAST) * pair, 128)
         out[:, 0:pair] = inputs[:, pl.ds(start, pair)]
-        out[:, pair:] = h.astype(BF16)
+        for n, value in enumerate((h, u, v)):
+            hidden = value.shape[1]
+            out[:, pair + n * hidden : pair + (n + 1) * hidden] = value.astype(BF16)
+
+
+def turn_kernel(*refs):
+    for ref, out in zip(refs[: len(refs) // 2], refs[len(refs) // 2 :]):
+        step = ref.shape[0] // W_CHUNKS
+        for k in range(W_CHUNKS):
+            part = slice(k * step, (k + 1) * step)
+            out[:, part] = ref[part, :].T
 
 
 def pass_kernel(*refs):
@@ -145,7 +157,7 @@
 def project_kernel(group, capacity, n_dp, *refs):
     received = restore(refs[:group], DISPATCH_ORDER)
     w_down, u_in, v_in, h_in, inputs = refs[group : group + 5]
-    sends = refs[group + 5 : -4]
+    sends = refs[group + 5 + TURNED : -4]
     da_out, db_out, gate_out, rows_buf = refs[-4:]
     rows, hidden = u_in.shape
     width = w_down.shape[1]
@@ -187,14 +199,17 @@
             send[:, pair : pair + hidden] = h
             base = pair + hidden
         send[:, base : base + pair] = rows_buf[:, pl.ds(start, pair)]
-        send[:, base + pair : base + pair + hidden] = da
-        send[:, base + pair + hidden :] = db
+        if m < LAST:
+            send[:, base + pair : base + pair + hidden] = da
+            send[:, base + pair + hidden :] = db
+        else:
+            send[:, pair:] = projected.astype(BF16)
 
 
 def input_kernel(group, capacity, da, db, gate, w_gate, w_up, *refs):
     outs = refs[-group:]
     rows = da.shape[0]
-    width = w_gate.shape[0]
+    width = max(w_gate.shape)
     span = width // BACK_CUTS
     step = width // W_CHUNKS
     per = W_CHUNKS // BACK_CUTS
@@ -210,8 +225,12 @@
     ]
     total = [jnp.zeros((group * packed, step), F32) for _ in range(per)]
     for k in range(W_CHUNKS):
-        part = nt(da[...], w_gate[k * step : (k + 1) * step, :])
-        part += nt(db[...], w_up[k * step : (k + 1) * step, :])
+        piece = slice(k * step, (k + 1) * step)
+        part = nn(da[...], w_gate[:, piece])
+        if TURNED > 1:
+            part += nn(db[...], w_up[:, piece])
+        else:
+            part += nt(db[...], w_up[piece, :])
         total[k % per] += nn(selects[k // per], part.astype(BF16))
     gates = nn(selects[0], gate[...])
     for n, out in enumerate(outs):
@@ -220,39 +239,47 @@
         out[:, span:] = gates[n * packed : (n + 1) * packed].astype(BF16)
 
 
-def halves(columns, refs):
-    first = [(ref, 0) for ref in refs[: LAST + 1]]
-    second = [(ref, columns) for ref in refs[:LAST]] + [(refs[-1], 0)]
-    return first, second
+def rows_of(block, hidden, core, refs):
+    start = pl.multiple_of(core * block, 128)
+    pair = 2 * block
+    first, last = refs[0], refs[-1]
+    base = pair + hidden if len(refs) == 1 else 0
+    grads = last[:, pl.ds(pl.multiple_of(base + start, 128), block)]
+    base += pair
+    da = last[:, base : base + hidden]
+    if len(refs) == 1:
+        db = last[:, base + hidden : base + 2 * hidden]
+    else:
+        projected = da.astype(F32)
+        u, v = (first[:, pair + n * hidden : pair + (n + 1) * hidden] for n in (1, 2))
+        da = (projected * v.astype(F32)).astype(BF16)
+        db = (projected * u.astype(F32)).astype(BF16)
+    return first[:, pl.ds(start, block)], first[:, pair : pair + hidden], grads, da, db
+
+
+def chips_of(refs):
+    return [refs[n : n + 1] for n in range(LAST)] + [refs[LAST:]]
 
 
 def share_kernel(block, hidden, *refs):
-    buffers, out = refs[:-1], refs[-1]
-    rows = buffers[0].shape[0]
-    start = (1 - lax.axis_index("dp") % 2) * block
-    first, second = halves(2 * block + hidden, buffers)
-    middle = block + hidden
-    for m in range(LAST + 1):
-        part = slice(m * rows, (m + 1) * rows)
-        for (ref, at), to, wide in ((first[m], 0, middle), (second[m], middle, middle + hidden)):
-            out[part, to : to + block] = ref[:, pl.ds(pl.multiple_of(at + start, 128), block)]
-            at += 2 * block
-            out[part, to + block : to + wide] = ref[:, at : at + wide - block]
+    out = refs[-1]
+    core = 1 - lax.axis_index("dp") % 2
+    for m, chip in enumerate(chips_of(refs[:-1])):
+        rows = chip[0].shape[0]
+        at = 0
+        for value in rows_of(block, hidden, core, chip):
+            out[m * rows : (m + 1) * rows, at : at + value.shape[1]] = value
+            at += value.shape[1]
 
 
 def weight_kernel(block, hidden, *refs):
-    buffers, out = refs[:-1], refs[-1]
-    start = (lax.axis_index("dp") % 2) * block
-    first, second = halves(2 * block + hidden, buffers)
-
-    def gather(side, skip, wide):
-        parts = [ref[:, pl.ds(pl.multiple_of(at + skip, 128), wide)] for ref, at in side]
-        return jnp.concatenate(parts, axis=0)
-
-    inputs, grads = gather(first, start, block), gather(second, start, block)
-    out[0] = tn(inputs, gather(second, 2 * block, hidden))
-    out[1] = tn(inputs, gather(second, 2 * block + hidden, hidden))
-    out[2] = tn(grads, gather(first, 2 * block, hidden))
+    out = refs[-1]
+    core = lax.axis_index("dp") % 2
+    chips = [rows_of(block, hidden, core, chip) for chip in chips_of(refs[:-1])]
+    inputs, h, grads, da, db = (jnp.concatenate(values, axis=0) for values in zip(*chips))
+    out[0] = tn(inputs, da)
+    out[1] = tn(inputs, db)
+    out[2] = tn(grads, h)
 
 
 def finish_weights(hidden, partial, shared, out_hbm, buf, sems):
@@ -370,7 +397,7 @@
     for mask in far_first(group):
         received[mask] = swap(own if mask < shards else other, "expert", group, mask)
     part = shape((rows, hidden), F32)
-    ahead = shape((rows, 2 * block + hidden), BF16)
+    ahead = shape((rows, 2 * block + 3 * hidden), BF16)
     *ahead, u, v, h = call(
         functools.partial(hidden_kernel, n_dp),
         (ahead,) * paired + (part,) * 3,
@@ -379,17 +406,24 @@
         flops=HEAVY,
         name="hidden",
     )
+    turned = call(
+        turn_kernel,
+        (shape((hidden, width), BF16),) * TURNED,
+        (w_gate, w_up)[:TURNED],
+        [VMEM] * TURNED,
+        flops=HEAVY,
+        name="turn",
+    )
     half = shape((rows, hidden), BF16)
-    late = shape((rows, 2 * block + 2 * hidden), BF16)
+    late = shape((rows, 2 * block + hidden), BF16)
     full = shape((rows, 4 * block + 3 * hidden), BF16)
     outward = (full,) * LAST + (late,) if paired else (shape((rows, width), BF16), half)
     *sends, da, db, gate = call(
         functools.partial(project_kernel, group, capacity, n_dp),
         outward + (half, half, shape((rows, GATE_LANES), BF16)),
-        (*arrange(received, DISPATCH_ORDER), w_down, u, v, h, saved_inputs),
-        [VMEM] * (group + 5),
+        (*arrange(received, DISPATCH_ORDER), w_down, u, v, h, saved_inputs, *turned),
+        [VMEM] * (group + 5) + [UNUSED] * TURNED,
         [pltpu.VMEM((rows, width), BF16)],
-        flops=HEAVY,
         name="project",
     )
     ahead = [swap(array, "dp", n_dp, 2 * LAST) for array in ahead]
@@ -397,7 +431,7 @@
     returns = call(
         functools.partial(input_kernel, group, capacity),
         (back,) * group,
-        (da, db, gate, w_gate, w_up, *ahead),
+        (da, db, gate, *turned, *(w_gate, w_up)[TURNED:], *ahead),
         [VMEM] * 5 + [UNUSED] * len(ahead),
         flops=HEAVY,
         name="input",

time: 32.6 us -> 32.3 us (level)
  Pallas kernels: 9.87 us -> 10.7 us
  starting transfers between devices: 16.9 us -> 16.2 us
  waiting for transfers between devices: 4.92 us -> 4.32 us
    pallas_call x8 -> x9, Pallas kernels: 9.87 us -> 10.7 us  [call(): pl.pallas_call(kernel, out_shape=outs, in_specs=specs, out_specs=out_spec...]
    ppermute x11, starting transfers between devices: 16.9 us -> 16.2 us  [swap(): return lax.ppermute(array, axis, [(n, n ^ mask) for n in range(size)])]
    ppermute x11, waiting for transfers between devices: 4.92 us -> 4.32 us  [swap(): return lax.ppermute(array, axis, [(n, n ^ mask) for n in range(size)])]
  transfers between devices with their start and end apart: 11 -> 11, of which waited for: 3 -> 4; matrix products, arithmetic and copies ran while one was open for 0% -> 0% of each run, Pallas kernels for 18% -> 21%
where the time goes in v8:
time: 32.3 us; the launch traced here: 32.1 us
  starting transfers between devices  16.2 us (50%)
  Pallas kernels  10.7 us (33%)
  waiting for transfers between devices  4.32 us (13%)
  between operations  0.78 us (2%)
    ppermute x11, starting transfers between devices, swap(): return lax.ppermute(array, axis, [(n, n ^ mask) for n in range(size)])  16.2 us
    pallas_call x9, Pallas kernels, call(): pl.pallas_call(kernel, out_shape=outs, in_specs=specs, out_specs=out_spec...  10.7 us
    ppermute x11, waiting for transfers between devices, swap(): return lax.ppermute(array, axis, [(n, n ^ mask) for n in range(size)])  4.32 us
  transfers between devices with their start and end apart: 11, of which 4 were waited for; matrix products, arithmetic and copies ran while one was open for 0% of the time, Pallas kernels for 21%

profile of v8, /device:TPU:0, one launch (start us, length us, event | category | flops | bytes accessed | tf_op | source)
XLA Modules:
  0.0 32.1 jit_solution(6588007356520506006)
XLA Ops:
  0.6 1.8 %pick.1 = (bf16[48,768]{1,0:T(8,128)(2,1)S(1)}, bf16[48,768]{1,0:T(8,128)(2,1)S(1)}, s32[8,256]{1,0:T(8,128)S(1)}) custom-call(s32[2,256]{1,0:T(2,128)} %bitcast.4, s32[2,256]{1,0:T(2,128)} %bitcast.6, bf16[256,3072]{1,0:T(8,128)(2,1)} %grad_hbm.1), custom_call_target="tpu_custom_call" | custom-call | tf_op jit(solution)/shard_map/pick/pallas_call | solution.py:51
  2.4 0.0 copy-start.1
  2.5 0.0 copy-start.4
  2.5 0.0 copy-start.5
  2.5 4.1 %collective-permute-start.1 = (bf16[48,768]{1,0:T(8,128)(2,1)S(1)}, bf16[48,768]{1,0:T(8,128)(2,1)S(1)}, u32[]{:S(2)}, u32[]{:S(2)}) collective-permute-start(bf16[48,768]{1,0:T(8,128)(2,1)S(1)} %get-tuple-element.31), channel_id=1, source_target_pairs={{0,2},{1,3},{2,0},{3,1},{4,6},{5,7},{6,4},{7,5},{8,10},{9,11},{10,... | collective-permute-start | bytes 221192 | tf_op jit(solution)/shard_map/ppermute | solution.py:345
  6.6 1.3 %collective-permute-start = (bf16[48,768]{1,0:T(8,128)(2,1)S(1)}, bf16[48,768]{1,0:T(8,128)(2,1)S(1)}, u32[]{:S(2)}, u32[]{:S(2)}) collective-permute-start(bf16[48,768]{1,0:T(8,128)(2,1)S(1)} %get-tuple-element.31), channel_id=1, source_target_pairs={{0,3},{1,2},{2,1},{3,0},{4,7},{5,6},{6,5},{7,4},{8,11},{9,10},{10,... | collective-permute-start | bytes 221192 | tf_op jit(solution)/shard_map/ppermute | solution.py:345
  7.9 0.2 collective-permute-start.2
  8.2 0.0 copy-done.1
  8.2 0.0 copy-done.4
  8.2 0.0 copy-done.5
  8.2 1.2 %hidden.1 = (bf16[48,2304]{1,0:T(8,128)(2,1)S(1)}, f32[48,512]{1,0:T(8,128)S(1)}, f32[48,512]{1,0:T(8,128)S(1)}, f32[48,512]{1,0:T(8,128)S(1)}) custom-call(bf16[48,3072]{1,0:T(8,128)(2,1)S(1)} %copy-done.1, bf16[3072,512]{1,0:T(8,128)(2,1)S(1)} %copy-done.4, bf16[3072,512]{1,0:T(8,128)(2,1)S(1)} %copy-done.5), custom_call_target="tpu_custom_call" | custom-call | flops 10000000000 | tf_op jit(solution)/shard_map/hidden/pallas_call | solution.py:51
  9.4 0.0 copy-start
  9.4 2.5 %collective-permute-start.3 = (bf16[48,2304]{1,0:T(8,128)(2,1)S(1)}, bf16[48,2304]{1,0:T(8,128)(2,1)S(1)}, u32[]{:S(2)}, u32[]{:S(2)}) collective-permute-start(bf16[48,2304]{1,0:T(8,128)(2,1)S(1)} %get-tuple-element.40), channel_id=1, source_target_pairs={{0,24},{4,28},{8,16},{12,20},{16,8},{20,12},{24,0},{28,4},{1,25},{... | collective-permute-start | bytes 663560 | tf_op jit(solution)/shard_map/ppermute | solution.py:345
  11.9 1.8 %turn.1 = (bf16[512,3072]{1,0:T(8,128)(2,1)S(1)}, bf16[512,3072]{1,0:T(8,128)(2,1)S(1)}) custom-call(bf16[3072,512]{1,0:T(8,128)(2,1)S(1)} %copy-done.4, bf16[3072,512]{1,0:T(8,128)(2,1)S(1)} %copy-done.5), custom_call_target="tpu_custom_call" | custom-call | flops 10000000000 | tf_op jit(solution)/shard_map/turn/pallas_call | solution.py:51
  13.7 0.0 collective-permute-done.2.refs_3_
  13.7 0.0 collective-permute-done.1.refs_2_
  13.7 0.0 collective-permute-done.refs_1_
  13.8 0.0 copy-done
  13.8 1.4 %project.1 = (bf16[48,3072]{1,0:T(8,128)(2,1)S(1)}, bf16[48,3072]{1,0:T(8,128)(2,1)S(1)}, bf16[48,3072]{1,0:T(8,128)(2,1)S(1)}, bf16[48,1280]{1,0:T(8,128)(2,1)S...) custom-call(bf16[48,768]{1,0:T(8,128)(2,1)S(1)} %get-tuple-element.30.refs_0_, ...), custom_call_target="tpu_custom_call" | custom-call | tf_op jit(solution)/shard_map/project/pallas_call | solution.py:51
  15.2 2.2 %collective-permute-start.9 = (bf16[48,1280]{1,0:T(8,128)(2,1)S(1)}, bf16[48,1280]{1,0:T(8,128)(2,1)S(1)}, u32[]{:S(2)}, u32[]{:S(2)}) collective-permute-start(bf16[48,1280]{1,0:T(8,128)(2,1)S(1)} %get-tuple-element.49), channel_id=1, source_target_pairs={{0,24},{4,28},{8,16},{12,20},{16,8},{20,12},{24,0},{28,4},{1,25},{... | collective-permute-start | bytes 368648 | tf_op jit(solution)/shard_map/ppermute | solution.py:345
  17.3 0.5 %collective-permute-start.7 = (bf16[48,3072]{1,0:T(8,128)(2,1)S(1)}, bf16[48,3072]{1,0:T(8,128)(2,1)S(1)}, u32[]{:S(2)}, u32[]{:S(2)}) collective-permute-start(bf16[48,3072]{1,0:T(8,128)(2,1)S(1)} %get-tuple-element.47), channel_id=1, source_target_pairs={{0,8},{4,12},{8,0},{12,4},{16,24},{20,28},{24,16},{28,20},{1,9},{5... | collective-permute-start | bytes 884744 | tf_op jit(solution)/shard_map/ppermute | solution.py:345
  17.9 0.8 %collective-permute-start.8 = (bf16[48,3072]{1,0:T(8,128)(2,1)S(1)}, bf16[48,3072]{1,0:T(8,128)(2,1)S(1)}, u32[]{:S(2)}, u32[]{:S(2)}) collective-permute-start(bf16[48,3072]{1,0:T(8,128)(2,1)S(1)} %get-tuple-element.48), channel_id=1, source_target_pairs={{0,16},{4,20},{8,24},{12,28},{16,0},{20,4},{24,8},{28,12},{1,17},{... | collective-permute-start | bytes 884744 | tf_op jit(solution)/shard_map/ppermute | solution.py:345
  18.7 0.0 collective-permute-done.3.refs_0_.refs_3_
  18.7 1.6 %input.1 = (bf16[24,1664]{1,0:T(8,128)(2,1)S(1)}, bf16[24,1664]{1,0:T(8,128)(2,1)S(1)}, bf16[24,1664]{1,0:T(8,128)(2,1)S(1)}, bf16[24,1664]{1,0:T(8,128)(2,1)S(1)}) custom-call(bf16[48,512]{1,0:T(8,128)(2,1)S(1)} %get-tuple-element.37.da, bf16[48,512]{1,0:T(8,128)(2,1)S(1)} %get-tuple-element.38.db, bf16[48,128]{1,0:T(8,128)(2,1)S(1)} %get-tuple-element.39.gate, ...), custom_call_target="tpu_custom_call" | custom-call | flops 10000000000 | tf_op jit(solution)/shard_map/input/pallas_call | solution.py:51
  20.3 3.0 %collective-permute-start.4 = (bf16[24,1664]{1,0:T(8,128)(2,1)S(1)}, bf16[24,1664]{1,0:T(8,128)(2,1)S(1)}, u32[]{:S(2)}, u32[]{:S(2)}) collective-permute-start(bf16[24,1664]{1,0:T(8,128)(2,1)S(1)} %get-tuple-element.42), channel_id=1, source_target_pairs={{0,3},{1,2},{2,1},{3,0},{4,7},{5,6},{6,5},{7,4},{8,11},{9,10},{10,... | collective-permute-start | bytes 239624 | tf_op jit(solution)/shard_map/ppermute | solution.py:345
  23.3 0.3 %collective-permute-start.5 = (bf16[24,1664]{1,0:T(8,128)(2,1)S(1)}, bf16[24,1664]{1,0:T(8,128)(2,1)S(1)}, u32[]{:S(2)}, u32[]{:S(2)}) collective-permute-start(bf16[24,1664]{1,0:T(8,128)(2,1)S(1)} %get-tuple-element.43), channel_id=1, source_target_pairs={{0,2},{1,3},{2,0},{3,1},{4,6},{5,7},{6,4},{7,5},{8,10},{9,11},{10,... | collective-permute-start | bytes 239624 | tf_op jit(solution)/shard_map/ppermute | solution.py:345
  23.6 0.0 collective-permute-done.9.refs_4_
  23.6 1.1 %collective-permute-start.6 = (bf16[24,1664]{1,0:T(8,128)(2,1)S(1)}, bf16[24,1664]{1,0:T(8,128)(2,1)S(1)}, u32[]{:S(2)}, u32[]{:S(2)}) collective-permute-start(bf16[24,1664]{1,0:T(8,128)(2,1)S(1)} %get-tuple-element.44), channel_id=1, source_target_pairs={{0,1},{1,0},{2,3},{3,2},{4,5},{5,4},{6,7},{7,6},{8,9},{9,8},{10,11... | collective-permute-start | bytes 239624 | tf_op jit(solution)/shard_map/ppermute | solution.py:345
  24.8 1.2 %collective-permute-done.7.refs_1_ = bf16[48,3072]{1,0:T(8,128)(2,1)S(1)} collective-permute-done((bf16[48,3072]{1,0:T(8,128)(2,1)S(1)}, bf16[48,3072]{1,0:T(8,128)(2,1)S(1)}, u32[]{:S(2)}, u32[]{:S(2)}) %collective-permute-start.7) | collective-permute-done | bytes 294944 | tf_op jit(solution)/shard_map/ppermute | solution.py:345
  26.0 0.7 %collective-permute-done.8.refs_2_ = bf16[48,3072]{1,0:T(8,128)(2,1)S(1)} collective-permute-done((bf16[48,3072]{1,0:T(8,128)(2,1)S(1)}, bf16[48,3072]{1,0:T(8,128)(2,1)S(1)}, u32[]{:S(2)}, u32[]{:S(2)}) %collective-permute-start.8) | collective-permute-done | bytes 294944 | tf_op jit(solution)/shard_map/ppermute | solution.py:345
  26.7 0.1 share.1
  26.8 0.0 copy-start.2
  26.8 0.0 copy-start.3
  26.8 0.1 collective-permute-start.10
  26.9 0.5 %weight.1.refs_7_ = f32[3,384,512]{2,1,0:T(8,128)S(1)} custom-call(bf16[48,3072]{1,0:T(8,128)(2,1)S(1)} %get-tuple-element.46.refs_0_, bf16[48,3072]{1,0:T(8,128)(2,1)S(1)} %collective-permute-done.7.refs_1_, bf16[48,3072]{1,0:T(8,128)(2,1)S(1)} %collective-permute-done.8.refs_2_, bf16[48,2304]{1,0:T(8,128)(2,1)S(1)} %collective-permute-done.3.refs_0_.refs_3_, ...), custom_call_target="tpu_custom_call" | custom-call | flops 10000000000 | tf_op jit(solution)/shard_map/weight/pallas_call | solution.py:51
  27.4 0.1 collective-permute-done.4.refs_1_
  27.4 2.3 %collective-permute-done.5.refs_2_ = bf16[24,1664]{1,0:T(8,128)(2,1)S(1)} collective-permute-done((bf16[24,1664]{1,0:T(8,128)(2,1)S(1)}, bf16[24,1664]{1,0:T(8,128)(2,1)S(1)}, u32[]{:S(2)}, u32[]{:S(2)}) %collective-permute-start.5) | collective-permute-done | bytes 79904 | tf_op jit(solution)/shard_map/ppermute | solution.py:345
  29.8 0.0 collective-permute-done.6.refs_3_
  29.8 0.0 collective-permute-done.10.refs_8_
  29.8 0.0 copy-done.2
  29.8 0.0 copy-done.3
  29.8 2.3 %finish.1 = (bf16[256,3072]{1,0:T(8,128)(2,1)}, f32[2,256]{1,0:T(2,128)}, f32[3,384,512]{2,1,0:T(8,128)}) custom-call(bf16[24,1664]{1,0:T(8,128)(2,1)S(1)} %get-tuple-element.41.refs_0_, bf16[24,1664]{1,0:T(8,128)(2,1)S(1)} %collective-permute-done.4.refs_1_, bf16[24,1664]{1,0:T(8,128)(2,1)S(1)} %collective-permute-done.5.refs_2_, ...), custom_call_target="tpu_custom_call" | custom-call | flops 10000000000 | tf_op jit(solution)/shard_map/finish/pallas_call | solution.py:51
  (1 shorter events, 0.0 us)
Async XLA Ops:
  2.4 5.7 %copy-start.1 = (bf16[48,3072]{1,0:T(8,128)(2,1)S(1)}, bf16[48,3072]{1,0:T(8,128)(2,1)}, u32[]{:S(2)}) copy-start(bf16[48,3072]{1,0:T(8,128)(2,1)} %refs_8_.1) | copy-start | bytes 884740
  2.5 5.7 %copy-start.4 = (bf16[3072,512]{1,0:T(8,128)(2,1)S(1)}, bf16[3072,512]{1,0:T(8,128)(2,1)}, u32[]{:S(2)}) copy-start(bf16[3072,512]{1,0:T(8,128)(2,1)} %refs_0_.1) | copy-start | bytes 9437188
  2.5 5.7 %copy-start.5 = (bf16[3072,512]{1,0:T(8,128)(2,1)S(1)}, bf16[3072,512]{1,0:T(8,128)(2,1)}, u32[]{:S(2)}) copy-start(bf16[3072,512]{1,0:T(8,128)(2,1)} %refs_1_.1) | copy-start | bytes 9437188
  2.5 11.2 %collective-permute-start.1 = (bf16[48,768]{1,0:T(8,128)(2,1)S(1)}, bf16[48,768]{1,0:T(8,128)(2,1)S(1)}, u32[]{:S(2)}, u32[]{:S(2)}) collective-permute-start(bf16[48,768]{1,0:T(8,128)(2,1)S(1)} %get-tuple-element.31), channel_id=1, source_target_pairs={{0,2},{1,3},{2,0},{3,1},{4,6},{5,7},{6,4},{7,5},{8,10},{9,11},{10,... | collective-permute-start | bytes 221192 | tf_op jit(solution)/shard_map/ppermute | solution.py:345
  6.6 7.2 %collective-permute-start = (bf16[48,768]{1,0:T(8,128)(2,1)S(1)}, bf16[48,768]{1,0:T(8,128)(2,1)S(1)}, u32[]{:S(2)}, u32[]{:S(2)}) collective-permute-start(bf16[48,768]{1,0:T(8,128)(2,1)S(1)} %get-tuple-element.31), channel_id=1, source_target_pairs={{0,3},{1,2},{2,1},{3,0},{4,7},{5,6},{6,5},{7,4},{8,11},{9,10},{10,... | collective-permute-start | bytes 221192 | tf_op jit(solution)/shard_map/ppermute | solution.py:345
  7.9 5.8 %collective-permute-start.2 = (bf16[48,768]{1,0:T(8,128)(2,1)S(1)}, bf16[48,768]{1,0:T(8,128)(2,1)S(1)}, u32[]{:S(2)}, u32[]{:S(2)}) collective-permute-start(bf16[48,768]{1,0:T(8,128)(2,1)S(1)} %get-tuple-element.30.refs_0_), channel_id=1, source_target_pairs={{0,1},{1,0},{2,3},{3,2},{4,5},{5,4},{6,7},{7,6},{8,9},{9,8},{10,11... | collective-permute-start | bytes 221192 | tf_op jit(solution)/shard_map/ppermute | solution.py:345
  9.4 4.4 %copy-start = (bf16[512,3072]{1,0:T(8,128)(2,1)S(1)}, bf16[512,3072]{1,0:T(8,128)(2,1)}, u32[]{:S(2)}) copy-start(bf16[512,3072]{1,0:T(8,128)(2,1)} %refs_4_.1) | copy-start | bytes 9437188
  9.4 9.3 %collective-permute-start.3 = (bf16[48,2304]{1,0:T(8,128)(2,1)S(1)}, bf16[48,2304]{1,0:T(8,128)(2,1)S(1)}, u32[]{:S(2)}, u32[]{:S(2)}) collective-permute-start(bf16[48,2304]{1,0:T(8,128)(2,1)S(1)} %get-tuple-element.40), channel_id=1, source_target_pairs={{0,24},{4,28},{8,16},{12,20},{16,8},{20,12},{24,0},{28,4},{1,25},{... | collective-permute-start | bytes 663560 | tf_op jit(solution)/shard_map/ppermute | solution.py:345
  15.2 8.5 %collective-permute-start.9 = (bf16[48,1280]{1,0:T(8,128)(2,1)S(1)}, bf16[48,1280]{1,0:T(8,128)(2,1)S(1)}, u32[]{:S(2)}, u32[]{:S(2)}) collective-permute-start(bf16[48,1280]{1,0:T(8,128)(2,1)S(1)} %get-tuple-element.49), channel_id=1, source_target_pairs={{0,24},{4,28},{8,16},{12,20},{16,8},{20,12},{24,0},{28,4},{1,25},{... | collective-permute-start | bytes 368648 | tf_op jit(solution)/shard_map/ppermute | solution.py:345
  17.3 8.6 %collective-permute-start.7 = (bf16[48,3072]{1,0:T(8,128)(2,1)S(1)}, bf16[48,3072]{1,0:T(8,128)(2,1)S(1)}, u32[]{:S(2)}, u32[]{:S(2)}) collective-permute-start(bf16[48,3072]{1,0:T(8,128)(2,1)S(1)} %get-tuple-element.47), channel_id=1, source_target_pairs={{0,8},{4,12},{8,0},{12,4},{16,24},{20,28},{24,16},{28,20},{1,9},{5... | collective-permute-start | bytes 884744 | tf_op jit(solution)/shard_map/ppermute | solution.py:345
  17.9 8.8 %collective-permute-start.8 = (bf16[48,3072]{1,0:T(8,128)(2,1)S(1)}, bf16[48,3072]{1,0:T(8,128)(2,1)S(1)}, u32[]{:S(2)}, u32[]{:S(2)}) collective-permute-start(bf16[48,3072]{1,0:T(8,128)(2,1)S(1)} %get-tuple-element.48), channel_id=1, source_target_pairs={{0,16},{4,20},{8,24},{12,28},{16,0},{20,4},{24,8},{28,12},{1,17},{... | collective-permute-start | bytes 884744 | tf_op jit(solution)/shard_map/ppermute | solution.py:345
  20.3 7.1 %collective-permute-start.4 = (bf16[24,1664]{1,0:T(8,128)(2,1)S(1)}, bf16[24,1664]{1,0:T(8,128)(2,1)S(1)}, u32[]{:S(2)}, u32[]{:S(2)}) collective-permute-start(bf16[24,1664]{1,0:T(8,128)(2,1)S(1)} %get-tuple-element.42), channel_id=1, source_target_pairs={{0,3},{1,2},{2,1},{3,0},{4,7},{5,6},{6,5},{7,4},{8,11},{9,10},{10,... | collective-permute-start | bytes 239624 | tf_op jit(solution)/shard_map/ppermute | solution.py:345
  23.3 6.5 %collective-permute-start.5 = (bf16[24,1664]{1,0:T(8,128)(2,1)S(1)}, bf16[24,1664]{1,0:T(8,128)(2,1)S(1)}, u32[]{:S(2)}, u32[]{:S(2)}) collective-permute-start(bf16[24,1664]{1,0:T(8,128)(2,1)S(1)} %get-tuple-element.43), channel_id=1, source_target_pairs={{0,2},{1,3},{2,0},{3,1},{4,6},{5,7},{6,4},{7,5},{8,10},{9,11},{10,... | collective-permute-start | bytes 239624 | tf_op jit(solution)/shard_map/ppermute | solution.py:345
  23.6 6.1 %collective-permute-start.6 = (bf16[24,1664]{1,0:T(8,128)(2,1)S(1)}, bf16[24,1664]{1,0:T(8,128)(2,1)S(1)}, u32[]{:S(2)}, u32[]{:S(2)}) collective-permute-start(bf16[24,1664]{1,0:T(8,128)(2,1)S(1)} %get-tuple-element.44), channel_id=1, source_target_pairs={{0,1},{1,0},{2,3},{3,2},{4,5},{5,4},{6,7},{7,6},{8,9},{9,8},{10,11... | collective-permute-start | bytes 239624 | tf_op jit(solution)/shard_map/ppermute | solution.py:345
  26.8 3.0 %copy-start.2 = (s32[256,2]{0,1:T(2,128)S(1)}, s32[256,2]{0,1:T(2,128)}, u32[]{:S(2)}) copy-start(s32[256,2]{0,1:T(2,128)} %param.8) | copy-start | bytes 6148
  26.8 3.0 %copy-start.3 = (s32[256,2]{0,1:T(2,128)S(1)}, s32[256,2]{0,1:T(2,128)}, u32[]{:S(2)}) copy-start(s32[256,2]{0,1:T(2,128)} %param.9) | copy-start | bytes 6148
  26.8 3.0 %collective-permute-start.10 = (bf16[192,2304]{1,0:T(8,128)(2,1)S(1)}, bf16[192,2304]{1,0:T(8,128)(2,1)S(1)}, u32[]{:S(2)}, u32[]{:S(2)}) collective-permute-start(bf16[192,2304]{1,0:T(8,128)(2,1)S(1)} %share.1), channel_id=1, source_target_pairs={{0,4},{4,0},{8,12},{12,8},{16,20},{20,16},{24,28},{28,24},{1,5},{5... | collective-permute-start | bytes 2654216 | tf_op jit(solution)/shard_map/ppermute | solution.py:345

commit v9 on v8

--- a/solution.py
+++ b/solution.py
@@ -41,7 +41,7 @@
     return lax.broadcasted_iota(jnp.int32, shape, dim)
 
 
-def call(kernel, outs, args, specs, scratch=(), near=True, out_specs=None, aliases=None, flops=0, name=None):
+def call(kernel, outs, args, specs, scratch=(), near=True, out_specs=None, flops=0, name=None):
     args = [
         pltpu.with_memory_space_constraint(arg, pltpu.HBM) if spec is HBM else arg
         for arg, spec in zip(args, specs)
@@ -54,7 +54,6 @@
         in_specs=specs,
         out_specs=out_specs or jax.tree.map(lambda _: VMEM, outs),
         scratch_shapes=scratch,
-        input_output_aliases=aliases or {},
         compiler_params=pltpu.CompilerParams(vmem_limit_bytes=24 * 1024 * 1024),
         cost_estimate=pl.CostEstimate(flops=flops, bytes_accessed=0, transcendentals=0),
         name=name,
@@ -150,8 +149,9 @@
             out[:, part] = ref[part, :].T
 
 
-def pass_kernel(*refs):
-    pass
+def pass_kernel(own, other, own_out, other_out):
+    own_out[...] = own[...]
+    other_out[...] = other[...]
 
 
 def project_kernel(group, capacity, n_dp, *refs):
@@ -389,7 +389,6 @@
         (packed,) * 2,
         (own, other),
         [VMEM] * 2,
-        aliases={0: 0, 1: 1},
         flops=HEAVY,
         name="pass",
     )

time: 32.3 us -> 32.3 us (level)
  no operation moved by 1% of the time
where the time goes in v9:
time: 32.3 us; the launch traced here: 32.1 us
  starting transfers between devices  16.2 us (50%)
  Pallas kernels  10.7 us (33%)
  waiting for transfers between devices  4.32 us (13%)
  between operations  0.78 us (2%)
    ppermute x11, starting transfers between devices, swap(): return lax.ppermute(array, axis, [(n, n ^ mask) for n in range(size)])  16.2 us
    pallas_call x9, Pallas kernels, call(): pl.pallas_call(kernel, out_shape=outs, in_specs=specs, out_specs=out_spec...  10.7 us
    ppermute x11, waiting for transfers between devices, swap(): return lax.ppermute(array, axis, [(n, n ^ mask) for n in range(size)])  4.32 us
  transfers between devices with their start and end apart: 11, of which 4 were waited for; matrix products, arithmetic and copies ran while one was open for 0% of the time, Pallas kernels for 21%

profile of v9, /device:TPU:0, one launch (start us, length us, event | category | flops | bytes accessed | tf_op | source)
XLA Modules:
  0.0 32.1 jit_solution(17041818753178431747)
XLA Ops:
  0.6 1.8 %pick.1 = (bf16[48,768]{1,0:T(8,128)(2,1)S(1)}, bf16[48,768]{1,0:T(8,128)(2,1)S(1)}, s32[8,256]{1,0:T(8,128)S(1)}) custom-call(s32[2,256]{1,0:T(2,128)} %bitcast.4, s32[2,256]{1,0:T(2,128)} %bitcast.6, bf16[256,3072]{1,0:T(8,128)(2,1)} %grad_hbm.1), custom_call_target="tpu_custom_call" | custom-call | tf_op jit(solution)/shard_map/pick/pallas_call | solution.py:51
  2.4 0.0 copy-start.1
  2.5 0.0 copy-start.4
  2.5 0.0 copy-start.5
  2.5 4.1 %collective-permute-start.1 = (bf16[48,768]{1,0:T(8,128)(2,1)S(1)}, bf16[48,768]{1,0:T(8,128)(2,1)S(1)}, u32[]{:S(2)}, u32[]{:S(2)}) collective-permute-start(bf16[48,768]{1,0:T(8,128)(2,1)S(1)} %get-tuple-element.31), channel_id=1, source_target_pairs={{0,2},{1,3},{2,0},{3,1},{4,6},{5,7},{6,4},{7,5},{8,10},{9,11},{10,... | collective-permute-start | bytes 221192 | tf_op jit(solution)/shard_map/ppermute | solution.py:345
  6.6 1.3 %collective-permute-start = (bf16[48,768]{1,0:T(8,128)(2,1)S(1)}, bf16[48,768]{1,0:T(8,128)(2,1)S(1)}, u32[]{:S(2)}, u32[]{:S(2)}) collective-permute-start(bf16[48,768]{1,0:T(8,128)(2,1)S(1)} %get-tuple-element.31), channel_id=1, source_target_pairs={{0,3},{1,2},{2,1},{3,0},{4,7},{5,6},{6,5},{7,4},{8,11},{9,10},{10,... | collective-permute-start | bytes 221192 | tf_op jit(solution)/shard_map/ppermute | solution.py:345
  7.9 0.2 collective-permute-start.2
  8.2 0.0 copy-done.1
  8.2 0.0 copy-done.4
  8.2 0.0 copy-done.5
  8.2 1.2 %hidden.1 = (bf16[48,2304]{1,0:T(8,128)(2,1)S(1)}, f32[48,512]{1,0:T(8,128)S(1)}, f32[48,512]{1,0:T(8,128)S(1)}, f32[48,512]{1,0:T(8,128)S(1)}) custom-call(bf16[48,3072]{1,0:T(8,128)(2,1)S(1)} %copy-done.1, bf16[3072,512]{1,0:T(8,128)(2,1)S(1)} %copy-done.4, bf16[3072,512]{1,0:T(8,128)(2,1)S(1)} %copy-done.5), custom_call_target="tpu_custom_call" | custom-call | flops 10000000000 | tf_op jit(solution)/shard_map/hidden/pallas_call | solution.py:51
  9.4 0.0 copy-start
  9.4 2.5 %collective-permute-start.3 = (bf16[48,2304]{1,0:T(8,128)(2,1)S(1)}, bf16[48,2304]{1,0:T(8,128)(2,1)S(1)}, u32[]{:S(2)}, u32[]{:S(2)}) collective-permute-start(bf16[48,2304]{1,0:T(8,128)(2,1)S(1)} %get-tuple-element.40), channel_id=1, source_target_pairs={{0,24},{4,28},{8,16},{12,20},{16,8},{20,12},{24,0},{28,4},{1,25},{... | collective-permute-start | bytes 663560 | tf_op jit(solution)/shard_map/ppermute | solution.py:345
  11.9 1.8 %turn.1 = (bf16[512,3072]{1,0:T(8,128)(2,1)S(1)}, bf16[512,3072]{1,0:T(8,128)(2,1)S(1)}) custom-call(bf16[3072,512]{1,0:T(8,128)(2,1)S(1)} %copy-done.4, bf16[3072,512]{1,0:T(8,128)(2,1)S(1)} %copy-done.5), custom_call_target="tpu_custom_call" | custom-call | flops 10000000000 | tf_op jit(solution)/shard_map/turn/pallas_call | solution.py:51
  13.7 0.0 collective-permute-done.2.refs_3_
  13.7 0.0 collective-permute-done.1.refs_2_
  13.8 0.0 collective-permute-done.refs_1_
  13.8 0.0 copy-done
  13.8 1.4 %project.1 = (bf16[48,3072]{1,0:T(8,128)(2,1)S(1)}, bf16[48,3072]{1,0:T(8,128)(2,1)S(1)}, bf16[48,3072]{1,0:T(8,128)(2,1)S(1)}, bf16[48,1280]{1,0:T(8,128)(2,1)S...) custom-call(bf16[48,768]{1,0:T(8,128)(2,1)S(1)} %get-tuple-element.30.refs_0_, ...), custom_call_target="tpu_custom_call" | custom-call | tf_op jit(solution)/shard_map/project/pallas_call | solution.py:51
  15.2 2.2 %collective-permute-start.9 = (bf16[48,1280]{1,0:T(8,128)(2,1)S(1)}, bf16[48,1280]{1,0:T(8,128)(2,1)S(1)}, u32[]{:S(2)}, u32[]{:S(2)}) collective-permute-start(bf16[48,1280]{1,0:T(8,128)(2,1)S(1)} %get-tuple-element.49), channel_id=1, source_target_pairs={{0,24},{4,28},{8,16},{12,20},{16,8},{20,12},{24,0},{28,4},{1,25},{... | collective-permute-start | bytes 368648 | tf_op jit(solution)/shard_map/ppermute | solution.py:345
  17.4 0.5 %collective-permute-start.7 = (bf16[48,3072]{1,0:T(8,128)(2,1)S(1)}, bf16[48,3072]{1,0:T(8,128)(2,1)S(1)}, u32[]{:S(2)}, u32[]{:S(2)}) collective-permute-start(bf16[48,3072]{1,0:T(8,128)(2,1)S(1)} %get-tuple-element.47), channel_id=1, source_target_pairs={{0,8},{4,12},{8,0},{12,4},{16,24},{20,28},{24,16},{28,20},{1,9},{5... | collective-permute-start | bytes 884744 | tf_op jit(solution)/shard_map/ppermute | solution.py:345
  17.9 0.8 %collective-permute-start.8 = (bf16[48,3072]{1,0:T(8,128)(2,1)S(1)}, bf16[48,3072]{1,0:T(8,128)(2,1)S(1)}, u32[]{:S(2)}, u32[]{:S(2)}) collective-permute-start(bf16[48,3072]{1,0:T(8,128)(2,1)S(1)} %get-tuple-element.48), channel_id=1, source_target_pairs={{0,16},{4,20},{8,24},{12,28},{16,0},{20,4},{24,8},{28,12},{1,17},{... | collective-permute-start | bytes 884744 | tf_op jit(solution)/shard_map/ppermute | solution.py:345
  18.7 0.0 collective-permute-done.3.refs_0_.refs_3_
  18.7 1.6 %input.1 = (bf16[24,1664]{1,0:T(8,128)(2,1)S(1)}, bf16[24,1664]{1,0:T(8,128)(2,1)S(1)}, bf16[24,1664]{1,0:T(8,128)(2,1)S(1)}, bf16[24,1664]{1,0:T(8,128)(2,1)S(1)}) custom-call(bf16[48,512]{1,0:T(8,128)(2,1)S(1)} %get-tuple-element.37.da, bf16[48,512]{1,0:T(8,128)(2,1)S(1)} %get-tuple-element.38.db, bf16[48,128]{1,0:T(8,128)(2,1)S(1)} %get-tuple-element.39.gate, ...), custom_call_target="tpu_custom_call" | custom-call | flops 10000000000 | tf_op jit(solution)/shard_map/input/pallas_call | solution.py:51
  20.3 3.0 %collective-permute-start.4 = (bf16[24,1664]{1,0:T(8,128)(2,1)S(1)}, bf16[24,1664]{1,0:T(8,128)(2,1)S(1)}, u32[]{:S(2)}, u32[]{:S(2)}) collective-permute-start(bf16[24,1664]{1,0:T(8,128)(2,1)S(1)} %get-tuple-element.42), channel_id=1, source_target_pairs={{0,3},{1,2},{2,1},{3,0},{4,7},{5,6},{6,5},{7,4},{8,11},{9,10},{10,... | collective-permute-start | bytes 239624 | tf_op jit(solution)/shard_map/ppermute | solution.py:345
  23.3 0.3 %collective-permute-start.5 = (bf16[24,1664]{1,0:T(8,128)(2,1)S(1)}, bf16[24,1664]{1,0:T(8,128)(2,1)S(1)}, u32[]{:S(2)}, u32[]{:S(2)}) collective-permute-start(bf16[24,1664]{1,0:T(8,128)(2,1)S(1)} %get-tuple-element.43), channel_id=1, source_target_pairs={{0,2},{1,3},{2,0},{3,1},{4,6},{5,7},{6,4},{7,5},{8,10},{9,11},{10,... | collective-permute-start | bytes 239624 | tf_op jit(solution)/shard_map/ppermute | solution.py:345
  23.7 0.0 collective-permute-done.9.refs_4_
  23.7 1.1 %collective-permute-start.6 = (bf16[24,1664]{1,0:T(8,128)(2,1)S(1)}, bf16[24,1664]{1,0:T(8,128)(2,1)S(1)}, u32[]{:S(2)}, u32[]{:S(2)}) collective-permute-start(bf16[24,1664]{1,0:T(8,128)(2,1)S(1)} %get-tuple-element.44), channel_id=1, source_target_pairs={{0,1},{1,0},{2,3},{3,2},{4,5},{5,4},{6,7},{7,6},{8,9},{9,8},{10,11... | collective-permute-start | bytes 239624 | tf_op jit(solution)/shard_map/ppermute | solution.py:345
  24.8 1.2 %collective-permute-done.7.refs_1_ = bf16[48,3072]{1,0:T(8,128)(2,1)S(1)} collective-permute-done((bf16[48,3072]{1,0:T(8,128)(2,1)S(1)}, bf16[48,3072]{1,0:T(8,128)(2,1)S(1)}, u32[]{:S(2)}, u32[]{:S(2)}) %collective-permute-start.7) | collective-permute-done | bytes 294944 | tf_op jit(solution)/shard_map/ppermute | solution.py:345
  26.0 0.7 %collective-permute-done.8.refs_2_ = bf16[48,3072]{1,0:T(8,128)(2,1)S(1)} collective-permute-done((bf16[48,3072]{1,0:T(8,128)(2,1)S(1)}, bf16[48,3072]{1,0:T(8,128)(2,1)S(1)}, u32[]{:S(2)}, u32[]{:S(2)}) %collective-permute-start.8) | collective-permute-done | bytes 294944 | tf_op jit(solution)/shard_map/ppermute | solution.py:345
  26.7 0.1 share.1
  26.8 0.0 copy-start.2
  26.8 0.0 copy-start.3
  26.8 0.1 collective-permute-start.10
  26.9 0.5 %weight.1.refs_7_ = f32[3,384,512]{2,1,0:T(8,128)S(1)} custom-call(bf16[48,3072]{1,0:T(8,128)(2,1)S(1)} %get-tuple-element.46.refs_0_, bf16[48,3072]{1,0:T(8,128)(2,1)S(1)} %collective-permute-done.7.refs_1_, bf16[48,3072]{1,0:T(8,128)(2,1)S(1)} %collective-permute-done.8.refs_2_, bf16[48,2304]{1,0:T(8,128)(2,1)S(1)} %collective-permute-done.3.refs_0_.refs_3_, ...), custom_call_target="tpu_custom_call" | custom-call | flops 10000000000 | tf_op jit(solution)/shard_map/weight/pallas_call | solution.py:51
  27.4 0.1 collective-permute-done.4.refs_1_
  27.5 2.3 %collective-permute-done.5.refs_2_ = bf16[24,1664]{1,0:T(8,128)(2,1)S(1)} collective-permute-done((bf16[24,1664]{1,0:T(8,128)(2,1)S(1)}, bf16[24,1664]{1,0:T(8,128)(2,1)S(1)}, u32[]{:S(2)}, u32[]{:S(2)}) %collective-permute-start.5) | collective-permute-done | bytes 79904 | tf_op jit(solution)/shard_map/ppermute | solution.py:345
  29.8 0.0 collective-permute-done.6.refs_3_
  29.8 0.0 collective-permute-done.10.refs_8_
  29.8 0.0 copy-done.2
  29.8 0.0 copy-done.3
  29.8 2.3 %finish.1 = (bf16[256,3072]{1,0:T(8,128)(2,1)}, f32[2,256]{1,0:T(2,128)}, f32[3,384,512]{2,1,0:T(8,128)}) custom-call(bf16[24,1664]{1,0:T(8,128)(2,1)S(1)} %get-tuple-element.41.refs_0_, bf16[24,1664]{1,0:T(8,128)(2,1)S(1)} %collective-permute-done.4.refs_1_, bf16[24,1664]{1,0:T(8,128)(2,1)S(1)} %collective-permute-done.5.refs_2_, ...), custom_call_target="tpu_custom_call" | custom-call | flops 10000000000 | tf_op jit(solution)/shard_map/finish/pallas_call | solution.py:51
  (1 shorter events, 0.0 us)
Async XLA Ops:
  2.4 5.7 %copy-start.1 = (bf16[48,3072]{1,0:T(8,128)(2,1)S(1)}, bf16[48,3072]{1,0:T(8,128)(2,1)}, u32[]{:S(2)}) copy-start(bf16[48,3072]{1,0:T(8,128)(2,1)} %refs_8_.1) | copy-start | bytes 884740
  2.5 5.7 %copy-start.4 = (bf16[3072,512]{1,0:T(8,128)(2,1)S(1)}, bf16[3072,512]{1,0:T(8,128)(2,1)}, u32[]{:S(2)}) copy-start(bf16[3072,512]{1,0:T(8,128)(2,1)} %refs_0_.1) | copy-start | bytes 9437188
  2.5 5.7 %copy-start.5 = (bf16[3072,512]{1,0:T(8,128)(2,1)S(1)}, bf16[3072,512]{1,0:T(8,128)(2,1)}, u32[]{:S(2)}) copy-start(bf16[3072,512]{1,0:T(8,128)(2,1)} %refs_1_.1) | copy-start | bytes 9437188
  2.5 11.2 %collective-permute-start.1 = (bf16[48,768]{1,0:T(8,128)(2,1)S(1)}, bf16[48,768]{1,0:T(8,128)(2,1)S(1)}, u32[]{:S(2)}, u32[]{:S(2)}) collective-permute-start(bf16[48,768]{1,0:T(8,128)(2,1)S(1)} %get-tuple-element.31), channel_id=1, source_target_pairs={{0,2},{1,3},{2,0},{3,1},{4,6},{5,7},{6,4},{7,5},{8,10},{9,11},{10,... | collective-permute-start | bytes 221192 | tf_op jit(solution)/shard_map/ppermute | solution.py:345
  6.6 7.2 %collective-permute-start = (bf16[48,768]{1,0:T(8,128)(2,1)S(1)}, bf16[48,768]{1,0:T(8,128)(2,1)S(1)}, u32[]{:S(2)}, u32[]{:S(2)}) collective-permute-start(bf16[48,768]{1,0:T(8,128)(2,1)S(1)} %get-tuple-element.31), channel_id=1, source_target_pairs={{0,3},{1,2},{2,1},{3,0},{4,7},{5,6},{6,5},{7,4},{8,11},{9,10},{10,... | collective-permute-start | bytes 221192 | tf_op jit(solution)/shard_map/ppermute | solution.py:345
  7.9 5.8 %collective-permute-start.2 = (bf16[48,768]{1,0:T(8,128)(2,1)S(1)}, bf16[48,768]{1,0:T(8,128)(2,1)S(1)}, u32[]{:S(2)}, u32[]{:S(2)}) collective-permute-start(bf16[48,768]{1,0:T(8,128)(2,1)S(1)} %get-tuple-element.30.refs_0_), channel_id=1, source_target_pairs={{0,1},{1,0},{2,3},{3,2},{4,5},{5,4},{6,7},{7,6},{8,9},{9,8},{10,11... | collective-permute-start | bytes 221192 | tf_op jit(solution)/shard_map/ppermute | solution.py:345
  9.4 4.4 %copy-start = (bf16[512,3072]{1,0:T(8,128)(2,1)S(1)}, bf16[512,3072]{1,0:T(8,128)(2,1)}, u32[]{:S(2)}) copy-start(bf16[512,3072]{1,0:T(8,128)(2,1)} %refs_4_.1) | copy-start | bytes 9437188
  9.4 9.3 %collective-permute-start.3 = (bf16[48,2304]{1,0:T(8,128)(2,1)S(1)}, bf16[48,2304]{1,0:T(8,128)(2,1)S(1)}, u32[]{:S(2)}, u32[]{:S(2)}) collective-permute-start(bf16[48,2304]{1,0:T(8,128)(2,1)S(1)} %get-tuple-element.40), channel_id=1, source_target_pairs={{0,24},{4,28},{8,16},{12,20},{16,8},{20,12},{24,0},{28,4},{1,25},{... | collective-permute-start | bytes 663560 | tf_op jit(solution)/shard_map/ppermute | solution.py:345
  15.2 8.5 %collective-permute-start.9 = (bf16[48,1280]{1,0:T(8,128)(2,1)S(1)}, bf16[48,1280]{1,0:T(8,128)(2,1)S(1)}, u32[]{:S(2)}, u32[]{:S(2)}) collective-permute-start(bf16[48,1280]{1,0:T(8,128)(2,1)S(1)} %get-tuple-element.49), channel_id=1, source_target_pairs={{0,24},{4,28},{8,16},{12,20},{16,8},{20,12},{24,0},{28,4},{1,25},{... | collective-permute-start | bytes 368648 | tf_op jit(solution)/shard_map/ppermute | solution.py:345
  17.4 8.6 %collective-permute-start.7 = (bf16[48,3072]{1,0:T(8,128)(2,1)S(1)}, bf16[48,3072]{1,0:T(8,128)(2,1)S(1)}, u32[]{:S(2)}, u32[]{:S(2)}) collective-permute-start(bf16[48,3072]{1,0:T(8,128)(2,1)S(1)} %get-tuple-element.47), channel_id=1, source_target_pairs={{0,8},{4,12},{8,0},{12,4},{16,24},{20,28},{24,16},{28,20},{1,9},{5... | collective-permute-start | bytes 884744 | tf_op jit(solution)/shard_map/ppermute | solution.py:345
  17.9 8.8 %collective-permute-start.8 = (bf16[48,3072]{1,0:T(8,128)(2,1)S(1)}, bf16[48,3072]{1,0:T(8,128)(2,1)S(1)}, u32[]{:S(2)}, u32[]{:S(2)}) collective-permute-start(bf16[48,3072]{1,0:T(8,128)(2,1)S(1)} %get-tuple-element.48), channel_id=1, source_target_pairs={{0,16},{4,20},{8,24},{12,28},{16,0},{20,4},{24,8},{28,12},{1,17},{... | collective-permute-start | bytes 884744 | tf_op jit(solution)/shard_map/ppermute | solution.py:345
  20.3 7.1 %collective-permute-start.4 = (bf16[24,1664]{1,0:T(8,128)(2,1)S(1)}, bf16[24,1664]{1,0:T(8,128)(2,1)S(1)}, u32[]{:S(2)}, u32[]{:S(2)}) collective-permute-start(bf16[24,1664]{1,0:T(8,128)(2,1)S(1)} %get-tuple-element.42), channel_id=1, source_target_pairs={{0,3},{1,2},{2,1},{3,0},{4,7},{5,6},{6,5},{7,4},{8,11},{9,10},{10,... | collective-permute-start | bytes 239624 | tf_op jit(solution)/shard_map/ppermute | solution.py:345
  23.3 6.5 %collective-permute-start.5 = (bf16[24,1664]{1,0:T(8,128)(2,1)S(1)}, bf16[24,1664]{1,0:T(8,128)(2,1)S(1)}, u32[]{:S(2)}, u32[]{:S(2)}) collective-permute-start(bf16[24,1664]{1,0:T(8,128)(2,1)S(1)} %get-tuple-element.43), channel_id=1, source_target_pairs={{0,2},{1,3},{2,0},{3,1},{4,6},{5,7},{6,4},{7,5},{8,10},{9,11},{10,... | collective-permute-start | bytes 239624 | tf_op jit(solution)/shard_map/ppermute | solution.py:345
  23.7 6.1 %collective-permute-start.6 = (bf16[24,1664]{1,0:T(8,128)(2,1)S(1)}, bf16[24,1664]{1,0:T(8,128)(2,1)S(1)}, u32[]{:S(2)}, u32[]{:S(2)}) collective-permute-start(bf16[24,1664]{1,0:T(8,128)(2,1)S(1)} %get-tuple-element.44), channel_id=1, source_target_pairs={{0,1},{1,0},{2,3},{3,2},{4,5},{5,4},{6,7},{7,6},{8,9},{9,8},{10,11... | collective-permute-start | bytes 239624 | tf_op jit(solution)/shard_map/ppermute | solution.py:345
  26.8 3.1 %copy-start.2 = (s32[256,2]{0,1:T(2,128)S(1)}, s32[256,2]{0,1:T(2,128)}, u32[]{:S(2)}) copy-start(s32[256,2]{0,1:T(2,128)} %param.8) | copy-start | bytes 6148
  26.8 3.1 %copy-start.3 = (s32[256,2]{0,1:T(2,128)S(1)}, s32[256,2]{0,1:T(2,128)}, u32[]{:S(2)}) copy-start(s32[256,2]{0,1:T(2,128)} %param.9) | copy-start | bytes 6148
  26.8 3.0 %collective-permute-start.10 = (bf16[192,2304]{1,0:T(8,128)(2,1)S(1)}, bf16[192,2304]{1,0:T(8,128)(2,1)S(1)}, u32[]{:S(2)}, u32[]{:S(2)}) collective-permute-start(bf16[192,2304]{1,0:T(8,128)(2,1)S(1)} %share.1), channel_id=1, source_target_pairs={{0,4},{4,0},{8,12},{12,8},{16,20},{20,16},{24,28},{28,24},{1,5},{5... | collective-permute-start | bytes 2654216 | tf_op jit(solution)/shard_map/ppermute | solution.py:345

commit v10 on v9

--- a/solution.py
+++ b/solution.py
@@ -11,7 +11,7 @@
 SEND_CUTS = 4
 BACK_CUTS = 2
 GATE_LANES = 128
-W_CHUNKS = 4
+W_CHUNKS = 2
 TURNED = 2
 LAST = 3
 HEAVY = 10**10

time: 32.3 us -> 32.1 us (level)
  transfers between devices with their start and end apart: 11 -> 11, of which waited for: 4 -> 3; matrix products, arithmetic and copies ran while one was open for 0% -> 0% of each run, Pallas kernels for 21% -> 20%
where the time goes in v10:
time: 32.1 us; the launch traced here: 32 us
  starting transfers between devices  16.2 us (50%)
  Pallas kernels  10.6 us (33%)
  waiting for transfers between devices  4.31 us (13%)
  between operations  0.79 us (2%)
    ppermute x11, starting transfers between devices, swap(): return lax.ppermute(array, axis, [(n, n ^ mask) for n in range(size)])  16.2 us
    pallas_call x9, Pallas kernels, call(): pl.pallas_call(kernel, out_shape=outs, in_specs=specs, out_specs=out_spec...  10.6 us
    ppermute x11, waiting for transfers between devices, swap(): return lax.ppermute(array, axis, [(n, n ^ mask) for n in range(size)])  4.31 us
  transfers between devices with their start and end apart: 11, of which 3 were waited for; matrix products, arithmetic and copies ran while one was open for 0% of the time, Pallas kernels for 20%

profile of v10, /device:TPU:0, one launch (start us, length us, event | category | flops | bytes accessed | tf_op | source)
XLA Modules:
  0.0 32.0 jit_solution(14741057676744267236)
XLA Ops:
  0.6 1.8 %pick.1 = (bf16[48,768]{1,0:T(8,128)(2,1)S(1)}, bf16[48,768]{1,0:T(8,128)(2,1)S(1)}, s32[8,256]{1,0:T(8,128)S(1)}) custom-call(s32[2,256]{1,0:T(2,128)} %bitcast.4, s32[2,256]{1,0:T(2,128)} %bitcast.6, bf16[256,3072]{1,0:T(8,128)(2,1)} %grad_hbm.1), custom_call_target="tpu_custom_call" | custom-call | tf_op jit(solution)/shard_map/pick/pallas_call | solution.py:51
  2.4 0.0 copy-start.1
  2.5 0.0 copy-start.4
  2.5 0.0 copy-start.5
  2.5 4.1 %collective-permute-start.1 = (bf16[48,768]{1,0:T(8,128)(2,1)S(1)}, bf16[48,768]{1,0:T(8,128)(2,1)S(1)}, u32[]{:S(2)}, u32[]{:S(2)}) collective-permute-start(bf16[48,768]{1,0:T(8,128)(2,1)S(1)} %get-tuple-element.31), channel_id=1, source_target_pairs={{0,2},{1,3},{2,0},{3,1},{4,6},{5,7},{6,4},{7,5},{8,10},{9,11},{10,... | collective-permute-start | bytes 221192 | tf_op jit(solution)/shard_map/ppermute | solution.py:345
  6.6 1.3 %collective-permute-start = (bf16[48,768]{1,0:T(8,128)(2,1)S(1)}, bf16[48,768]{1,0:T(8,128)(2,1)S(1)}, u32[]{:S(2)}, u32[]{:S(2)}) collective-permute-start(bf16[48,768]{1,0:T(8,128)(2,1)S(1)} %get-tuple-element.31), channel_id=1, source_target_pairs={{0,3},{1,2},{2,1},{3,0},{4,7},{5,6},{6,5},{7,4},{8,11},{9,10},{10,... | collective-permute-start | bytes 221192 | tf_op jit(solution)/shard_map/ppermute | solution.py:345
  7.9 0.2 collective-permute-start.2
  8.2 0.0 copy-done.1
  8.2 0.0 copy-done.4
  8.2 0.0 copy-done.5
  8.2 1.2 %hidden.1 = (bf16[48,2304]{1,0:T(8,128)(2,1)S(1)}, f32[48,512]{1,0:T(8,128)S(1)}, f32[48,512]{1,0:T(8,128)S(1)}, f32[48,512]{1,0:T(8,128)S(1)}) custom-call(bf16[48,3072]{1,0:T(8,128)(2,1)S(1)} %copy-done.1, bf16[3072,512]{1,0:T(8,128)(2,1)S(1)} %copy-done.4, bf16[3072,512]{1,0:T(8,128)(2,1)S(1)} %copy-done.5), custom_call_target="tpu_custom_call" | custom-call | flops 10000000000 | tf_op jit(solution)/shard_map/hidden/pallas_call | solution.py:51
  9.4 0.0 copy-start
  9.4 2.5 %collective-permute-start.3 = (bf16[48,2304]{1,0:T(8,128)(2,1)S(1)}, bf16[48,2304]{1,0:T(8,128)(2,1)S(1)}, u32[]{:S(2)}, u32[]{:S(2)}) collective-permute-start(bf16[48,2304]{1,0:T(8,128)(2,1)S(1)} %get-tuple-element.40), channel_id=1, source_target_pairs={{0,24},{4,28},{8,16},{12,20},{16,8},{20,12},{24,0},{28,4},{1,25},{... | collective-permute-start | bytes 663560 | tf_op jit(solution)/shard_map/ppermute | solution.py:345
  11.9 1.8 %turn.1 = (bf16[512,3072]{1,0:T(8,128)(2,1)S(1)}, bf16[512,3072]{1,0:T(8,128)(2,1)S(1)}) custom-call(bf16[3072,512]{1,0:T(8,128)(2,1)S(1)} %copy-done.4, bf16[3072,512]{1,0:T(8,128)(2,1)S(1)} %copy-done.5), custom_call_target="tpu_custom_call" | custom-call | flops 10000000000 | tf_op jit(solution)/shard_map/turn/pallas_call | solution.py:51
  13.7 0.0 collective-permute-done.2.refs_3_
  13.7 0.0 collective-permute-done.1.refs_2_
  13.8 0.0 collective-permute-done.refs_1_
  13.8 0.0 copy-done
  13.8 1.4 %project.1 = (bf16[48,3072]{1,0:T(8,128)(2,1)S(1)}, bf16[48,3072]{1,0:T(8,128)(2,1)S(1)}, bf16[48,3072]{1,0:T(8,128)(2,1)S(1)}, bf16[48,1280]{1,0:T(8,128)(2,1)S...) custom-call(bf16[48,768]{1,0:T(8,128)(2,1)S(1)} %get-tuple-element.30.refs_0_, ...), custom_call_target="tpu_custom_call" | custom-call | tf_op jit(solution)/shard_map/project/pallas_call | solution.py:51
  15.2 2.2 %collective-permute-start.9 = (bf16[48,1280]{1,0:T(8,128)(2,1)S(1)}, bf16[48,1280]{1,0:T(8,128)(2,1)S(1)}, u32[]{:S(2)}, u32[]{:S(2)}) collective-permute-start(bf16[48,1280]{1,0:T(8,128)(2,1)S(1)} %get-tuple-element.49), channel_id=1, source_target_pairs={{0,24},{4,28},{8,16},{12,20},{16,8},{20,12},{24,0},{28,4},{1,25},{... | collective-permute-start | bytes 368648 | tf_op jit(solution)/shard_map/ppermute | solution.py:345
  17.4 0.5 %collective-permute-start.7 = (bf16[48,3072]{1,0:T(8,128)(2,1)S(1)}, bf16[48,3072]{1,0:T(8,128)(2,1)S(1)}, u32[]{:S(2)}, u32[]{:S(2)}) collective-permute-start(bf16[48,3072]{1,0:T(8,128)(2,1)S(1)} %get-tuple-element.47), channel_id=1, source_target_pairs={{0,8},{4,12},{8,0},{12,4},{16,24},{20,28},{24,16},{28,20},{1,9},{5... | collective-permute-start | bytes 884744 | tf_op jit(solution)/shard_map/ppermute | solution.py:345
  17.9 0.8 %collective-permute-start.8 = (bf16[48,3072]{1,0:T(8,128)(2,1)S(1)}, bf16[48,3072]{1,0:T(8,128)(2,1)S(1)}, u32[]{:S(2)}, u32[]{:S(2)}) collective-permute-start(bf16[48,3072]{1,0:T(8,128)(2,1)S(1)} %get-tuple-element.48), channel_id=1, source_target_pairs={{0,16},{4,20},{8,24},{12,28},{16,0},{20,4},{24,8},{28,12},{1,17},{... | collective-permute-start | bytes 884744 | tf_op jit(solution)/shard_map/ppermute | solution.py:345
  18.7 0.0 collective-permute-done.3.refs_0_.refs_3_
  18.7 1.5 %input.1 = (bf16[24,1664]{1,0:T(8,128)(2,1)S(1)}, bf16[24,1664]{1,0:T(8,128)(2,1)S(1)}, bf16[24,1664]{1,0:T(8,128)(2,1)S(1)}, bf16[24,1664]{1,0:T(8,128)(2,1)S(1)}) custom-call(bf16[48,512]{1,0:T(8,128)(2,1)S(1)} %get-tuple-element.37.da, bf16[48,512]{1,0:T(8,128)(2,1)S(1)} %get-tuple-element.38.db, bf16[48,128]{1,0:T(8,128)(2,1)S(1)} %get-tuple-element.39.gate, ...), custom_call_target="tpu_custom_call" | custom-call | flops 10000000000 | tf_op jit(solution)/shard_map/input/pallas_call | solution.py:51
  20.2 3.0 %collective-permute-start.4 = (bf16[24,1664]{1,0:T(8,128)(2,1)S(1)}, bf16[24,1664]{1,0:T(8,128)(2,1)S(1)}, u32[]{:S(2)}, u32[]{:S(2)}) collective-permute-start(bf16[24,1664]{1,0:T(8,128)(2,1)S(1)} %get-tuple-element.42), channel_id=1, source_target_pairs={{0,3},{1,2},{2,1},{3,0},{4,7},{5,6},{6,5},{7,4},{8,11},{9,10},{10,... | collective-permute-start | bytes 239624 | tf_op jit(solution)/shard_map/ppermute | solution.py:345
  23.2 0.3 %collective-permute-start.5 = (bf16[24,1664]{1,0:T(8,128)(2,1)S(1)}, bf16[24,1664]{1,0:T(8,128)(2,1)S(1)}, u32[]{:S(2)}, u32[]{:S(2)}) collective-permute-start(bf16[24,1664]{1,0:T(8,128)(2,1)S(1)} %get-tuple-element.43), channel_id=1, source_target_pairs={{0,2},{1,3},{2,0},{3,1},{4,6},{5,7},{6,4},{7,5},{8,10},{9,11},{10,... | collective-permute-start | bytes 239624 | tf_op jit(solution)/shard_map/ppermute | solution.py:345
  23.5 0.0 collective-permute-done.9.refs_4_
  23.5 1.1 %collective-permute-start.6 = (bf16[24,1664]{1,0:T(8,128)(2,1)S(1)}, bf16[24,1664]{1,0:T(8,128)(2,1)S(1)}, u32[]{:S(2)}, u32[]{:S(2)}) collective-permute-start(bf16[24,1664]{1,0:T(8,128)(2,1)S(1)} %get-tuple-element.44), channel_id=1, source_target_pairs={{0,1},{1,0},{2,3},{3,2},{4,5},{5,4},{6,7},{7,6},{8,9},{9,8},{10,11... | collective-permute-start | bytes 239624 | tf_op jit(solution)/shard_map/ppermute | solution.py:345
  24.6 1.3 %collective-permute-done.7.refs_1_ = bf16[48,3072]{1,0:T(8,128)(2,1)S(1)} collective-permute-done((bf16[48,3072]{1,0:T(8,128)(2,1)S(1)}, bf16[48,3072]{1,0:T(8,128)(2,1)S(1)}, u32[]{:S(2)}, u32[]{:S(2)}) %collective-permute-start.7) | collective-permute-done | bytes 294944 | tf_op jit(solution)/shard_map/ppermute | solution.py:345
  26.0 0.7 %collective-permute-done.8.refs_2_ = bf16[48,3072]{1,0:T(8,128)(2,1)S(1)} collective-permute-done((bf16[48,3072]{1,0:T(8,128)(2,1)S(1)}, bf16[48,3072]{1,0:T(8,128)(2,1)S(1)}, u32[]{:S(2)}, u32[]{:S(2)}) %collective-permute-start.8) | collective-permute-done | bytes 294944 | tf_op jit(solution)/shard_map/ppermute | solution.py:345
  26.7 0.1 share.1
  26.8 0.0 copy-start.2
  26.8 0.0 copy-start.3
  26.8 0.1 collective-permute-start.10
  26.9 0.5 %weight.1.refs_7_ = f32[3,384,512]{2,1,0:T(8,128)S(1)} custom-call(bf16[48,3072]{1,0:T(8,128)(2,1)S(1)} %get-tuple-element.46.refs_0_, bf16[48,3072]{1,0:T(8,128)(2,1)S(1)} %collective-permute-done.7.refs_1_, bf16[48,3072]{1,0:T(8,128)(2,1)S(1)} %collective-permute-done.8.refs_2_, bf16[48,2304]{1,0:T(8,128)(2,1)S(1)} %collective-permute-done.3.refs_0_.refs_3_, ...), custom_call_target="tpu_custom_call" | custom-call | flops 10000000000 | tf_op jit(solution)/shard_map/weight/pallas_call | solution.py:51
  27.4 0.0 collective-permute-done.4.refs_1_
  27.4 2.3 %collective-permute-done.5.refs_2_ = bf16[24,1664]{1,0:T(8,128)(2,1)S(1)} collective-permute-done((bf16[24,1664]{1,0:T(8,128)(2,1)S(1)}, bf16[24,1664]{1,0:T(8,128)(2,1)S(1)}, u32[]{:S(2)}, u32[]{:S(2)}) %collective-permute-start.5) | collective-permute-done | bytes 79904 | tf_op jit(solution)/shard_map/ppermute | solution.py:345
  29.7 0.0 collective-permute-done.6.refs_3_
  29.7 0.0 collective-permute-done.10.refs_8_
  29.7 0.0 copy-done.2
  29.7 0.0 copy-done.3
  29.7 2.3 %finish.1 = (bf16[256,3072]{1,0:T(8,128)(2,1)}, f32[2,256]{1,0:T(2,128)}, f32[3,384,512]{2,1,0:T(8,128)}) custom-call(bf16[24,1664]{1,0:T(8,128)(2,1)S(1)} %get-tuple-element.41.refs_0_, bf16[24,1664]{1,0:T(8,128)(2,1)S(1)} %collective-permute-done.4.refs_1_, bf16[24,1664]{1,0:T(8,128)(2,1)S(1)} %collective-permute-done.5.refs_2_, ...), custom_call_target="tpu_custom_call" | custom-call | flops 10000000000 | tf_op jit(solution)/shard_map/finish/pallas_call | solution.py:51
  (1 shorter events, 0.0 us)
Async XLA Ops:
  2.4 5.7 %copy-start.1 = (bf16[48,3072]{1,0:T(8,128)(2,1)S(1)}, bf16[48,3072]{1,0:T(8,128)(2,1)}, u32[]{:S(2)}) copy-start(bf16[48,3072]{1,0:T(8,128)(2,1)} %refs_8_.1) | copy-start | bytes 884740
  2.5 5.7 %copy-start.4 = (bf16[3072,512]{1,0:T(8,128)(2,1)S(1)}, bf16[3072,512]{1,0:T(8,128)(2,1)}, u32[]{:S(2)}) copy-start(bf16[3072,512]{1,0:T(8,128)(2,1)} %refs_0_.1) | copy-start | bytes 9437188
  2.5 5.7 %copy-start.5 = (bf16[3072,512]{1,0:T(8,128)(2,1)S(1)}, bf16[3072,512]{1,0:T(8,128)(2,1)}, u32[]{:S(2)}) copy-start(bf16[3072,512]{1,0:T(8,128)(2,1)} %refs_1_.1) | copy-start | bytes 9437188
  2.5 11.2 %collective-permute-start.1 = (bf16[48,768]{1,0:T(8,128)(2,1)S(1)}, bf16[48,768]{1,0:T(8,128)(2,1)S(1)}, u32[]{:S(2)}, u32[]{:S(2)}) collective-permute-start(bf16[48,768]{1,0:T(8,128)(2,1)S(1)} %get-tuple-element.31), channel_id=1, source_target_pairs={{0,2},{1,3},{2,0},{3,1},{4,6},{5,7},{6,4},{7,5},{8,10},{9,11},{10,... | collective-permute-start | bytes 221192 | tf_op jit(solution)/shard_map/ppermute | solution.py:345
  6.6 7.2 %collective-permute-start = (bf16[48,768]{1,0:T(8,128)(2,1)S(1)}, bf16[48,768]{1,0:T(8,128)(2,1)S(1)}, u32[]{:S(2)}, u32[]{:S(2)}) collective-permute-start(bf16[48,768]{1,0:T(8,128)(2,1)S(1)} %get-tuple-element.31), channel_id=1, source_target_pairs={{0,3},{1,2},{2,1},{3,0},{4,7},{5,6},{6,5},{7,4},{8,11},{9,10},{10,... | collective-permute-start | bytes 221192 | tf_op jit(solution)/shard_map/ppermute | solution.py:345
  7.9 5.8 %collective-permute-start.2 = (bf16[48,768]{1,0:T(8,128)(2,1)S(1)}, bf16[48,768]{1,0:T(8,128)(2,1)S(1)}, u32[]{:S(2)}, u32[]{:S(2)}) collective-permute-start(bf16[48,768]{1,0:T(8,128)(2,1)S(1)} %get-tuple-element.30.refs_0_), channel_id=1, source_target_pairs={{0,1},{1,0},{2,3},{3,2},{4,5},{5,4},{6,7},{7,6},{8,9},{9,8},{10,11... | collective-permute-start | bytes 221192 | tf_op jit(solution)/shard_map/ppermute | solution.py:345
  9.4 4.4 %copy-start = (bf16[512,3072]{1,0:T(8,128)(2,1)S(1)}, bf16[512,3072]{1,0:T(8,128)(2,1)}, u32[]{:S(2)}) copy-start(bf16[512,3072]{1,0:T(8,128)(2,1)} %refs_4_.1) | copy-start | bytes 9437188
  9.4 9.3 %collective-permute-start.3 = (bf16[48,2304]{1,0:T(8,128)(2,1)S(1)}, bf16[48,2304]{1,0:T(8,128)(2,1)S(1)}, u32[]{:S(2)}, u32[]{:S(2)}) collective-permute-start(bf16[48,2304]{1,0:T(8,128)(2,1)S(1)} %get-tuple-element.40), channel_id=1, source_target_pairs={{0,24},{4,28},{8,16},{12,20},{16,8},{20,12},{24,0},{28,4},{1,25},{... | collective-permute-start | bytes 663560 | tf_op jit(solution)/shard_map/ppermute | solution.py:345
  15.2 8.3 %collective-permute-start.9 = (bf16[48,1280]{1,0:T(8,128)(2,1)S(1)}, bf16[48,1280]{1,0:T(8,128)(2,1)S(1)}, u32[]{:S(2)}, u32[]{:S(2)}) collective-permute-start(bf16[48,1280]{1,0:T(8,128)(2,1)S(1)} %get-tuple-element.49), channel_id=1, source_target_pairs={{0,24},{4,28},{8,16},{12,20},{16,8},{20,12},{24,0},{28,4},{1,25},{... | collective-permute-start | bytes 368648 | tf_op jit(solution)/shard_map/ppermute | solution.py:345
  17.4 8.6 %collective-permute-start.7 = (bf16[48,3072]{1,0:T(8,128)(2,1)S(1)}, bf16[48,3072]{1,0:T(8,128)(2,1)S(1)}, u32[]{:S(2)}, u32[]{:S(2)}) collective-permute-start(bf16[48,3072]{1,0:T(8,128)(2,1)S(1)} %get-tuple-element.47), channel_id=1, source_target_pairs={{0,8},{4,12},{8,0},{12,4},{16,24},{20,28},{24,16},{28,20},{1,9},{5... | collective-permute-start | bytes 884744 | tf_op jit(solution)/shard_map/ppermute | solution.py:345
  17.9 8.8 %collective-permute-start.8 = (bf16[48,3072]{1,0:T(8,128)(2,1)S(1)}, bf16[48,3072]{1,0:T(8,128)(2,1)S(1)}, u32[]{:S(2)}, u32[]{:S(2)}) collective-permute-start(bf16[48,3072]{1,0:T(8,128)(2,1)S(1)} %get-tuple-element.48), channel_id=1, source_target_pairs={{0,16},{4,20},{8,24},{12,28},{16,0},{20,4},{24,8},{28,12},{1,17},{... | collective-permute-start | bytes 884744 | tf_op jit(solution)/shard_map/ppermute | solution.py:345
  20.2 7.2 %collective-permute-start.4 = (bf16[24,1664]{1,0:T(8,128)(2,1)S(1)}, bf16[24,1664]{1,0:T(8,128)(2,1)S(1)}, u32[]{:S(2)}, u32[]{:S(2)}) collective-permute-start(bf16[24,1664]{1,0:T(8,128)(2,1)S(1)} %get-tuple-element.42), channel_id=1, source_target_pairs={{0,3},{1,2},{2,1},{3,0},{4,7},{5,6},{6,5},{7,4},{8,11},{9,10},{10,... | collective-permute-start | bytes 239624 | tf_op jit(solution)/shard_map/ppermute | solution.py:345
  23.2 6.5 %collective-permute-start.5 = (bf16[24,1664]{1,0:T(8,128)(2,1)S(1)}, bf16[24,1664]{1,0:T(8,128)(2,1)S(1)}, u32[]{:S(2)}, u32[]{:S(2)}) collective-permute-start(bf16[24,1664]{1,0:T(8,128)(2,1)S(1)} %get-tuple-element.43), channel_id=1, source_target_pairs={{0,2},{1,3},{2,0},{3,1},{4,6},{5,7},{6,4},{7,5},{8,10},{9,11},{10,... | collective-permute-start | bytes 239624 | tf_op jit(solution)/shard_map/ppermute | solution.py:345
  23.5 6.1 %collective-permute-start.6 = (bf16[24,1664]{1,0:T(8,128)(2,1)S(1)}, bf16[24,1664]{1,0:T(8,128)(2,1)S(1)}, u32[]{:S(2)}, u32[]{:S(2)}) collective-permute-start(bf16[24,1664]{1,0:T(8,128)(2,1)S(1)} %get-tuple-element.44), channel_id=1, source_target_pairs={{0,1},{1,0},{2,3},{3,2},{4,5},{5,4},{6,7},{7,6},{8,9},{9,8},{10,11... | collective-permute-start | bytes 239624 | tf_op jit(solution)/shard_map/ppermute | solution.py:345
  26.8 2.9 %copy-start.2 = (s32[256,2]{0,1:T(2,128)S(1)}, s32[256,2]{0,1:T(2,128)}, u32[]{:S(2)}) copy-start(s32[256,2]{0,1:T(2,128)} %param.8) | copy-start | bytes 6148
  26.8 2.9 %copy-start.3 = (s32[256,2]{0,1:T(2,128)S(1)}, s32[256,2]{0,1:T(2,128)}, u32[]{:S(2)}) copy-start(s32[256,2]{0,1:T(2,128)} %param.9) | copy-start | bytes 6148
  26.8 2.9 %collective-permute-start.10 = (bf16[192,2304]{1,0:T(8,128)(2,1)S(1)}, bf16[192,2304]{1,0:T(8,128)(2,1)S(1)}, u32[]{:S(2)}, u32[]{:S(2)}) collective-permute-start(bf16[192,2304]{1,0:T(8,128)(2,1)S(1)} %share.1), channel_id=1, source_target_pairs={{0,4},{4,0},{8,12},{12,8},{16,20},{20,16},{24,28},{28,24},{1,5},{5... | collective-permute-start | bytes 2654216 | tf_op jit(solution)/shard_map/ppermute | solution.py:345

commit v11 on v10

--- a/solution.py
+++ b/solution.py
@@ -10,6 +10,7 @@
 EXPERTS_W = 2
 SEND_CUTS = 4
 BACK_CUTS = 2
+HEAD = 8
 GATE_LANES = 128
 W_CHUNKS = 2
 TURNED = 2
@@ -183,7 +184,8 @@
     db_out[...] = db
     gate = jnp.sum(h * projected, axis=1, keepdims=True)
     lane = iota((rows, GATE_LANES), 1)
-    gate_out[...] = jnp.where(lane == me // (group // EXPERTS_W), gate, 0.0).astype(BF16)
+    own = (lane < BACK_CUTS * EXPERTS_W) & (lane % EXPERTS_W == me // (group // EXPERTS_W))
+    gate_out[...] = jnp.where(own, gate, 0.0).astype(BF16)
     h = h.astype(BF16)
     if n_dp != PAIRED:
         sends[0][...] = rows_buf[...]
@@ -209,34 +211,34 @@
 def input_kernel(group, capacity, da, db, gate, w_gate, w_up, *refs):
     outs = refs[-group:]
     rows = da.shape[0]
-    width = max(w_gate.shape)
+    width = w_gate.shape[1]
     span = width // BACK_CUTS
-    step = width // W_CHUNKS
-    per = W_CHUNKS // BACK_CUTS
+    tail = capacity - HEAD
     me = lax.axis_index("expert")
-    packed = BACK_CUTS * capacity
-    to = iota((group * packed, rows), 0)
-    at = iota((group * packed, rows), 1)
-    target = (to // packed) ^ me
-    within = to % packed
-    match = (at // capacity == target) & (at % capacity == within % capacity)
-    selects = [
-        (match & (within // capacity == cut)).astype(F32).astype(BF16) for cut in range(BACK_CUTS)
-    ]
-    total = [jnp.zeros((group * packed, step), F32) for _ in range(per)]
-    for k in range(W_CHUNKS):
-        piece = slice(k * step, (k + 1) * step)
-        part = nn(da[...], w_gate[:, piece])
-        if TURNED > 1:
-            part += nn(db[...], w_up[:, piece])
-        else:
-            part += nt(db[...], w_up[piece, :])
-        total[k % per] += nn(selects[k // per], part.astype(BF16))
-    gates = nn(selects[0], gate[...])
+    to = iota((group * HEAD, rows), 0)
+    at = iota((group * HEAD, rows), 1)
+    place = to % HEAD
+    mine = at // capacity == (to // HEAD) ^ me
+    head = (mine & (at % capacity == place)).astype(F32).astype(BF16)
+    rest = mine & (at % capacity == HEAD + place % tail)
+    rests = [(rest & (place // tail == cut)).astype(F32).astype(BF16) for cut in range(BACK_CUTS)]
+    heads = []
+    lower = jnp.zeros((group * HEAD, span), F32)
+    for cut in range(BACK_CUTS):
+        piece = slice(cut * span, (cut + 1) * span)
+        part = (nn(da[...], w_gate[:, piece]) + nn(db[...], w_up[:, piece])).astype(BF16)
+        heads.append(nn(head, part))
+        lower += nn(rests[cut], part)
+    gates = gate[...].astype(F32)
+    early = iota(gates.shape, 1) < EXPERTS_W
+    gates = nn(head, jnp.where(early, gates, 0.0).astype(BF16)) + nn(
+        rests[0], jnp.where(early, 0.0, gates).astype(BF16)
+    )
     for n, out in enumerate(outs):
-        for q in range(per):
-            out[:, q * step : (q + 1) * step] = total[q][n * packed : (n + 1) * packed].astype(BF16)
-        out[:, span:] = gates[n * packed : (n + 1) * packed].astype(BF16)
+        block = slice(n * HEAD, (n + 1) * HEAD)
+        for cut, value in enumerate((*heads, lower)):
+            out[:, cut * span : (cut + 1) * span] = value[block].astype(BF16)
+        out[:, width + span :] = gates[block].astype(BF16)
 
 
 def rows_of(block, hidden, core, refs):
@@ -308,30 +310,34 @@
     input_buf, gate_buf, sems = refs[-3:]
     tokens, width = input_buf.shape
     span = width // BACK_CUTS
-    packed = BACK_CUTS * capacity
     shards = group // EXPERTS_W
+    tail = capacity - HEAD
     me = lax.axis_index("expert")
     every = jnp.concatenate([ref[...] for ref in backs], axis=0)
-    row = iota((group * packed, tokens), 0)
-    expert = ((row // packed) ^ me) // shards
-    within = row % packed
+    row = iota((group * HEAD, tokens), 0)
+    expert = ((row // HEAD) ^ me) // shards
+    place = row % HEAD
     slot = jnp.where(expert == 0, slots[0:1, :], slots[1:2, :])
-    match = within % capacity == slot
-    picks = [
-        (match & (within // capacity == cut)).astype(F32).astype(BF16) for cut in range(BACK_CUTS)
-    ]
-    gates = tn(every[:, span:], picks[0])
+    head = (slot == place).astype(F32).astype(BF16)
+    rest = slot == HEAD + place % tail
+    rests = [(rest & (place // tail == cut)).astype(F32).astype(BF16) for cut in range(BACK_CUTS)]
+    gates = tn(every[:, width + span :], head)[0:EXPERTS_W]
+    gates += tn(every[:, width + span :], rests[0])[EXPERTS_W : 2 * EXPERTS_W]
     for k in range(2):
         route = routes[k : k + 1, :]
         value = jnp.where(route == 0, gates[0:1, :], jnp.where(route == 1, gates[1:2, :], 0.0))
         gate_buf[k : k + 1, :] = value * (16.0 / levels[k : k + 1, :].astype(F32))
     copies.append(pltpu.make_async_copy(gate_buf, gate_hbm, sems.at[2 * BACK_CUTS]))
     copies[-1].start()
-    for cut, pick in enumerate(picks):
-        half = span // 2
+    half = span // 2
+    for cut in range(BACK_CUTS):
+        pick = jnp.concatenate([head, rests[cut]], axis=0)
         for n in range(2):
-            part = pl.ds(cut * span + n * half, half)
-            input_buf[:, part] = tn(pick, every[:, n * half : (n + 1) * half]).astype(BF16)
+            start = cut * span + n * half
+            lower = every[:, width + n * half : width + (n + 1) * half]
+            values = jnp.concatenate([every[:, start : start + half], lower], axis=0)
+            part = pl.ds(start, half)
+            input_buf[:, part] = tn(pick, values).astype(BF16)
             copy = pltpu.make_async_copy(
                 input_buf.at[:, part], input_hbm.at[:, part], sems.at[2 * cut + n]
             )
@@ -426,7 +432,7 @@
         name="project",
     )
     ahead = [swap(array, "dp", n_dp, 2 * LAST) for array in ahead]
-    back = shape((BACK_CUTS * capacity, width // BACK_CUTS + GATE_LANES), BF16)
+    back = shape((HEAD, width + width // BACK_CUTS + GATE_LANES), BF16)
     returns = call(
         functools.partial(input_kernel, group, capacity),
         (back,) * group,

time: 32.1 us -> 32 us (level)
  transfers between devices with their start and end apart: 11 -> 11, of which waited for: 3 -> 3; matrix products, arithmetic and copies ran while one was open for 0% -> 0% of each run, Pallas kernels for 20% -> 21%
where the time goes in v11:
time: 32 us; the launch traced here: 31.8 us
  starting transfers between devices  16.2 us (51%)
  Pallas kernels  10.7 us (33%)
  waiting for transfers between devices  4.05 us (13%)
  between operations  0.79 us (2%)
    ppermute x11, starting transfers between devices, swap(): return lax.ppermute(array, axis, [(n, n ^ mask) for n in range(size)])  16.2 us
    pallas_call x9, Pallas kernels, call(): pl.pallas_call(kernel, out_shape=outs, in_specs=specs, out_specs=out_spec...  10.7 us
    ppermute x11, waiting for transfers between devices, swap(): return lax.ppermute(array, axis, [(n, n ^ mask) for n in range(size)])  4.05 us
  transfers between devices with their start and end apart: 11, of which 3 were waited for; matrix products, arithmetic and copies ran while one was open for 0% of the time, Pallas kernels for 21%

profile of v11, /device:TPU:0, one launch (start us, length us, event | category | flops | bytes accessed | tf_op | source)
XLA Modules:
  0.0 31.8 jit_solution(8767399529770652317)
XLA Ops:
  0.6 1.8 %pick.1 = (bf16[48,768]{1,0:T(8,128)(2,1)S(1)}, bf16[48,768]{1,0:T(8,128)(2,1)S(1)}, s32[8,256]{1,0:T(8,128)S(1)}) custom-call(s32[2,256]{1,0:T(2,128)} %bitcast.4, s32[2,256]{1,0:T(2,128)} %bitcast.6, bf16[256,3072]{1,0:T(8,128)(2,1)} %grad_hbm.1), custom_call_target="tpu_custom_call" | custom-call | tf_op jit(solution)/shard_map/pick/pallas_call | solution.py:52
  2.4 0.0 copy-start.1
  2.5 0.0 copy-start.4
  2.5 0.0 copy-start.5
  2.5 4.1 %collective-permute-start.1 = (bf16[48,768]{1,0:T(8,128)(2,1)S(1)}, bf16[48,768]{1,0:T(8,128)(2,1)S(1)}, u32[]{:S(2)}, u32[]{:S(2)}) collective-permute-start(bf16[48,768]{1,0:T(8,128)(2,1)S(1)} %get-tuple-element.31), channel_id=1, source_target_pairs={{0,2},{1,3},{2,0},{3,1},{4,6},{5,7},{6,4},{7,5},{8,10},{9,11},{10,... | collective-permute-start | bytes 221192 | tf_op jit(solution)/shard_map/ppermute | solution.py:351
  6.6 1.3 %collective-permute-start = (bf16[48,768]{1,0:T(8,128)(2,1)S(1)}, bf16[48,768]{1,0:T(8,128)(2,1)S(1)}, u32[]{:S(2)}, u32[]{:S(2)}) collective-permute-start(bf16[48,768]{1,0:T(8,128)(2,1)S(1)} %get-tuple-element.31), channel_id=1, source_target_pairs={{0,3},{1,2},{2,1},{3,0},{4,7},{5,6},{6,5},{7,4},{8,11},{9,10},{10,... | collective-permute-start | bytes 221192 | tf_op jit(solution)/shard_map/ppermute | solution.py:351
  7.9 0.2 collective-permute-start.2
  8.2 0.0 copy-done.1
  8.2 0.0 copy-done.4
  8.2 0.0 copy-done.5
  8.2 1.2 %hidden.1 = (bf16[48,2304]{1,0:T(8,128)(2,1)S(1)}, f32[48,512]{1,0:T(8,128)S(1)}, f32[48,512]{1,0:T(8,128)S(1)}, f32[48,512]{1,0:T(8,128)S(1)}) custom-call(bf16[48,3072]{1,0:T(8,128)(2,1)S(1)} %copy-done.1, bf16[3072,512]{1,0:T(8,128)(2,1)S(1)} %copy-done.4, bf16[3072,512]{1,0:T(8,128)(2,1)S(1)} %copy-done.5), custom_call_target="tpu_custom_call" | custom-call | flops 10000000000 | tf_op jit(solution)/shard_map/hidden/pallas_call | solution.py:52
  9.4 0.0 copy-start
  9.4 2.5 %collective-permute-start.3 = (bf16[48,2304]{1,0:T(8,128)(2,1)S(1)}, bf16[48,2304]{1,0:T(8,128)(2,1)S(1)}, u32[]{:S(2)}, u32[]{:S(2)}) collective-permute-start(bf16[48,2304]{1,0:T(8,128)(2,1)S(1)} %get-tuple-element.40), channel_id=1, source_target_pairs={{0,24},{4,28},{8,16},{12,20},{16,8},{20,12},{24,0},{28,4},{1,25},{... | collective-permute-start | bytes 663560 | tf_op jit(solution)/shard_map/ppermute | solution.py:351
  11.9 1.8 %turn.1 = (bf16[512,3072]{1,0:T(8,128)(2,1)S(1)}, bf16[512,3072]{1,0:T(8,128)(2,1)S(1)}) custom-call(bf16[3072,512]{1,0:T(8,128)(2,1)S(1)} %copy-done.4, bf16[3072,512]{1,0:T(8,128)(2,1)S(1)} %copy-done.5), custom_call_target="tpu_custom_call" | custom-call | flops 10000000000 | tf_op jit(solution)/shard_map/turn/pallas_call | solution.py:52
  13.7 0.0 collective-permute-done.2.refs_3_
  13.7 0.0 collective-permute-done.1.refs_2_
  13.8 0.0 collective-permute-done.refs_1_
  13.8 0.0 copy-done
  13.8 1.4 %project.1 = (bf16[48,3072]{1,0:T(8,128)(2,1)S(1)}, bf16[48,3072]{1,0:T(8,128)(2,1)S(1)}, bf16[48,3072]{1,0:T(8,128)(2,1)S(1)}, bf16[48,1280]{1,0:T(8,128)(2,1)S...) custom-call(bf16[48,768]{1,0:T(8,128)(2,1)S(1)} %get-tuple-element.30.refs_0_, ...), custom_call_target="tpu_custom_call" | custom-call | tf_op jit(solution)/shard_map/project/pallas_call | solution.py:52
  15.2 2.2 %collective-permute-start.9 = (bf16[48,1280]{1,0:T(8,128)(2,1)S(1)}, bf16[48,1280]{1,0:T(8,128)(2,1)S(1)}, u32[]{:S(2)}, u32[]{:S(2)}) collective-permute-start(bf16[48,1280]{1,0:T(8,128)(2,1)S(1)} %get-tuple-element.49), channel_id=1, source_target_pairs={{0,24},{4,28},{8,16},{12,20},{16,8},{20,12},{24,0},{28,4},{1,25},{... | collective-permute-start | bytes 368648 | tf_op jit(solution)/shard_map/ppermute | solution.py:351
  17.4 0.5 %collective-permute-start.7 = (bf16[48,3072]{1,0:T(8,128)(2,1)S(1)}, bf16[48,3072]{1,0:T(8,128)(2,1)S(1)}, u32[]{:S(2)}, u32[]{:S(2)}) collective-permute-start(bf16[48,3072]{1,0:T(8,128)(2,1)S(1)} %get-tuple-element.47), channel_id=1, source_target_pairs={{0,8},{4,12},{8,0},{12,4},{16,24},{20,28},{24,16},{28,20},{1,9},{5... | collective-permute-start | bytes 884744 | tf_op jit(solution)/shard_map/ppermute | solution.py:351
  17.9 0.8 %collective-permute-start.8 = (bf16[48,3072]{1,0:T(8,128)(2,1)S(1)}, bf16[48,3072]{1,0:T(8,128)(2,1)S(1)}, u32[]{:S(2)}, u32[]{:S(2)}) collective-permute-start(bf16[48,3072]{1,0:T(8,128)(2,1)S(1)} %get-tuple-element.48), channel_id=1, source_target_pairs={{0,16},{4,20},{8,24},{12,28},{16,0},{20,4},{24,8},{28,12},{1,17},{... | collective-permute-start | bytes 884744 | tf_op jit(solution)/shard_map/ppermute | solution.py:351
  18.7 0.0 collective-permute-done.3.refs_0_.refs_3_
  18.7 1.5 %input.1 = (bf16[8,4736]{1,0:T(8,128)(2,1)S(1)}, bf16[8,4736]{1,0:T(8,128)(2,1)S(1)}, bf16[8,4736]{1,0:T(8,128)(2,1)S(1)}, bf16[8,4736]{1,0:T(8,128)(2,1)S(1)}) custom-call(bf16[48,512]{1,0:T(8,128)(2,1)S(1)} %get-tuple-element.37.da, bf16[48,512]{1,0:T(8,128)(2,1)S(1)} %get-tuple-element.38.db, bf16[48,128]{1,0:T(8,128)(2,1)S(1)} %get-tuple-element.39.gate, ...), custom_call_target="tpu_custom_call" | custom-call | flops 10000000000 | tf_op jit(solution)/shard_map/input/pallas_call | solution.py:52
  20.3 3.0 %collective-permute-start.4 = (bf16[8,4736]{1,0:T(8,128)(2,1)S(1)}, bf16[8,4736]{1,0:T(8,128)(2,1)S(1)}, u32[]{:S(2)}, u32[]{:S(2)}) collective-permute-start(bf16[8,4736]{1,0:T(8,128)(2,1)S(1)} %get-tuple-element.42), channel_id=1, source_target_pairs={{0,3},{1,2},{2,1},{3,0},{4,7},{5,6},{6,5},{7,4},{8,11},{9,10},{10,... | collective-permute-start | bytes 227336 | tf_op jit(solution)/shard_map/ppermute | solution.py:351
  23.3 0.3 %collective-permute-start.5 = (bf16[8,4736]{1,0:T(8,128)(2,1)S(1)}, bf16[8,4736]{1,0:T(8,128)(2,1)S(1)}, u32[]{:S(2)}, u32[]{:S(2)}) collective-permute-start(bf16[8,4736]{1,0:T(8,128)(2,1)S(1)} %get-tuple-element.43), channel_id=1, source_target_pairs={{0,2},{1,3},{2,0},{3,1},{4,6},{5,7},{6,4},{7,5},{8,10},{9,11},{10,... | collective-permute-start | bytes 227336 | tf_op jit(solution)/shard_map/ppermute | solution.py:351
  23.6 0.0 collective-permute-done.9.refs_4_
  23.6 1.1 %collective-permute-start.6 = (bf16[8,4736]{1,0:T(8,128)(2,1)S(1)}, bf16[8,4736]{1,0:T(8,128)(2,1)S(1)}, u32[]{:S(2)}, u32[]{:S(2)}) collective-permute-start(bf16[8,4736]{1,0:T(8,128)(2,1)S(1)} %get-tuple-element.44), channel_id=1, source_target_pairs={{0,1},{1,0},{2,3},{3,2},{4,5},{5,4},{6,7},{7,6},{8,9},{9,8},{10,11... | collective-permute-start | bytes 227336 | tf_op jit(solution)/shard_map/ppermute | solution.py:351
  24.7 1.3 %collective-permute-done.7.refs_1_ = bf16[48,3072]{1,0:T(8,128)(2,1)S(1)} collective-permute-done((bf16[48,3072]{1,0:T(8,128)(2,1)S(1)}, bf16[48,3072]{1,0:T(8,128)(2,1)S(1)}, u32[]{:S(2)}, u32[]{:S(2)}) %collective-permute-start.7) | collective-permute-done | bytes 294944 | tf_op jit(solution)/shard_map/ppermute | solution.py:351
  26.0 0.7 %collective-permute-done.8.refs_2_ = bf16[48,3072]{1,0:T(8,128)(2,1)S(1)} collective-permute-done((bf16[48,3072]{1,0:T(8,128)(2,1)S(1)}, bf16[48,3072]{1,0:T(8,128)(2,1)S(1)}, u32[]{:S(2)}, u32[]{:S(2)}) %collective-permute-start.8) | collective-permute-done | bytes 294944 | tf_op jit(solution)/shard_map/ppermute | solution.py:351
  26.7 0.1 share.1
  26.8 0.0 copy-start.2
  26.8 0.0 copy-start.3
  26.8 0.1 collective-permute-start.10
  26.9 0.5 %weight.1.refs_7_ = f32[3,384,512]{2,1,0:T(8,128)S(1)} custom-call(bf16[48,3072]{1,0:T(8,128)(2,1)S(1)} %get-tuple-element.46.refs_0_, bf16[48,3072]{1,0:T(8,128)(2,1)S(1)} %collective-permute-done.7.refs_1_, bf16[48,3072]{1,0:T(8,128)(2,1)S(1)} %collective-permute-done.8.refs_2_, bf16[48,2304]{1,0:T(8,128)(2,1)S(1)} %collective-permute-done.3.refs_0_.refs_3_, ...), custom_call_target="tpu_custom_call" | custom-call | flops 10000000000 | tf_op jit(solution)/shard_map/weight/pallas_call | solution.py:52
  27.4 0.0 collective-permute-done.4.refs_1_
  27.4 2.1 %collective-permute-done.5.refs_2_ = bf16[8,4736]{1,0:T(8,128)(2,1)S(1)} collective-permute-done((bf16[8,4736]{1,0:T(8,128)(2,1)S(1)}, bf16[8,4736]{1,0:T(8,128)(2,1)S(1)}, u32[]{:S(2)}, u32[]{:S(2)}) %collective-permute-start.5) | collective-permute-done | bytes 75808 | tf_op jit(solution)/shard_map/ppermute | solution.py:351
  29.5 0.0 collective-permute-done.6.refs_3_
  29.5 0.0 collective-permute-done.10.refs_8_
  29.5 0.0 copy-done.2
  29.5 0.0 copy-done.3
  29.5 2.3 %finish.1 = (bf16[256,3072]{1,0:T(8,128)(2,1)}, f32[2,256]{1,0:T(2,128)}, f32[3,384,512]{2,1,0:T(8,128)}) custom-call(bf16[8,4736]{1,0:T(8,128)(2,1)S(1)} %get-tuple-element.41.refs_0_, bf16[8,4736]{1,0:T(8,128)(2,1)S(1)} %collective-permute-done.4.refs_1_, bf16[8,4736]{1,0:T(8,128)(2,1)S(1)} %collective-permute-done.5.refs_2_, ...), custom_call_target="tpu_custom_call" | custom-call | flops 10000000000 | tf_op jit(solution)/shard_map/finish/pallas_call | solution.py:52
  (1 shorter events, 0.0 us)
Async XLA Ops:
  2.4 5.7 %copy-start.1 = (bf16[48,3072]{1,0:T(8,128)(2,1)S(1)}, bf16[48,3072]{1,0:T(8,128)(2,1)}, u32[]{:S(2)}) copy-start(bf16[48,3072]{1,0:T(8,128)(2,1)} %refs_8_.1) | copy-start | bytes 884740
  2.5 5.7 %copy-start.4 = (bf16[3072,512]{1,0:T(8,128)(2,1)S(1)}, bf16[3072,512]{1,0:T(8,128)(2,1)}, u32[]{:S(2)}) copy-start(bf16[3072,512]{1,0:T(8,128)(2,1)} %refs_0_.1) | copy-start | bytes 9437188
  2.5 5.7 %copy-start.5 = (bf16[3072,512]{1,0:T(8,128)(2,1)S(1)}, bf16[3072,512]{1,0:T(8,128)(2,1)}, u32[]{:S(2)}) copy-start(bf16[3072,512]{1,0:T(8,128)(2,1)} %refs_1_.1) | copy-start | bytes 9437188
  2.5 11.2 %collective-permute-start.1 = (bf16[48,768]{1,0:T(8,128)(2,1)S(1)}, bf16[48,768]{1,0:T(8,128)(2,1)S(1)}, u32[]{:S(2)}, u32[]{:S(2)}) collective-permute-start(bf16[48,768]{1,0:T(8,128)(2,1)S(1)} %get-tuple-element.31), channel_id=1, source_target_pairs={{0,2},{1,3},{2,0},{3,1},{4,6},{5,7},{6,4},{7,5},{8,10},{9,11},{10,... | collective-permute-start | bytes 221192 | tf_op jit(solution)/shard_map/ppermute | solution.py:351
  6.6 7.2 %collective-permute-start = (bf16[48,768]{1,0:T(8,128)(2,1)S(1)}, bf16[48,768]{1,0:T(8,128)(2,1)S(1)}, u32[]{:S(2)}, u32[]{:S(2)}) collective-permute-start(bf16[48,768]{1,0:T(8,128)(2,1)S(1)} %get-tuple-element.31), channel_id=1, source_target_pairs={{0,3},{1,2},{2,1},{3,0},{4,7},{5,6},{6,5},{7,4},{8,11},{9,10},{10,... | collective-permute-start | bytes 221192 | tf_op jit(solution)/shard_map/ppermute | solution.py:351
  7.9 5.8 %collective-permute-start.2 = (bf16[48,768]{1,0:T(8,128)(2,1)S(1)}, bf16[48,768]{1,0:T(8,128)(2,1)S(1)}, u32[]{:S(2)}, u32[]{:S(2)}) collective-permute-start(bf16[48,768]{1,0:T(8,128)(2,1)S(1)} %get-tuple-element.30.refs_0_), channel_id=1, source_target_pairs={{0,1},{1,0},{2,3},{3,2},{4,5},{5,4},{6,7},{7,6},{8,9},{9,8},{10,11... | collective-permute-start | bytes 221192 | tf_op jit(solution)/shard_map/ppermute | solution.py:351
  9.4 4.4 %copy-start = (bf16[512,3072]{1,0:T(8,128)(2,1)S(1)}, bf16[512,3072]{1,0:T(8,128)(2,1)}, u32[]{:S(2)}) copy-start(bf16[512,3072]{1,0:T(8,128)(2,1)} %refs_4_.1) | copy-start | bytes 9437188
  9.4 9.3 %collective-permute-start.3 = (bf16[48,2304]{1,0:T(8,128)(2,1)S(1)}, bf16[48,2304]{1,0:T(8,128)(2,1)S(1)}, u32[]{:S(2)}, u32[]{:S(2)}) collective-permute-start(bf16[48,2304]{1,0:T(8,128)(2,1)S(1)} %get-tuple-element.40), channel_id=1, source_target_pairs={{0,24},{4,28},{8,16},{12,20},{16,8},{20,12},{24,0},{28,4},{1,25},{... | collective-permute-start | bytes 663560 | tf_op jit(solution)/shard_map/ppermute | solution.py:351
  15.2 8.4 %collective-permute-start.9 = (bf16[48,1280]{1,0:T(8,128)(2,1)S(1)}, bf16[48,1280]{1,0:T(8,128)(2,1)S(1)}, u32[]{:S(2)}, u32[]{:S(2)}) collective-permute-start(bf16[48,1280]{1,0:T(8,128)(2,1)S(1)} %get-tuple-element.49), channel_id=1, source_target_pairs={{0,24},{4,28},{8,16},{12,20},{16,8},{20,12},{24,0},{28,4},{1,25},{... | collective-permute-start | bytes 368648 | tf_op jit(solution)/shard_map/ppermute | solution.py:351
  17.4 8.6 %collective-permute-start.7 = (bf16[48,3072]{1,0:T(8,128)(2,1)S(1)}, bf16[48,3072]{1,0:T(8,128)(2,1)S(1)}, u32[]{:S(2)}, u32[]{:S(2)}) collective-permute-start(bf16[48,3072]{1,0:T(8,128)(2,1)S(1)} %get-tuple-element.47), channel_id=1, source_target_pairs={{0,8},{4,12},{8,0},{12,4},{16,24},{20,28},{24,16},{28,20},{1,9},{5... | collective-permute-start | bytes 884744 | tf_op jit(solution)/shard_map/ppermute | solution.py:351
  17.9 8.8 %collective-permute-start.8 = (bf16[48,3072]{1,0:T(8,128)(2,1)S(1)}, bf16[48,3072]{1,0:T(8,128)(2,1)S(1)}, u32[]{:S(2)}, u32[]{:S(2)}) collective-permute-start(bf16[48,3072]{1,0:T(8,128)(2,1)S(1)} %get-tuple-element.48), channel_id=1, source_target_pairs={{0,16},{4,20},{8,24},{12,28},{16,0},{20,4},{24,8},{28,12},{1,17},{... | collective-permute-start | bytes 884744 | tf_op jit(solution)/shard_map/ppermute | solution.py:351
  20.3 7.1 %collective-permute-start.4 = (bf16[8,4736]{1,0:T(8,128)(2,1)S(1)}, bf16[8,4736]{1,0:T(8,128)(2,1)S(1)}, u32[]{:S(2)}, u32[]{:S(2)}) collective-permute-start(bf16[8,4736]{1,0:T(8,128)(2,1)S(1)} %get-tuple-element.42), channel_id=1, source_target_pairs={{0,3},{1,2},{2,1},{3,0},{4,7},{5,6},{6,5},{7,4},{8,11},{9,10},{10,... | collective-permute-start | bytes 227336 | tf_op jit(solution)/shard_map/ppermute | solution.py:351
  23.3 6.2 %collective-permute-start.5 = (bf16[8,4736]{1,0:T(8,128)(2,1)S(1)}, bf16[8,4736]{1,0:T(8,128)(2,1)S(1)}, u32[]{:S(2)}, u32[]{:S(2)}) collective-permute-start(bf16[8,4736]{1,0:T(8,128)(2,1)S(1)} %get-tuple-element.43), channel_id=1, source_target_pairs={{0,2},{1,3},{2,0},{3,1},{4,6},{5,7},{6,4},{7,5},{8,10},{9,11},{10,... | collective-permute-start | bytes 227336 | tf_op jit(solution)/shard_map/ppermute | solution.py:351
  23.6 5.9 %collective-permute-start.6 = (bf16[8,4736]{1,0:T(8,128)(2,1)S(1)}, bf16[8,4736]{1,0:T(8,128)(2,1)S(1)}, u32[]{:S(2)}, u32[]{:S(2)}) collective-permute-start(bf16[8,4736]{1,0:T(8,128)(2,1)S(1)} %get-tuple-element.44), channel_id=1, source_target_pairs={{0,1},{1,0},{2,3},{3,2},{4,5},{5,4},{6,7},{7,6},{8,9},{9,8},{10,11... | collective-permute-start | bytes 227336 | tf_op jit(solution)/shard_map/ppermute | solution.py:351
  26.8 2.7 %copy-start.2 = (s32[256,2]{0,1:T(2,128)S(1)}, s32[256,2]{0,1:T(2,128)}, u32[]{:S(2)}) copy-start(s32[256,2]{0,1:T(2,128)} %param.8) | copy-start | bytes 6148
  26.8 2.7 %copy-start.3 = (s32[256,2]{0,1:T(2,128)S(1)}, s32[256,2]{0,1:T(2,128)}, u32[]{:S(2)}) copy-start(s32[256,2]{0,1:T(2,128)} %param.9) | copy-start | bytes 6148
  26.8 2.7 %collective-permute-start.10 = (bf16[192,2304]{1,0:T(8,128)(2,1)S(1)}, bf16[192,2304]{1,0:T(8,128)(2,1)S(1)}, u32[]{:S(2)}, u32[]{:S(2)}) collective-permute-start(bf16[192,2304]{1,0:T(8,128)(2,1)S(1)} %share.1), channel_id=1, source_target_pairs={{0,4},{4,0},{8,12},{12,8},{16,20},{20,16},{24,28},{28,24},{1,5},{5... | collective-permute-start | bytes 2654216 | tf_op jit(solution)/shard_map/ppermute | solution.py:351
